TPU v7x, 1024 devices: a whole 4x4x32 slice. The times are simulated.
1024 devices in a mesh: blk: 512 (over z, y, x_hi, core), group: 2 (over x_lo).
Axes of the slice: x: 4 (x_hi: 2, x_lo: 2; x = x_hi * 2 + x_lo), y: 4, z: 32, core: 2. Of those that a mesh axis runs over, the one named last changes fastest.
Arguments:
- image_feats: bfloat16 [131072, 768], P(('blk', 'group')), may hold values from -0.796875 to 0.796875
- text_feats: bfloat16 [131072, 768], P(('blk', 'group')), may hold values from -0.796875 to 0.796875
- image_proj: bfloat16 [768, 768], replicated, may hold values from -0.21875 to 0.21875
- text_proj: bfloat16 [768, 768], replicated, may hold values from -0.21875 to 0.21875
- logit_scale: float32 [1], replicated, may hold values from 5 to 20
- logit_bias: float32 [1], replicated, may hold values from -3 to 0
- match: int32 [131072], P(('blk', 'group')), may hold values from 0 to 131071, as said below
Outputs:
- grad_image_feats: bfloat16 [131072, 768], P(('blk', 'group'))
- grad_text_feats: bfloat16 [131072, 768], P(('blk', 'group'))
Inputs may be any that keep to these rules, and one draw needn't show every extreme that they name: match of an image row in block b (rows b * 2 * 128 to (b + 1) * 2 * 128 - 1) names a report row of one of the blocks (b - k) mod 512, k below 4.
All inputs are finite; a program needn't handle non-finite values.
Results may differ from a plain program's by a relative error of at most 0.02.
Values may be sent and summed in bfloat16 or wider, within the bound.
No kernel may reach another device: no remote copies, remote signals or barrier semaphores. Data moves between devices by JAX's collectives and lax.ppermute only.
A program may use at most 32 MiB of HBM per device.

v0:
```python
import jax
import jax.numpy as jnp
from jax import lax
from jax.sharding import PartitionSpec as P

SPAN = 4


def passed_along(block, axis, distance):
    devices = range(lax.axis_size(axis))
    route = [((i - distance) % len(devices), i) for i in devices]
    return lax.ppermute(block, axis, route)


def embed(feats, proj):
    x = jnp.dot(feats, proj, preferred_element_type=jnp.float32)
    inv = lax.rsqrt(jnp.sum(x * x, axis=-1, keepdims=True) + 1e-06)
    return (x * inv, inv)


def back_norm(grad, unit, inv, proj):
    inner = jnp.sum(grad * unit, axis=-1, keepdims=True)
    grad_x = (inv * (grad - inner * unit)).astype(jnp.bfloat16)
    out = lax.dot_general(
        grad_x, proj, (((1,), (1,)), ((), ())), preferred_element_type=jnp.float32
    )
    return out.astype(jnp.bfloat16)


def pair_coef(images, image_match, texts, text_ids, scale, bias):
    sign = jnp.where(image_match[:, None] == text_ids[None, :], jnp.float32(1.0), jnp.float32(-1.0))
    logits = (
        scale
        * lax.dot_general(
            images, texts, (((1,), (1,)), ((), ())), preferred_element_type=jnp.float32
        )
        + bias
    )
    return (-sign * jax.nn.sigmoid(-sign * logits) * scale).astype(jnp.bfloat16)


def body(image_feats, text_feats, image_proj, text_proj, logit_scale, logit_bias, match):
    image_unit, image_inv = embed(image_feats, image_proj)
    text_unit, text_inv = embed(text_feats, text_proj)
    image_emb = image_unit.astype(jnp.bfloat16)
    text_emb = text_unit.astype(jnp.bfloat16)
    scale = logit_scale[0]
    bias = logit_bias[0]
    blk_count = lax.axis_size("blk")
    block_id = lax.axis_index("blk")
    own_rows = image_feats.shape[0]
    width_rows = 2 * own_rows
    local_ids = jnp.arange(width_rows, dtype=jnp.int32)
    visiting = lax.all_gather(text_emb, "group", axis=0, tiled=True)
    grad_image = jnp.zeros(image_unit.shape, jnp.float32)
    carried = None
    for step in range(SPAN):
        if step > 0:
            visiting = passed_along(visiting, "blk", 1)
        source = (block_id - step) % blk_count
        text_ids = source * width_rows + local_ids
        coef = pair_coef(image_emb, match, visiting, text_ids, scale, bias)
        grad_image = grad_image + jnp.dot(coef, visiting, preferred_element_type=jnp.float32)
        term = lax.dot_general(
            coef, image_emb, (((0,), (0,)), ((), ())), preferred_element_type=jnp.float32
        )
        if step == 0:
            carried = term
        else:
            carried = (
                passed_along(carried.astype(jnp.bfloat16), "blk", 1).astype(carried.dtype) + term
            )
    carried = passed_along(carried.astype(jnp.bfloat16), "blk", blk_count - (SPAN - 1)).astype(
        carried.dtype
    )
    grad_text = lax.psum_scatter(
        carried.astype(jnp.bfloat16), "group", scatter_dimension=0, tiled=True
    ).astype(jnp.float32)
    return (
        back_norm(grad_image, image_unit, image_inv, image_proj),
        back_norm(grad_text, text_unit, text_inv, text_proj),
    )


def solution(mesh):
    return jax.shard_map(
        body,
        mesh=mesh,
        in_specs=(
            P(("blk", "group"), None),
            P(("blk", "group"), None),
            P(),
            P(),
            P(),
            P(),
            P(("blk", "group")),
        ),
        out_specs=(P(("blk", "group"), None), P(("blk", "group"), None)),
        check_vma=False,
    )
```

profile of v0, /device:TPU:1, one launch (start us, length us, event | category | flops | bytes accessed | tf_op | source)
XLA Modules:
  0.0 126.9 jit_solution(12933246778716982490)
XLA Ops:
  7.2 1.9 %multiply_reduce_fusion.1 = (f32[128]{0:T(128)S(1)}, f32[128,768]{1,0:T(8,128)S(1)}) fusion(bf16[128,768]{1,0:T(8,128)(2,1)} %param.8, bf16[768,768]{1,0:T(8,128)(2,1)} %param.10), kind=kOutput, calls=%fused_computation.56 | convolution fusion | flops 151191424 | bytes 1769984 | tf_op jit(solution)/shard_map/dot_general | solution.py:16
  9.2 5.8 %all_gather.3 = bf16[256,768]{1,0:T(8,128)(2,1)S(1)} all-gather(bf16[128,768]{1,0:T(8,128)(2,1)S(1)} %multiply_convert_fusion.1), channel_id=1, replica_groups=mesh['blk'=512,'group'=2] {'group'}, dimensions={0}, use_global_device_ids=true | all-gather | bytes 589824 | tf_op jit(solution)/shard_map/all_gather | solution.py:54
  15.0 7.6 %collective-permute-start = (bf16[256,768]{1,0:T(8,128)(2,1)S(1)}, bf16[256,768]{1,0:T(8,128)(2,1)S(1)}, u32[]{:S(2)}, u32[]{:S(2)}) collective-permute-start(bf16[256,768]{1,0:T(8,128)(2,1)S(1)} %all_gather.3), channel_id=1, source_target_pairs={{1022,0},{0,2},{2,4},{4,6},{6,8},{8,10},{10,12},{12,14},{14,16},{1... | collective-permute-start | bytes 1179656 | tf_op jit(solution)/shard_map/ppermute | solution.py:12
  23.9 0.4 multiply_reduce_fusion.2
  24.9 1.0 convolution_convert_fusion
  26.0 1.9 %collective-permute-start.3 = (bf16[256,768]{1,0:T(8,128)(2,1)}, bf16[256,768]{1,0:T(8,128)(2,1)}, u32[]{:S(2)}, u32[]{:S(2)}) collective-permute-start(bf16[256,768]{1,0:T(8,128)(2,1)} %convolution_convert_fusion), channel_id=1, source_target_pairs={{1022,0},{0,2},{2,4},{4,6},{6,8},{8,10},{10,12},{12,14},{14,16},{1... | collective-permute-start | bytes 1179656 | tf_op jit(solution)/shard_map/ppermute | solution.py:12
  28.0 6.7 %collective-permute-done = bf16[256,768]{1,0:T(8,128)(2,1)S(1)} collective-permute-done((bf16[256,768]{1,0:T(8,128)(2,1)S(1)}, bf16[256,768]{1,0:T(8,128)(2,1)S(1)}, u32[]{:S(2)}, u32[]{:S(2)}) %collective-permute-start) | collective-permute-done | bytes 393248 | tf_op jit(solution)/shard_map/ppermute | solution.py:12
  34.7 1.9 %collective-permute-start.1 = (bf16[256,768]{1,0:T(8,128)(2,1)S(1)}, bf16[256,768]{1,0:T(8,128)(2,1)S(1)}, u32[]{:S(2)}, u32[]{:S(2)}) collective-permute-start(bf16[256,768]{1,0:T(8,128)(2,1)S(1)} %collective-permute-done), channel_id=1, source_target_pairs={{1022,0},{0,2},{2,4},{4,6},{6,8},{8,10},{10,12},{12,14},{14,16},{1... | collective-permute-start | bytes 1179656 | tf_op jit(solution)/shard_map/ppermute | solution.py:12
  37.0 3.4 %collective-permute-done.3 = bf16[256,768]{1,0:T(8,128)(2,1)} collective-permute-done((bf16[256,768]{1,0:T(8,128)(2,1)}, bf16[256,768]{1,0:T(8,128)(2,1)}, u32[]{:S(2)}, u32[]{:S(2)}) %collective-permute-start.3) | collective-permute-done | bytes 393248 | tf_op jit(solution)/shard_map/ppermute | solution.py:12
  40.3 1.3 %add_convert_fusion.2 = bf16[256,768]{1,0:T(8,128)(2,1)S(1)} fusion(bf16[256,768]{1,0:T(8,128)(2,1)} %collective-permute-done.3, bf16[128,256]{1,0:T(8,128)(2,1)S(1)} %fusion.33, bf16[128,768]{1,0:T(8,128)(2,1)S(1)} %multiply_convert_fusion.2), kind=kOutput, calls=%fused_computation.48 | convolution fusion | flops 50921472 | bytes 1048576 | tf_op jit(solution)/shard_map/dot_general | solution.py:64
  41.6 1.9 %collective-permute-start.4 = (bf16[256,768]{1,0:T(8,128)(2,1)S(1)}, bf16[256,768]{1,0:T(8,128)(2,1)S(1)}, u32[]{:S(2)}, u32[]{:S(2)}) collective-permute-start(bf16[256,768]{1,0:T(8,128)(2,1)S(1)} %add_convert_fusion.2), channel_id=1, source_target_pairs={{1022,0},{0,2},{2,4},{4,6},{6,8},{8,10},{10,12},{12,14},{14,16},{1... | collective-permute-start | bytes 1179656 | tf_op jit(solution)/shard_map/ppermute | solution.py:12
  43.5 6.0 %collective-permute-done.1 = bf16[256,768]{1,0:T(8,128)(2,1)S(1)} collective-permute-done((bf16[256,768]{1,0:T(8,128)(2,1)S(1)}, bf16[256,768]{1,0:T(8,128)(2,1)S(1)}, u32[]{:S(2)}, u32[]{:S(2)}) %collective-permute-start.1) | collective-permute-done | bytes 393248 | tf_op jit(solution)/shard_map/ppermute | solution.py:12
  49.5 1.9 %collective-permute-start.2 = (bf16[256,768]{1,0:T(8,128)(2,1)S(1)}, bf16[256,768]{1,0:T(8,128)(2,1)S(1)}, u32[]{:S(2)}, u32[]{:S(2)}) collective-permute-start(bf16[256,768]{1,0:T(8,128)(2,1)S(1)} %collective-permute-done.1), channel_id=1, source_target_pairs={{1022,0},{0,2},{2,4},{4,6},{6,8},{8,10},{10,12},{12,14},{14,16},{1... | collective-permute-start | bytes 1179656 | tf_op jit(solution)/shard_map/ppermute | solution.py:12
  51.4 0.3 fusion.34
  52.1 4.4 %collective-permute-done.4 = bf16[256,768]{1,0:T(8,128)(2,1)S(1)} collective-permute-done((bf16[256,768]{1,0:T(8,128)(2,1)S(1)}, bf16[256,768]{1,0:T(8,128)(2,1)S(1)}, u32[]{:S(2)}, u32[]{:S(2)}) %collective-permute-start.4) | collective-permute-done | bytes 393248 | tf_op jit(solution)/shard_map/ppermute | solution.py:12
  56.5 1.9 %collective-permute-start.5 = (bf16[256,768]{1,0:T(8,128)(2,1)S(1)}, bf16[256,768]{1,0:T(8,128)(2,1)S(1)}, u32[]{:S(2)}, u32[]{:S(2)}) collective-permute-start(bf16[256,768]{1,0:T(8,128)(2,1)S(1)} %add_convert_fusion.1), channel_id=1, source_target_pairs={{1022,0},{0,2},{2,4},{4,6},{6,8},{8,10},{10,12},{12,14},{14,16},{1... | collective-permute-start | bytes 1179656 | tf_op jit(solution)/shard_map/ppermute | solution.py:12
  58.4 5.9 %collective-permute-done.2 = bf16[256,768]{1,0:T(8,128)(2,1)S(1)} collective-permute-done((bf16[256,768]{1,0:T(8,128)(2,1)S(1)}, bf16[256,768]{1,0:T(8,128)(2,1)S(1)}, u32[]{:S(2)}, u32[]{:S(2)}) %collective-permute-start.2) | collective-permute-done | bytes 393248 | tf_op jit(solution)/shard_map/ppermute | solution.py:12
  65.1 6.2 %collective-permute-done.5 = bf16[256,768]{1,0:T(8,128)(2,1)S(1)} collective-permute-done((bf16[256,768]{1,0:T(8,128)(2,1)S(1)}, bf16[256,768]{1,0:T(8,128)(2,1)S(1)}, u32[]{:S(2)}, u32[]{:S(2)}) %collective-permute-start.5) | collective-permute-done | bytes 393248 | tf_op jit(solution)/shard_map/ppermute | solution.py:12
  71.4 8.7 %collective-permute-start.6 = (bf16[256,768]{1,0:T(8,128)(2,1)S(1)}, bf16[256,768]{1,0:T(8,128)(2,1)}, u32[]{:S(2)}, u32[]{:S(2)}) collective-permute-start(bf16[256,768]{1,0:T(8,128)(2,1)S(1)} %add_convert_fusion), channel_id=1, source_target_pairs={{6,0},{8,2},{10,4},{12,6},{14,8},{16,10},{18,12},{20,14},{22,16},{... | collective-permute-start | bytes 1179656 | tf_op jit(solution)/shard_map/ppermute | solution.py:12
  80.5 4.2 %collective-permute-done.6 = bf16[256,768]{1,0:T(8,128)(2,1)} collective-permute-done((bf16[256,768]{1,0:T(8,128)(2,1)S(1)}, bf16[256,768]{1,0:T(8,128)(2,1)}, u32[]{:S(2)}, u32[]{:S(2)}) %collective-permute-start.6) | collective-permute-done | bytes 393248 | tf_op jit(solution)/shard_map/ppermute | solution.py:12
  85.4 1.2 convolution_convert_fusion.2
  86.6 30.1 %reduce-scatter.2.cloned.1.call-done = bf16[128,768]{1,0:T(8,128)(2,1)} async-done(((bf16[256,768]{1,0:T(8,128)(2,1)}), bf16[128,768]{1,0:T(8,128)(2,1)}) %reduce-scatter.2.cloned.1.call-update) | async-done | bytes 196624 | tf_op jit(solution)/shard_map/reduce_scatter | solution.py:76
  116.7 1.1 fusion.36
  117.9 2.1 %convolution_convert_fusion.1 = bf16[128,768]{1,0:T(8,128)(2,1)} fusion(bf16[768,768]{1,0:T(8,128)(2,1)S(1)} %copy-done.1, bf16[128,768]{1,0:T(8,128)(2,1)} %reduce-scatter.2.cloned.1.call-done, f32[128,768]{1,0:T(8,128)S(1)} %get-tuple-element.5, f32[128]{0:T(128)S(1)} %fusion.36, f32[128]{0:T(128)S(1)} %add_rsqrt_fusion), kind=kOutput, calls=%fused_computation.4 | convolution fusion | flops 151683072 | bytes 1967104 | tf_op jit(solution)/shard_map/dot_general | solution.py:24
  (33 shorter events, 3.2 us)
Async XLA Ops:
  7.2 16.8 %copy-start = (bf16[768,768]{1,0:T(8,128)(2,1)S(1)}, bf16[768,768]{1,0:T(8,128)(2,1)}, u32[]{:S(2)}) copy-start(bf16[768,768]{1,0:T(8,128)(2,1)} %param.9) | copy-start | bytes 3538948
  7.2 16.7 %copy-start.4 = (bf16[128,768]{1,0:T(8,128)(2,1)S(1)}, bf16[128,768]{1,0:T(8,128)(2,1)}, u32[]{:S(2)}) copy-start(bf16[128,768]{1,0:T(8,128)(2,1)} %param.7) | copy-start | bytes 589828
  7.2 109.5 %reduce-scatter.2.cloned.1.call-start = ((), (), s32[]{:S(2)}) async-start(), calls=%async_computation.1 | async-start | bytes 589824 | tf_op jit(solution)/shard_map/reduce_scatter | solution.py:76
  15.0 19.7 %collective-permute-start = (bf16[256,768]{1,0:T(8,128)(2,1)S(1)}, bf16[256,768]{1,0:T(8,128)(2,1)S(1)}, u32[]{:S(2)}, u32[]{:S(2)}) collective-permute-start(bf16[256,768]{1,0:T(8,128)(2,1)S(1)} %all_gather.3), channel_id=1, source_target_pairs={{1022,0},{0,2},{2,4},{4,6},{6,8},{8,10},{10,12},{12,14},{14,16},{1... | collective-permute-start | bytes 1179656 | tf_op jit(solution)/shard_map/ppermute | solution.py:12
  23.9 0.7 copy-start.5
  26.0 14.4 %collective-permute-start.3 = (bf16[256,768]{1,0:T(8,128)(2,1)}, bf16[256,768]{1,0:T(8,128)(2,1)}, u32[]{:S(2)}, u32[]{:S(2)}) collective-permute-start(bf16[256,768]{1,0:T(8,128)(2,1)} %convolution_convert_fusion), channel_id=1, source_target_pairs={{1022,0},{0,2},{2,4},{4,6},{6,8},{8,10},{10,12},{12,14},{14,16},{1... | collective-permute-start | bytes 1179656 | tf_op jit(solution)/shard_map/ppermute | solution.py:12
  34.7 14.8 %collective-permute-start.1 = (bf16[256,768]{1,0:T(8,128)(2,1)S(1)}, bf16[256,768]{1,0:T(8,128)(2,1)S(1)}, u32[]{:S(2)}, u32[]{:S(2)}) collective-permute-start(bf16[256,768]{1,0:T(8,128)(2,1)S(1)} %collective-permute-done), channel_id=1, source_target_pairs={{1022,0},{0,2},{2,4},{4,6},{6,8},{8,10},{10,12},{12,14},{14,16},{1... | collective-permute-start | bytes 1179656 | tf_op jit(solution)/shard_map/ppermute | solution.py:12
  41.6 14.8 %collective-permute-start.4 = (bf16[256,768]{1,0:T(8,128)(2,1)S(1)}, bf16[256,768]{1,0:T(8,128)(2,1)S(1)}, u32[]{:S(2)}, u32[]{:S(2)}) collective-permute-start(bf16[256,768]{1,0:T(8,128)(2,1)S(1)} %add_convert_fusion.2), channel_id=1, source_target_pairs={{1022,0},{0,2},{2,4},{4,6},{6,8},{8,10},{10,12},{12,14},{14,16},{1... | collective-permute-start | bytes 1179656 | tf_op jit(solution)/shard_map/ppermute | solution.py:12
  49.5 14.8 %collective-permute-start.2 = (bf16[256,768]{1,0:T(8,128)(2,1)S(1)}, bf16[256,768]{1,0:T(8,128)(2,1)S(1)}, u32[]{:S(2)}, u32[]{:S(2)}) collective-permute-start(bf16[256,768]{1,0:T(8,128)(2,1)S(1)} %collective-permute-done.1), channel_id=1, source_target_pairs={{1022,0},{0,2},{2,4},{4,6},{6,8},{8,10},{10,12},{12,14},{14,16},{1... | collective-permute-start | bytes 1179656 | tf_op jit(solution)/shard_map/ppermute | solution.py:12
  56.5 14.8 %collective-permute-start.5 = (bf16[256,768]{1,0:T(8,128)(2,1)S(1)}, bf16[256,768]{1,0:T(8,128)(2,1)S(1)}, u32[]{:S(2)}, u32[]{:S(2)}) collective-permute-start(bf16[256,768]{1,0:T(8,128)(2,1)S(1)} %add_convert_fusion.1), channel_id=1, source_target_pairs={{1022,0},{0,2},{2,4},{4,6},{6,8},{8,10},{10,12},{12,14},{14,16},{1... | collective-permute-start | bytes 1179656 | tf_op jit(solution)/shard_map/ppermute | solution.py:12
  64.3 0.7 copy-start.2
  71.4 13.4 %collective-permute-start.6 = (bf16[256,768]{1,0:T(8,128)(2,1)S(1)}, bf16[256,768]{1,0:T(8,128)(2,1)}, u32[]{:S(2)}, u32[]{:S(2)}) collective-permute-start(bf16[256,768]{1,0:T(8,128)(2,1)S(1)} %add_convert_fusion), channel_id=1, source_target_pairs={{6,0},{8,2},{10,4},{12,6},{14,8},{16,10},{18,12},{20,14},{22,16},{... | collective-permute-start | bytes 1179656 | tf_op jit(solution)/shard_map/ppermute | solution.py:12
  80.5 4.5 %copy-start.3 = (bf16[256,768]{1,0:T(8,128)(2,1)S(1)}, bf16[256,768]{1,0:T(8,128)(2,1)}, u32[]{:S(2)}) copy-start(bf16[256,768]{1,0:T(8,128)(2,1)} %copy-done.2) | copy-start | bytes 1179652
  85.4 32.5 %copy-start.1 = (bf16[768,768]{1,0:T(8,128)(2,1)S(1)}, bf16[768,768]{1,0:T(8,128)(2,1)}, u32[]{:S(2)}) copy-start(bf16[768,768]{1,0:T(8,128)(2,1)} %param.10) | copy-start | bytes 3538948
Sparse Core Ops, SparseCore 0:
  84.9 31.7 reduce-scatter.1
where the time goes:
time: 127 us
  waiting for transfers between devices  67 us (53%)
  starting transfers between devices  25.9 us (20%)
  between operations  15.7 us (12%)
  matrix products  10.8 us (9%)
  blocking collectives  5.76 us (5%)
  other arithmetic  1.49 us (1%)
    ppermute x7, waiting for transfers between devices, passed_along(): return lax.ppermute(block, axis, route)  36.8 us
    reduce_scatter x1, waiting for transfers between devices, body(): lax.psum_scatter(carried.astype(jnp.bfloat16), 'group', scatter_dimension...  30.1 us
    ppermute x7, starting transfers between devices, passed_along(): return lax.ppermute(block, axis, route)  25.9 us
    all_gather x1, blocking collectives, body(): visiting = lax.all_gather(text_emb, 'group', axis=0, tiled=True)  5.76 us
    dot_general x2, matrix products, back_norm(): lax.dot_general(grad_x, proj, (((1,), (1,)), ((), ())), preferred_element...  3.37 us
    dot_general x4, matrix products, body(): lax.dot_general(coef, image_emb, (((0,), (0,)), ((), ())), preferred_elem...  2.86 us
  transfers between devices with their start and end apart: 8, of which 8 were waited for; matrix products, arithmetic and copies ran while one was open for 6% of the time, Pallas kernels for 0%

commit v1 on v0

v1 whole, which is shorter than its diff:
```python
import jax
import jax.numpy as jnp
from jax import lax
from jax.sharding import PartitionSpec as P

AXES = ("blk", "group")
KEY_ROWS = 16


def embed(feats, proj):
    x = jnp.dot(feats, proj, preferred_element_type=jnp.float32)
    inv = lax.rsqrt(jnp.sum(x * x, axis=-1, keepdims=True) + 1e-06)
    return (x * inv, inv)


def back_norm(grad, unit, inv, proj):
    inner = jnp.sum(grad * unit, axis=-1, keepdims=True)
    grad_x = (inv * (grad - inner * unit)).astype(jnp.bfloat16)
    out = lax.dot_general(
        grad_x, proj, (((1,), (1,)), ((), ())), preferred_element_type=jnp.float32
    )
    return out.astype(jnp.bfloat16)


def split_key(ids):
    return ((ids >> 8) & 255).astype(jnp.bfloat16), (ids & 255).astype(jnp.bfloat16)


def key_block(high, low, width):
    rows = jnp.stack([high, low])
    return jnp.pad(rows, ((0, KEY_ROWS - 2), (0, width - rows.shape[1])))


def joined_key(high, low):
    return high.astype(jnp.float32) * 256.0 + low.astype(jnp.float32)


def body(image_feats, text_feats, image_proj, text_proj, logit_scale, logit_bias, match):
    rows, width = image_feats.shape
    blk_count = lax.axis_size("blk")
    pair_count = blk_count // 2
    block = lax.axis_index("blk")
    half = lax.axis_index("group")
    core = block % 2
    on_text = core == 0

    def route(target):
        pairs = []
        for b in range(blk_count):
            for h in range(2):
                s, c, g = target(b // 2, b % 2, h)
                pairs.append((2 * b + h, 2 * (2 * (s % pair_count) + c) + g))
        return pairs

    def forward(core_id):
        return 1 if core_id == 0 else -1

    def flip(x):
        return lax.ppermute(x, AXES, route(lambda s, c, h: (s, 1 - c, h)))

    def swap_or_next(x):
        return lax.ppermute(
            x, AXES, route(lambda s, c, h: (s, c, 1 - h) if c == 0 else (s - 1, c, 1 - h))
        )

    def next_or_swap(x):
        return lax.ppermute(
            x, AXES, route(lambda s, c, h: (s + 1, c, 1 - h) if c == 0 else (s, c, 1 - h))
        )

    def second_next(x, cross):
        return lax.ppermute(
            x,
            AXES,
            route(lambda s, c, h: (s + 2 * forward(c), c, 1 - h if cross else h)),
        )

    high, low = split_key(match)
    raw = jnp.concatenate([image_feats, text_feats, key_block(high, low, width)])
    other = flip(raw)
    images = jnp.concatenate([image_feats, other[:rows]])
    texts = jnp.concatenate([text_feats, other[rows : 2 * rows]])
    image_unit, image_inv = embed(images, image_proj)
    text_unit, text_inv = embed(texts, text_proj)
    image_emb = image_unit.astype(jnp.bfloat16)
    text_emb = text_unit.astype(jnp.bfloat16)

    local = jnp.arange(rows, dtype=jnp.int32) + half * rows
    text_ids = jnp.concatenate([block * (2 * rows) + local, (block ^ 1) * (2 * rows) + local])
    text_high, text_low = split_key(text_ids)
    match_high = jnp.concatenate([high, other[2 * rows, :rows]])
    match_low = jnp.concatenate([low, other[2 * rows + 1, :rows]])

    def pick(text_value, image_value):
        return jnp.where(on_text, text_value, image_value)

    keys = key_block(pick(text_high, match_high), pick(text_low, match_low), width)
    sent = jnp.concatenate([pick(text_emb, image_emb), keys])
    row_key = pick(joined_key(match_high, match_low), joined_key(text_high, text_low))
    row_emb = pick(image_emb, text_emb)
    row_unit = pick(image_unit, text_unit)
    row_inv = pick(image_inv, text_inv)
    row_proj = pick(image_proj, text_proj)
    scale = logit_scale[0]
    bias = logit_bias[0]

    def pair_grad(row_from, row_to, cols, key_row, lane):
        col_emb = cols
        n = col_emb.shape[0]
        col_key = joined_key(key_row[0, lane : lane + n], key_row[1, lane : lane + n])
        sign = jnp.where(
            row_key[row_from:row_to, None] == col_key[None, :], jnp.float32(1.0), jnp.float32(-1.0)
        )
        logits = (
            scale
            * lax.dot_general(
                row_emb[row_from:row_to],
                col_emb,
                (((1,), (1,)), ((), ())),
                preferred_element_type=jnp.float32,
            )
            + bias
        )
        coef = (-sign * jax.nn.sigmoid(-sign * logits) * scale).astype(jnp.bfloat16)
        return jnp.dot(coef, col_emb, preferred_element_type=jnp.float32)

    first = swap_or_next(sent)
    second = next_or_swap(sent)
    third = second_next(sent[rows:], False)
    fourth = second_next(sent[rows:], True)
    fifth = next_or_swap(first)

    both = 2 * rows
    swapped = pick(first, second)
    near = pick(second, first)

    def block_grad(got, own_cols_only):
        keys_at = got[both:]
        if own_cols_only:
            top = pair_grad(0, rows, got[:rows], keys_at, 0)
            bottom = pair_grad(rows, both, got[:both], keys_at, 0)
            return jnp.concatenate([top, bottom])
        return pair_grad(0, both, got[:both], keys_at, 0)

    def last_grad(got):
        return pair_grad(0, rows, got[:rows], got[rows:], rows)

    grad = block_grad(sent, True)
    grad = grad + block_grad(swapped, True)
    grad = grad + block_grad(near, False)
    tail = last_grad(third) + last_grad(fourth)
    grad = grad + block_grad(fifth, False)
    grad = jnp.concatenate([grad[:rows] + tail, grad[rows:]])
    out = back_norm(grad, row_unit, row_inv, row_proj)
    own, given = out[:rows], flip(out[rows:])
    return pick(own, given), pick(given, own)


def solution(mesh):
    return jax.shard_map(
        body,
        mesh=mesh,
        in_specs=(
            P(AXES, None),
            P(AXES, None),
            P(),
            P(),
            P(),
            P(),
            P(AXES),
        ),
        out_specs=(P(AXES, None), P(AXES, None)),
        check_vma=False,
    )
```

time: 127 us -> 80 us (0.63)
  waiting for transfers between devices: 67 us -> 7.3 us
  starting transfers between devices: 25.9 us -> 44.5 us
  between operations: 15.7 us -> 2.21 us
  matrix products: 10.8 us -> 17 us
  blocking collectives: 5.76 us -> 0 us
  other arithmetic: 1.49 us -> 6.22 us
  local copies, waits for them, and re-layouts: 0.26 us -> 2.21 us
    reduce_scatter x1 -> x0, waiting for transfers between devices: 30.1 us -> none  [body(): lax.psum_scatter(carried.astype(jnp.bfloat16), 'group', scatter_dimension...]
    ppermute x7, waiting for transfers between devices: 36.8 us -> 7.3 us  [the longest x2 3.81 us: next_or_swap(): lax.ppermute(x, AXES, route(lambda s, c, h: (s + 1, c, 1 - h) if c == 0 e...]
    ppermute x7, starting transfers between devices: 25.9 us -> 44.5 us  [the longest x2 24.9 us: flip(): return lax.ppermute(x, AXES, route(lambda s, c, h: (s, 1 - c, h)))]
    dot_general x12 -> x8, matrix products: 5.15 us -> 13.8 us  [pair_grad(): return jnp.dot(coef, col_emb, preferred_element_type=jnp.float32)]
    all_gather x1 -> x0, blocking collectives: 5.76 us -> none  [body(): visiting = lax.all_gather(text_emb, 'group', axis=0, tiled=True)]
    dot_general x2 -> x1, matrix products: 3.37 us -> 0.66 us  [back_norm(): lax.dot_general(grad_x, proj, (((1,), (1,)), ((), ())), preferred_element...]
    select_n x0 -> x6, other arithmetic: none -> 2.1 us  [pick(): return jnp.where(on_text, text_value, image_value)]
    unnamed x12 -> x14, local copies, waits for them, and re-layouts: 0.26 us -> 2.13 us
  transfers between devices with their start and end apart: 8 -> 7, of which waited for: 8 -> 4; matrix products, arithmetic and copies ran while one was open for 6% -> 12% of each run, Pallas kernels for 0% -> 0%
where the time goes in v1:
time: 80 us; the launch traced here: 79.4 us
  starting transfers between devices  44.5 us (56%)
  matrix products  17 us (21%)
  waiting for transfers between devices  7.3 us (9%)
  other arithmetic  6.22 us (8%)
  local copies, waits for them, and re-layouts  2.21 us (3%)
  between operations  2.21 us (3%)
    ppermute x2, starting transfers between devices, flip(): return lax.ppermute(x, AXES, route(lambda s, c, h: (s, 1 - c, h)))  24.9 us
    dot_general x8, matrix products, pair_grad(): return jnp.dot(coef, col_emb, preferred_element_type=jnp.float32)  13.8 us
    ppermute x1, starting transfers between devices, swap_or_next(): lax.ppermute(x, AXES, route(lambda s, c, h: (s, c, 1 - h) if c == 0 else...  10.9 us
    ppermute x2, starting transfers between devices, second_next(): lax.ppermute(x, AXES, route(lambda s, c, h: (s + 2 * forward(c), c, 1 - h...  4.47 us
    ppermute x2, starting transfers between devices, next_or_swap(): lax.ppermute(x, AXES, route(lambda s, c, h: (s + 1, c, 1 - h) if c == 0 e...  4.13 us
    ppermute x2, waiting for transfers between devices, next_or_swap(): lax.ppermute(x, AXES, route(lambda s, c, h: (s + 1, c, 1 - h) if c == 0 e...  3.81 us
    dot_general x2, matrix products, embed(): x = jnp.dot(feats, proj, preferred_element_type=jnp.float32)  2.5 us
    ppermute x2, waiting for transfers between devices, second_next(): lax.ppermute(x, AXES, route(lambda s, c, h: (s + 2 * forward(c), c, 1 - h...  2.39 us
  transfers between devices with their start and end apart: 7, of which 4 were waited for; matrix products, arithmetic and copies ran while one was open for 12% of the time, Pallas kernels for 0%

profile of v1, /device:TPU:1, one launch (start us, length us, event | category | flops | bytes accessed | tf_op | source)
XLA Modules:
  0.0 79.4 jit_solution(2778709543596953158)
XLA Ops:
  1.4 1.1 %pad_maximum_fusion.2 = bf16[272,768]{1,0:T(8,128)(2,1)S(1)} fusion(bf16[16,768]{1,0:T(8,128)(2,1)S(1)} %fusion.203, bf16[128,768]{1,0:T(8,128)(2,1)} %param.8, bf16[128,768]{1,0:T(8,128)(2,1)} %param.7), kind=kLoop, calls=%fused_computation.102 | loop fusion | flops 1253376 | bytes 835584 | tf_op jit(solution)/shard_map/concatenate | solution.py:79
  2.4 16.1 %collective-permute-start = (bf16[272,768]{1,0:T(8,128)(2,1)S(1)}, bf16[272,768]{1,0:T(8,128)(2,1)S(1)}, u32[]{:S(2)}, u32[]{:S(2)}) collective-permute-start(bf16[272,768]{1,0:T(8,128)(2,1)S(1)} %pad_maximum_fusion.2), channel_id=1, source_target_pairs={{0,2},{1,3},{2,0},{3,1},{4,6},{5,7},{6,4},{7,5},{8,10},{9,11},{10,... | collective-permute-start | bytes 1253384 | tf_op jit(solution)/shard_map/ppermute | solution.py:59
  20.0 1.9 %multiply_reduce_fusion.2 = (f32[256]{0:T(256)S(1)}, f32[256,768]{1,0:T(8,128)S(1)}) fusion(bf16[768,768]{1,0:T(8,128)(2,1)} %param.9, bf16[128,768]{1,0:T(8,128)(2,1)S(1)} %get-tuple-element.13, bf16[128,768]{1,0:T(8,128)(2,1)S(1)} %copy-done.1), kind=kOutput, calls=%fused_computation.96 | convolution fusion | flops 303169280 | bytes 2360320 | tf_op jit(solution)/shard_map/dot_general | solution.py:11
  22.7 1.9 %collective-permute-start.2 = (bf16[272,768]{1,0:T(8,128)(2,1)S(1)}, bf16[272,768]{1,0:T(8,128)(2,1)S(1)}, u32[]{:S(2)}, u32[]{:S(2)}) collective-permute-start(bf16[272,768]{1,0:T(8,128)(2,1)S(1)} %pad_maximum_fusion.1), channel_id=1, source_target_pairs={{0,5},{1,4},{2,3},{3,2},{4,9},{5,8},{6,7},{7,6},{8,13},{9,12},{10,... | collective-permute-start | bytes 1253384 | tf_op jit(solution)/shard_map/ppermute | solution.py:67
  24.7 10.9 %collective-permute-start.1 = (bf16[272,768]{1,0:T(8,128)(2,1)S(1)}, bf16[272,768]{1,0:T(8,128)(2,1)}, u32[]{:S(2)}, u32[]{:S(2)}) collective-permute-start(bf16[272,768]{1,0:T(8,128)(2,1)S(1)} %pad_maximum_fusion.1), channel_id=1, source_target_pairs={{0,1},{1,0},{2,1023},{3,1022},{4,5},{5,4},{6,3},{7,2},{8,9},{9,8},... | collective-permute-start | bytes 1253384 | tf_op jit(solution)/shard_map/ppermute | solution.py:62
  36.3 2.4 %collective-permute-start.5 = (bf16[144,768]{1,0:T(8,128)(2,1)}, bf16[144,768]{1,0:T(8,128)(2,1)}, u32[]{:S(2)}, u32[]{:S(2)}) collective-permute-start(bf16[144,768]{1,0:T(8,128)(2,1)} %fusion.101), channel_id=1, source_target_pairs={{0,9},{1,8},{2,1019},{3,1018},{4,13},{5,12},{6,1023},{7,1022},{8,1... | collective-permute-start | bytes 663560 | tf_op jit(solution)/shard_map/ppermute | solution.py:72
  38.7 2.1 %collective-permute-start.4 = (bf16[144,768]{1,0:T(8,128)(2,1)}, bf16[144,768]{1,0:T(8,128)(2,1)S(1)}, u32[]{:S(2)}, u32[]{:S(2)}) collective-permute-start(bf16[144,768]{1,0:T(8,128)(2,1)} %fusion.101), channel_id=1, source_target_pairs={{0,8},{1,9},{2,1018},{3,1019},{4,12},{5,13},{6,1022},{7,1023},{8,1... | collective-permute-start | bytes 663560 | tf_op jit(solution)/shard_map/ppermute | solution.py:72
  40.8 1.3 %fusion.39 = f32[128,768]{1,0:T(8,128)} fusion(bf16[256,768]{1,0:T(8,128)(2,1)S(1)} %get-tuple-element.2, bf16[256,768]{1,0:T(8,128)(2,1)S(1)} %get-tuple-element.3, f32[]{:T(128)} %bitcast.38, f32[]{:T(128)} %bitcast.33, f32[256]{0:T(256)S(1)} %get-tuple-element.15, f32[128]{0:T(128)S(1)} %get-tuple-element.20), kind=kOutput, calls=%fused_computation.47 | convolution fusion | flops 101056512 | bytes 1377800 | tf_op jit(solution)/shard_map/dot_general | solution.py:125
  42.1 1.2 %fusion.76 = f32[128,768]{1,0:T(8,128)} fusion(bf16[256,768]{1,0:T(8,128)(2,1)S(1)} %get-tuple-element.2, bf16[256,768]{1,0:T(8,128)(2,1)S(1)} %get-tuple-element.3, f32[]{:T(128)} %bitcast.37, f32[]{:T(128)} %bitcast.36, f32[128]{0:T(128)S(1)} %fusion.220, f32[128]{0:T(128)S(1)} %get-tuple-element.19), kind=kOutput, calls=%fused_computation.88 | convolution fusion | flops 50528256 | bytes 984072 | tf_op jit(solution)/shard_map/dot_general | solution.py:125
  43.3 1.1 %collective-permute-done.5 = bf16[144,768]{1,0:T(8,128)(2,1)} collective-permute-done((bf16[144,768]{1,0:T(8,128)(2,1)}, bf16[144,768]{1,0:T(8,128)(2,1)}, u32[]{:S(2)}, u32[]{:S(2)}) %collective-permute-start.5) | collective-permute-done | bytes 221216 | tf_op jit(solution)/shard_map/ppermute | solution.py:72
  45.1 1.3 %collective-permute-done.4 = bf16[144,768]{1,0:T(8,128)(2,1)S(1)} collective-permute-done((bf16[144,768]{1,0:T(8,128)(2,1)}, bf16[144,768]{1,0:T(8,128)(2,1)S(1)}, u32[]{:S(2)}, u32[]{:S(2)}) %collective-permute-start.4) | collective-permute-done | bytes 221216 | tf_op jit(solution)/shard_map/ppermute | solution.py:72
  47.0 2.2 %fusion.78 = f32[128,768]{1,0:T(8,128)} fusion(bf16[144,768]{1,0:T(8,128)(2,1)} %collective-permute-done.5, bf16[256,768]{1,0:T(8,128)(2,1)S(1)} %get-tuple-element.3, f32[128]{0:T(128)S(1)} %fusion.211, f32[]{:T(128)} %bitcast.42, f32[]{:T(128)} %bitcast.29, f32[128]{0:T(128)S(1)} %get-tuple-element.19), kind=kOutput, calls=%fused_computation.90 | convolution fusion | flops 50528256 | bytes 985088 | tf_op jit(solution)/shard_map/dot_general | solution.py:125
  49.2 1.1 %broadcast_select_fusion = (bf16[272,768]{1,0:T(8,128)(2,1)S(1)}, bf16[272,768]{1,0:T(8,128)(2,1)S(1)}) fusion(bf16[272,768]{1,0:T(8,128)(2,1)S(1)} %collective-permute-done.2, bf16[272,768]{1,0:T(8,128)(2,1)} %collective-permute-done.1, pred[]{:T(512)S(6)} %eq.56), kind=kLoop, calls=%fused_computation.103 | loop fusion | flops 417792 | bytes 1671169 | tf_op jit(solution)/shard_map/jit(_where)/select_n | solution.py:95
  50.3 1.3 %fusion.38 = f32[128,768]{1,0:T(8,128)} fusion(bf16[272,768]{1,0:T(8,128)(2,1)S(1)} %get-tuple-element.5, bf16[256,768]{1,0:T(8,128)(2,1)S(1)} %get-tuple-element.3, f32[256]{0:T(256)S(1)} %bitcast.49, f32[]{:T(128)} %bitcast.41, f32[]{:T(128)} %bitcast.30, f32[128]{0:T(128)S(1)} %get-tuple-element.20), kind=kOutput, calls=%fused_computation.46 | convolution fusion | flops 101056512 | bytes 1377800 | tf_op jit(solution)/shard_map/dot_general | solution.py:125
  51.6 1.2 %fusion.77 = f32[128,768]{1,0:T(8,128)} fusion(bf16[272,768]{1,0:T(8,128)(2,1)S(1)} %get-tuple-element.5, bf16[256,768]{1,0:T(8,128)(2,1)S(1)} %get-tuple-element.3, f32[128]{0:T(128)S(1)} %fusion.217, f32[]{:T(128)} %bitcast.44, f32[]{:T(128)} %bitcast.34, f32[128]{0:T(128)S(1)} %get-tuple-element.19), kind=kOutput, calls=%fused_computation.89 | convolution fusion | flops 50528256 | bytes 984072 | tf_op jit(solution)/shard_map/dot_general | solution.py:125
  52.8 2.2 %collective-permute-start.3 = (bf16[272,768]{1,0:T(8,128)(2,1)}, bf16[272,768]{1,0:T(8,128)(2,1)S(1)}, u32[]{:S(2)}, u32[]{:S(2)}) collective-permute-start(bf16[272,768]{1,0:T(8,128)(2,1)} %collective-permute-done.1), channel_id=1, source_target_pairs={{0,5},{1,4},{2,3},{3,2},{4,9},{5,8},{6,7},{7,6},{8,13},{9,12},{10,... | collective-permute-start | bytes 1253384 | tf_op jit(solution)/shard_map/ppermute | solution.py:67
  55.1 2.9 %convolution_add_fusion.1 = f32[256,768]{1,0:T(8,128)} fusion(bf16[256,768]{1,0:T(8,128)(2,1)S(1)} %get-tuple-element.3, f32[128,768]{1,0:T(8,128)} %fusion.39, f32[128,768]{1,0:T(8,128)} %fusion.76, f32[128,768]{1,0:T(8,128)} %fusion.38, f32[128,768]{1,0:T(8,128)} %fusion.77, bf16[272,768]{1,0:T(8,128)(2,1)S(1)} %get-tuple-element.4, f32[]{:T(128)} %bitcast.39, ...), kind=kOutput, calls=%fused_computation.1 | convolution fusion | flops 202899456 | bytes 3541000 | tf_op jit(solution)/shard_map/dot_general | solution.py:125
  58.0 3.8 %collective-permute-done.3 = bf16[272,768]{1,0:T(8,128)(2,1)S(1)} collective-permute-done((bf16[272,768]{1,0:T(8,128)(2,1)}, bf16[272,768]{1,0:T(8,128)(2,1)S(1)}, u32[]{:S(2)}, u32[]{:S(2)}) %collective-permute-start.3) | collective-permute-done | bytes 417824 | tf_op jit(solution)/shard_map/ppermute | solution.py:67
  62.6 2.1 %convolution_add_fusion = f32[256,768]{1,0:T(8,128)S(1)} fusion(f32[256,768]{1,0:T(8,128)} %convolution_add_fusion.1, bf16[256,768]{1,0:T(8,128)(2,1)S(1)} %get-tuple-element.3, bf16[272,768]{1,0:T(8,128)(2,1)} %copy-done.3, f32[256]{0:T(256)S(1)} %bitcast.48, f32[]{:T(128)} %bitcast.40, f32[]{:T(128)} %bitcast.31, f32[256]{0:T(256)S(1)} %get-tuple-element.14), kind=kOutput, calls=%fused_computation | convolution fusion | flops 202309632 | bytes 2755584 | tf_op jit(solution)/shard_map/dot_general | solution.py:125
  64.7 1.7 %slice_add_fusion = f32[128,768]{1,0:T(8,128)S(1)} fusion(f32[256,768]{1,0:T(8,128)S(1)} %convolution_add_fusion, f32[128,768]{1,0:T(8,128)} %fusion.78, bf16[144,768]{1,0:T(8,128)(2,1)} %copy-done, bf16[256,768]{1,0:T(8,128)(2,1)S(1)} %get-tuple-element.3, f32[128]{0:T(128)} %fusion.214, f32[]{:T(128)} %bitcast.43, f32[]{:T(128)} %bitcast.35, ...), kind=kOutput, calls=%fused_computation.105 | convolution fusion | flops 50724864 | bytes 1771520 | tf_op jit(solution)/shard_map/dot_general | solution.py:125
  66.6 1.0 %copy-done.4 = bf16[768,768]{1,0:T(8,128)(2,1)S(1)} copy-done((bf16[768,768]{1,0:T(8,128)(2,1)S(1)}, bf16[768,768]{1,0:T(8,128)(2,1)}, u32[]{:S(2)}) %copy-start.4) | copy-done | bytes 1179672
  68.7 8.9 %collective-permute-start.6 = (bf16[128,768]{1,0:T(8,128)(2,1)S(1)}, bf16[128,768]{1,0:T(8,128)(2,1)S(1)}, u32[]{:S(2)}, u32[]{:S(2)}) collective-permute-start(bf16[128,768]{1,0:T(8,128)(2,1)S(1)} %slice.202), channel_id=1, source_target_pairs={{0,2},{1,3},{2,0},{3,1},{4,6},{5,7},{6,4},{7,5},{8,10},{9,11},{10,... | collective-permute-start | bytes 589832 | tf_op jit(solution)/shard_map/ppermute | solution.py:59
  77.5 1.0 %collective-permute-done.6 = bf16[128,768]{1,0:T(8,128)(2,1)S(1)} collective-permute-done((bf16[128,768]{1,0:T(8,128)(2,1)S(1)}, bf16[128,768]{1,0:T(8,128)(2,1)S(1)}, u32[]{:S(2)}, u32[]{:S(2)}) %collective-permute-start.6) | collective-permute-done | bytes 196640 | tf_op jit(solution)/shard_map/ppermute | solution.py:59
  78.6 0.8 broadcast_select_fusion.4
  (41 shorter events, 5.8 us)
Async XLA Ops:
  0.6 19.3 %copy-start.1 = (bf16[128,768]{1,0:T(8,128)(2,1)S(1)}, bf16[128,768]{1,0:T(8,128)(2,1)}, u32[]{:S(2)}) copy-start(bf16[128,768]{1,0:T(8,128)(2,1)} %param.7) | copy-start | bytes 589828
  2.4 17.4 %collective-permute-start = (bf16[272,768]{1,0:T(8,128)(2,1)S(1)}, bf16[272,768]{1,0:T(8,128)(2,1)S(1)}, u32[]{:S(2)}, u32[]{:S(2)}) collective-permute-start(bf16[272,768]{1,0:T(8,128)(2,1)S(1)} %pad_maximum_fusion.2), channel_id=1, source_target_pairs={{0,2},{1,3},{2,0},{3,1},{4,6},{5,7},{6,4},{7,5},{8,10},{9,11},{10,... | collective-permute-start | bytes 1253384 | tf_op jit(solution)/shard_map/ppermute | solution.py:59
  19.9 2.0 %copy-start.2 = (bf16[128,768]{1,0:T(8,128)(2,1)S(1)}, bf16[128,768]{1,0:T(8,128)(2,1)}, u32[]{:S(2)}) copy-start(bf16[128,768]{1,0:T(8,128)(2,1)} %param.8) | copy-start | bytes 589828
  19.9 2.0 %copy-start.5 = (bf16[768,768]{1,0:T(8,128)(2,1)S(1)}, bf16[768,768]{1,0:T(8,128)(2,1)}, u32[]{:S(2)}) copy-start(bf16[768,768]{1,0:T(8,128)(2,1)} %param.10) | copy-start | bytes 3538948
  22.7 26.5 %collective-permute-start.2 = (bf16[272,768]{1,0:T(8,128)(2,1)S(1)}, bf16[272,768]{1,0:T(8,128)(2,1)S(1)}, u32[]{:S(2)}, u32[]{:S(2)}) collective-permute-start(bf16[272,768]{1,0:T(8,128)(2,1)S(1)} %pad_maximum_fusion.1), channel_id=1, source_target_pairs={{0,5},{1,4},{2,3},{3,2},{4,9},{5,8},{6,7},{7,6},{8,13},{9,12},{10,... | collective-permute-start | bytes 1253384 | tf_op jit(solution)/shard_map/ppermute | solution.py:67
  24.7 24.6 %collective-permute-start.1 = (bf16[272,768]{1,0:T(8,128)(2,1)S(1)}, bf16[272,768]{1,0:T(8,128)(2,1)}, u32[]{:S(2)}, u32[]{:S(2)}) collective-permute-start(bf16[272,768]{1,0:T(8,128)(2,1)S(1)} %pad_maximum_fusion.1), channel_id=1, source_target_pairs={{0,1},{1,0},{2,1023},{3,1022},{4,5},{5,4},{6,3},{7,2},{8,9},{9,8},... | collective-permute-start | bytes 1253384 | tf_op jit(solution)/shard_map/ppermute | solution.py:62
  36.3 8.1 %collective-permute-start.5 = (bf16[144,768]{1,0:T(8,128)(2,1)}, bf16[144,768]{1,0:T(8,128)(2,1)}, u32[]{:S(2)}, u32[]{:S(2)}) collective-permute-start(bf16[144,768]{1,0:T(8,128)(2,1)} %fusion.101), channel_id=1, source_target_pairs={{0,9},{1,8},{2,1019},{3,1018},{4,13},{5,12},{6,1023},{7,1022},{8,1... | collective-permute-start | bytes 663560 | tf_op jit(solution)/shard_map/ppermute | solution.py:72
  38.7 7.7 %collective-permute-start.4 = (bf16[144,768]{1,0:T(8,128)(2,1)}, bf16[144,768]{1,0:T(8,128)(2,1)S(1)}, u32[]{:S(2)}, u32[]{:S(2)}) collective-permute-start(bf16[144,768]{1,0:T(8,128)(2,1)} %fusion.101), channel_id=1, source_target_pairs={{0,8},{1,9},{2,1018},{3,1019},{4,12},{5,13},{6,1022},{7,1023},{8,1... | collective-permute-start | bytes 663560 | tf_op jit(solution)/shard_map/ppermute | solution.py:72
  46.5 3.8 %copy-start = (bf16[144,768]{1,0:T(8,128)(2,1)}, bf16[144,768]{1,0:T(8,128)(2,1)S(1)}, u32[]{:S(2)}) copy-start(bf16[144,768]{1,0:T(8,128)(2,1)S(1)} %collective-permute-done.4) | copy-start | bytes 663556
  52.8 9.0 %collective-permute-start.3 = (bf16[272,768]{1,0:T(8,128)(2,1)}, bf16[272,768]{1,0:T(8,128)(2,1)S(1)}, u32[]{:S(2)}, u32[]{:S(2)}) collective-permute-start(bf16[272,768]{1,0:T(8,128)(2,1)} %collective-permute-done.1), channel_id=1, source_target_pairs={{0,5},{1,4},{2,3},{3,2},{4,9},{5,8},{6,7},{7,6},{8,13},{9,12},{10,... | collective-permute-start | bytes 1253384 | tf_op jit(solution)/shard_map/ppermute | solution.py:67
  61.8 0.8 copy-start.3
  66.3 1.3 %copy-start.4 = (bf16[768,768]{1,0:T(8,128)(2,1)S(1)}, bf16[768,768]{1,0:T(8,128)(2,1)}, u32[]{:S(2)}) copy-start(bf16[768,768]{1,0:T(8,128)(2,1)} %param.9) | copy-start | bytes 3538948
  66.4 1.6 %copy-start.6 = (bf16[768,768]{1,0:T(8,128)(2,1)S(1)}, bf16[768,768]{1,0:T(8,128)(2,1)}, u32[]{:S(2)}) copy-start(bf16[768,768]{1,0:T(8,128)(2,1)} %param.10) | copy-start | bytes 3538948
  68.7 9.9 %collective-permute-start.6 = (bf16[128,768]{1,0:T(8,128)(2,1)S(1)}, bf16[128,768]{1,0:T(8,128)(2,1)S(1)}, u32[]{:S(2)}, u32[]{:S(2)}) collective-permute-start(bf16[128,768]{1,0:T(8,128)(2,1)S(1)} %slice.202), channel_id=1, source_target_pairs={{0,2},{1,3},{2,0},{3,1},{4,6},{5,7},{6,4},{7,5},{8,10},{9,11},{10,... | collective-permute-start | bytes 589832 | tf_op jit(solution)/shard_map/ppermute | solution.py:59

commit v2 on v0

v2 whole, which is shorter than its diff:
```python
import functools

import jax
import jax.numpy as jnp
from jax import lax
from jax.experimental import pallas as pl
from jax.experimental.pallas import tpu as pltpu
from jax.sharding import PartitionSpec as P

AXES = ("blk", "group")
KEY_ROWS = 16
F32 = jnp.float32
BF16 = jnp.bfloat16


def rows_dot(a, b):
    return lax.dot_general(a, b, (((1,), (1,)), ((), ())), preferred_element_type=F32)


def key_tile(high, low, width):
    row = lax.broadcasted_iota(jnp.int32, (KEY_ROWS, width), 0)
    return jnp.where(row == 0, high, jnp.where(row == 1, low, 0)).astype(F32).astype(BF16)


def place():
    block = lax.axis_index("blk")
    return block, lax.axis_index("group"), lax.rem(block, 2)


def text_key_tile(block, half, rows):
    lane = lax.broadcasted_iota(jnp.int32, (KEY_ROWS, rows), 1)
    return key_tile(block & 255, half * rows + lane, rows)


def as_column(key):
    n = key.shape[1]
    eye = lax.broadcasted_iota(jnp.int32, (n, n), 0) == lax.broadcasted_iota(jnp.int32, (n, n), 1)
    return jnp.sum(jnp.where(eye, key, 0.0), axis=1, keepdims=True)


def joined_key(tile):
    return tile[0:1].astype(F32) * 256.0 + tile[1:2].astype(F32)


def pack_kernel(
    image_ref,
    text_ref,
    match_ref,
    raw_ref,
    match_vmem,
    sems,
):
    rows, width = image_ref.shape
    copies = [
        pltpu.make_async_copy(match_ref, match_vmem, sems.at[0]),
        pltpu.make_async_copy(image_ref, raw_ref.at[:rows], sems.at[1]),
        pltpu.make_async_copy(text_ref, raw_ref.at[rows : 2 * rows], sems.at[2]),
    ]
    for copy in copies:
        copy.start()
    raw_ref[2 * rows :, rows:] = jnp.zeros((KEY_ROWS, width - rows), BF16)
    copies[0].wait()
    match = match_vmem[...]
    raw_ref[2 * rows :, :rows] = key_tile((match >> 8) & 255, match & 255, rows)
    for copy in copies[1:]:
        copy.wait()


def load_kernel(raw_ref, image_proj_ref, text_proj_ref, col_proj_ref, row_proj_ref, sems):
    _, _, core = place()

    def load(col_from, row_from):
        copies = [
            pltpu.make_async_copy(col_from, col_proj_ref, sems.at[0]),
            pltpu.make_async_copy(row_from, row_proj_ref, sems.at[1]),
        ]
        for copy in copies:
            copy.start()
        for copy in copies:
            copy.wait()

    @pl.when(core == 0)
    def _():
        load(text_proj_ref, image_proj_ref)

    @pl.when(core == 1)
    def _():
        load(image_proj_ref, text_proj_ref)


def normed(feats, proj):
    x = jnp.dot(feats, proj, preferred_element_type=F32)
    inv = lax.rsqrt(jnp.sum(x * x, axis=-1, keepdims=True) + 1e-06)
    return x * inv, inv


def sent_kernel(raw_ref, other_ref, proj_ref, sent_ref, again_ref, far_ref):
    rows = (raw_ref.shape[0] - KEY_ROWS) // 2
    both = 2 * rows
    width = raw_ref.shape[1]
    block, half, core = place()
    start = pl.multiple_of((1 - core) * rows, rows)
    for n, ref in enumerate((raw_ref, other_ref)):
        unit, _ = normed(ref[pl.ds(start, rows)], proj_ref[...])
        sent_ref[n * rows : (n + 1) * rows] = unit.astype(BF16)
        sent_ref[both:, n * rows : (n + 1) * rows] = jnp.where(
            core == 0, text_key_tile(block ^ n, half, rows), ref[both:, :rows]
        )
    sent_ref[both:, both:] = jnp.zeros((KEY_ROWS, width - both), BF16)
    again_ref[...] = sent_ref[...]
    far_ref[...] = sent_ref[rows:]


def pair_grad(row_emb, row_key, col_emb, col_tile):
    scale, bias = row_key[:, 1:2], row_key[:, 2:3]
    logits = scale * rows_dot(row_emb, col_emb) + bias
    sign = jnp.where(row_key[:, :1] == joined_key(col_tile), F32(1.0), F32(-1.0))
    coef = (-sign * scale / (1.0 + jnp.exp(sign * logits))).astype(BF16)
    return jnp.dot(coef, col_emb, preferred_element_type=F32)


def own_kernel(
    raw_ref,
    other_ref,
    sent_ref,
    proj_ref,
    scale_ref,
    bias_ref,
    emb_ref,
    unit_ref,
    inv_ref,
    key_ref,
    grad_ref,
):
    rows = (raw_ref.shape[0] - KEY_ROWS) // 2
    both = 2 * rows
    block, half, core = place()
    start = pl.multiple_of(core * rows, rows)
    lane = lax.broadcasted_iota(jnp.int32, (rows, 128), 1)
    for n, ref in enumerate((raw_ref, other_ref)):
        at = slice(n * rows, (n + 1) * rows)
        unit, inv = normed(ref[pl.ds(start, rows)], proj_ref[...])
        unit_ref[at] = unit
        inv_ref[at] = jnp.broadcast_to(inv, (rows, 128))
        emb_ref[at] = unit.astype(BF16)
        tile = jnp.where(core == 0, ref[both:, :rows], text_key_tile(block ^ n, half, rows))
        scalars = jnp.where(lane == 1, scale_ref[0], bias_ref[0])
        key_ref[at] = jnp.where(lane == 0, as_column(joined_key(tile)), scalars)
    own_pairs(emb_ref, key_ref, sent_ref, grad_ref, False)


def own_pairs(emb_ref, key_ref, cols_ref, grad_ref, add):
    rows = emb_ref.shape[0] // 2
    both = 2 * rows
    top = pair_grad(emb_ref[:rows], key_ref[:rows], cols_ref[:rows], cols_ref[both:, :rows])
    bottom = pair_grad(emb_ref[rows:], key_ref[rows:], cols_ref[:both], cols_ref[both:, :both])
    if add:
        top = grad_ref[:rows] + top
        bottom = grad_ref[rows:] + bottom
    grad_ref[:rows] = top
    grad_ref[rows:] = bottom


def all_pairs(emb_ref, key_ref, cols_ref):
    both = emb_ref.shape[0]
    return pair_grad(emb_ref[...], key_ref[...], cols_ref[:both], cols_ref[both:, :both])


def after_kernel(*refs):
    pass


def far_kernel(emb_ref, key_ref, third_ref, fourth_ref, grad_ref, out_ref):
    both = emb_ref.shape[0]
    rows = both // 2
    total = grad_ref[:rows]
    for far_ref in (third_ref, fourth_ref):
        total += pair_grad(
            emb_ref[:rows], key_ref[:rows], far_ref[:rows], far_ref[rows:, rows:both]
        )
    out_ref[:rows] = total
    out_ref[rows:] = grad_ref[rows:]


def near_kernel(emb_ref, key_ref, first_ref, second_ref, grad_ref, out_ref):
    _, _, core = place()
    out_ref[...] = grad_ref[...]

    def pairs(swapped_ref, near_ref):
        own_pairs(emb_ref, key_ref, swapped_ref, out_ref, True)
        out_ref[...] += all_pairs(emb_ref, key_ref, near_ref)

    @pl.when(core == 0)
    def _():
        pairs(first_ref, second_ref)

    @pl.when(core == 1)
    def _():
        pairs(second_ref, first_ref)


def back_kernel(start, emb_ref, key_ref, cols_ref, grad_ref, unit_ref, inv_ref, proj_ref, out_ref):
    rows = out_ref.shape[0]
    both = 2 * rows
    at = slice(start, start + rows)
    grad = grad_ref[at] + pair_grad(
        emb_ref[at], key_ref[at], cols_ref[:both], cols_ref[both:, :both]
    )
    unit = unit_ref[at]
    inner = jnp.sum(grad * unit, axis=-1, keepdims=True)
    grad_x = (inv_ref[at, :1] * (grad - inner * unit)).astype(BF16)
    out_ref[...] = rows_dot(grad_x, proj_ref[...]).astype(BF16)


def choose_kernel(own_ref, given_ref, image_ref, text_ref, sems):
    _, _, core = place()

    def store(image_from, text_from):
        copies = [
            pltpu.make_async_copy(image_from, image_ref, sems.at[0]),
            pltpu.make_async_copy(text_from, text_ref, sems.at[1]),
        ]
        for copy in copies:
            copy.start()
        for copy in copies:
            copy.wait()

    @pl.when(core == 0)
    def _():
        store(own_ref, given_ref)

    @pl.when(core == 1)
    def _():
        store(given_ref, own_ref)


VMEM = pl.BlockSpec(memory_space=pltpu.VMEM)
SMEM = pl.BlockSpec(memory_space=pltpu.SMEM)
HBM = pl.BlockSpec(memory_space=pltpu.HBM)
ANY = pl.BlockSpec(memory_space=pl.ANY)


def call(kernel, in_specs, outs, out_spec=VMEM, scratch=(), aliases={}, vmem=24 * 2**20):
    where = pltpu.VMEM if out_spec is VMEM else jax.ShapeDtypeStruct
    shapes = tuple(where(shape, kind) for shape, kind in outs)
    return pl.pallas_call(
        kernel,
        out_shape=shapes,
        in_specs=in_specs,
        out_specs=tuple(out_spec for _ in shapes),
        scratch_shapes=scratch,
        input_output_aliases=aliases,
        compiler_params=pltpu.CompilerParams(vmem_limit_bytes=vmem),
        cost_estimate=pl.CostEstimate(flops=0, bytes_accessed=0, transcendentals=0),
    )


def body(image_feats, text_feats, image_proj, text_proj, logit_scale, logit_bias, match):
    rows, width = image_feats.shape
    both = 2 * rows
    blk_count = lax.axis_size("blk")
    pair_count = blk_count // 2

    def route(target):
        pairs = []
        for b in range(blk_count):
            for h in range(2):
                s, c, g = target(b // 2, b % 2, h)
                pairs.append((2 * b + h, 2 * (2 * (s % pair_count) + c) + g))
        return pairs

    def flip(x):
        return lax.ppermute(x, AXES, route(lambda s, c, h: (s, 1 - c, h)))

    def swap_or_next(x):
        return lax.ppermute(x, AXES, route(lambda s, c, h: (s - c, c, 1 - h)))

    def next_or_swap(x):
        return lax.ppermute(x, AXES, route(lambda s, c, h: (s + 1 - c, c, 1 - h)))

    def second_next(x, cross):
        return lax.ppermute(
            x, AXES, route(lambda s, c, h: (s + 2 - 4 * c, c, 1 - h if cross else h))
        )

    packet = ((both + KEY_ROWS, width), BF16)
    block_rows = ((rows, width), BF16)
    semaphores = pltpu.SemaphoreType.DMA
    def held(x):
        return pltpu.with_memory_space_constraint(x, pltpu.HBM)

    (raw,) = call(
        pack_kernel,
        [HBM] * 3,
        [packet],
        scratch=[pltpu.VMEM((1, rows), jnp.int32), semaphores((3,))],
    )(held(image_feats), held(text_feats), held(match.reshape(1, rows)))
    other = flip(raw)
    square = ((width, width), BF16)
    col_proj, row_proj = call(
        load_kernel, [ANY] + [HBM] * 2, [square] * 2, scratch=[semaphores((2,))]
    )(raw, held(image_proj), held(text_proj))
    sent, again, far = call(
        sent_kernel, [VMEM] * 3, [packet, packet, ((rows + KEY_ROWS, width), BF16)]
    )(raw, other, col_proj)

    def after(array, *others):
        return call(
            after_kernel, [ANY] * (1 + len(others)), [packet], ANY, aliases={0: 0}
        )(array, *others)[0]

    first = swap_or_next(sent)
    third = second_next(far, False)
    fourth = second_next(far, True)
    total = ((both, width), F32)
    emb, unit, inv, key, grad = call(
        own_kernel,
        [VMEM] * 4 + [SMEM] * 2,
        [((both, width), BF16), total, ((both, 128), F32), ((both, 128), F32), total],
    )(raw, other, sent, row_proj, logit_scale, logit_bias)
    second = next_or_swap(after(again, key))
    (grad,) = call(far_kernel, [VMEM] * 5, [total])(emb, key, third, fourth, grad)
    first = after(first, grad)
    fifth = next_or_swap(first)
    (grad,) = call(near_kernel, [VMEM] * 5, [total])(emb, key, first, second, grad)

    def back(start):
        return call(functools.partial(back_kernel, start), [VMEM] * 7, [block_rows])(
            emb, key, fifth, grad, unit, inv, row_proj
        )[0]

    given = flip(back(rows))
    own = back(0)
    return call(choose_kernel, [VMEM] * 2, [block_rows] * 2, HBM, [semaphores((2,))])(own, given)


def solution(mesh):
    return jax.shard_map(
        body,
        mesh=mesh,
        in_specs=(P(AXES, None), P(AXES, None), P(), P(), P(), P(), P(AXES)),
        out_specs=(P(AXES, None), P(AXES, None)),
        check_vma=False,
    )
```

time: 127 us -> 59.8 us (0.47)
  waiting for transfers between devices: 67 us -> 6.18 us
  starting transfers between devices: 25.9 us -> 41.6 us
  between operations: 15.7 us -> 2.1 us
  matrix products: 10.8 us -> 0 us
  Pallas kernels: 0 us -> 9.62 us
  blocking collectives: 5.76 us -> 0 us
  other arithmetic: 1.49 us -> 0 us
    ppermute x7, waiting for transfers between devices: 36.8 us -> 6.18 us  [the longest x2 6.17 us: next_or_swap(): return lax.ppermute(x, AXES, route(lambda s, c, h: (s + 1 - c, c, 1 - h)))]
    reduce_scatter x1 -> x0, waiting for transfers between devices: 30.1 us -> none  [body(): lax.psum_scatter(carried.astype(jnp.bfloat16), 'group', scatter_dimension...]
    ppermute x7, starting transfers between devices: 25.9 us -> 41.6 us  [the longest x2 21.6 us: flip(): return lax.ppermute(x, AXES, route(lambda s, c, h: (s, 1 - c, h)))]
    dot_general x16 -> x0, matrix products: 10.8 us -> none  [the longest x2 3.37 us: back_norm(): lax.dot_general(grad_x, proj, (((1,), (1,)), ((), ())), preferred_element...]
    pallas_call x0 -> x11, Pallas kernels: none -> 9.62 us  [the longest x2 2.32 us: back(): call(functools.partial(back_kernel, start), [VMEM] * 7, [block_rows])]
    all_gather x1 -> x0, blocking collectives: 5.76 us -> none  [body(): visiting = lax.all_gather(text_emb, 'group', axis=0, tiled=True)]
  transfers between devices with their start and end apart: 8 -> 7, of which waited for: 8 -> 2; matrix products, arithmetic and copies ran while one was open for 6% -> 0% of each run, Pallas kernels for 0% -> 10%
where the time goes in v2:
time: 59.8 us; the launch traced here: 59.5 us
  starting transfers between devices  41.6 us (70%)
  Pallas kernels  9.62 us (16%)
  waiting for transfers between devices  6.18 us (10%)
  between operations  2.1 us (4%)
    ppermute x2, starting transfers between devices, flip(): return lax.ppermute(x, AXES, route(lambda s, c, h: (s, 1 - c, h)))  21.6 us
    ppermute x1, starting transfers between devices, swap_or_next(): return lax.ppermute(x, AXES, route(lambda s, c, h: (s - c, c, 1 - h)))  10.4 us
    ppermute x2, waiting for transfers between devices, next_or_swap(): return lax.ppermute(x, AXES, route(lambda s, c, h: (s + 1 - c, c, 1 - h)))  6.17 us
    ppermute x2, starting transfers between devices, next_or_swap(): return lax.ppermute(x, AXES, route(lambda s, c, h: (s + 1 - c, c, 1 - h)))  5.27 us
    ppermute x2, starting transfers between devices, second_next(): lax.ppermute(x, AXES, route(lambda s, c, h: (s + 2 - 4 * c, c, 1 - h if c...  4.29 us
    pallas_call x2, Pallas kernels, back(): call(functools.partial(back_kernel, start), [VMEM] * 7, [block_rows])  2.32 us
    pallas_call x1, Pallas kernels, body(): call(load_kernel, [ANY] + [HBM] * 2, [square] * 2, scratch=[semaphores((2...  1.66 us
    pallas_call x1, Pallas kernels, body(): call(near_kernel, [VMEM] * 5, [total])(emb, key, first, second, grad)  1.33 us
  transfers between devices with their start and end apart: 7, of which 2 were waited for; matrix products, arithmetic and copies ran while one was open for 0% of the time, Pallas kernels for 10%

profile of v2, /device:TPU:1, one launch (start us, length us, event | category | flops | bytes accessed | tf_op | source)
XLA Modules:
  0.0 59.5 jit_solution(13347565560204056028)
XLA Ops:
  0.6 1.1 %shard_map.86.raw_ref = bf16[272,768]{1,0:T(8,128)(2,1)S(1)} custom-call(bf16[128,768]{1,0:T(8,128)(2,1)} %image_ref.1, bf16[128,768]{1,0:T(8,128)(2,1)} %text_ref.1, s32[1,128]{1,0:T(1,128)} %bitcast.1), custom_call_target="tpu_custom_call" | custom-call | tf_op jit(solution)/shard_map/pallas_call | solution.py:292
  1.7 16.1 %collective-permute-start = (bf16[272,768]{1,0:T(8,128)(2,1)S(1)}, bf16[272,768]{1,0:T(8,128)(2,1)S(1)}, u32[]{:S(2)}, u32[]{:S(2)}) collective-permute-start(bf16[272,768]{1,0:T(8,128)(2,1)S(1)} %shard_map.86.raw_ref), channel_id=1, source_target_pairs={{0,2},{1,3},{2,0},{3,1},{4,6},{5,7},{6,4},{7,5},{8,10},{9,11},{10,... | collective-permute-start | bytes 1253384 | tf_op jit(solution)/shard_map/ppermute | solution.py:273
  17.8 1.7 %shard_map.87 = (bf16[768,768]{1,0:T(8,128)(2,1)S(1)}, bf16[768,768]{1,0:T(8,128)(2,1)S(1)}) custom-call(bf16[272,768]{1,0:T(8,128)(2,1)S(1)} %shard_map.86.raw_ref, bf16[768,768]{1,0:T(8,128)(2,1)} %image_proj_ref.1, bf16[768,768]{1,0:T(8,128)(2,1)} %text_proj_ref.1), custom_call_target="tpu_custom_call" | custom-call | tf_op jit(solution)/shard_map/pallas_call | solution.py:300
  19.4 0.0 collective-permute-done.other_ref
  19.5 0.6 shard_map.88
  20.0 10.4 %collective-permute-start.1 = (bf16[272,768]{1,0:T(8,128)(2,1)S(1)}, bf16[272,768]{1,0:T(8,128)(2,1)S(1)}, u32[]{:S(2)}, u32[]{:S(2)}) collective-permute-start(bf16[272,768]{1,0:T(8,128)(2,1)S(1)} %get-tuple-element.13.sent_ref), channel_id=1, source_target_pairs={{0,1},{1,0},{2,1023},{3,1022},{4,5},{5,4},{6,3},{7,2},{8,9},{9,8},... | collective-permute-start | bytes 1253384 | tf_op jit(solution)/shard_map/ppermute | solution.py:276
  30.4 2.4 %collective-permute-start.2 = (bf16[144,768]{1,0:T(8,128)(2,1)S(1)}, bf16[144,768]{1,0:T(8,128)(2,1)S(1)}, u32[]{:S(2)}, u32[]{:S(2)}) collective-permute-start(bf16[144,768]{1,0:T(8,128)(2,1)S(1)} %get-tuple-element.17), channel_id=1, source_target_pairs={{0,8},{1,9},{2,1018},{3,1019},{4,12},{5,13},{6,1022},{7,1023},{8,1... | collective-permute-start | bytes 663560 | tf_op jit(solution)/shard_map/ppermute | solution.py:282
  32.8 1.9 %collective-permute-start.3 = (bf16[144,768]{1,0:T(8,128)(2,1)S(1)}, bf16[144,768]{1,0:T(8,128)(2,1)S(1)}, u32[]{:S(2)}, u32[]{:S(2)}) collective-permute-start(bf16[144,768]{1,0:T(8,128)(2,1)S(1)} %get-tuple-element.17), channel_id=1, source_target_pairs={{0,9},{1,8},{2,1019},{3,1018},{4,13},{5,12},{6,1023},{7,1022},{8,1... | collective-permute-start | bytes 663560 | tf_op jit(solution)/shard_map/ppermute | solution.py:282
  36.0 1.2 %shard_map.89 = (bf16[256,768]{1,0:T(8,128)(2,1)S(1)}, f32[256,768]{1,0:T(8,128)S(1)}, f32[256,128]{1,0:T(8,128)S(1)}, f32[256,128]{1,0:T(8,128)S(1)}, f32[256,768]{1,0:T(8,128)S(1)}) custom-call(bf16[272,768]{1,0:T(8,128)(2,1)S(1)} %shard_map.86.raw_ref, bf16[272,768]{1,0:T(8,128)(2,1)S(1)} %collective-permute-done.other_ref, ...), custom_call_target="tpu_custom_call" | custom-call | tf_op jit(solution)/shard_map/pallas_call | solution.py:316
  37.2 3.2 %collective-permute-start.5 = (bf16[272,768]{1,0:T(8,128)(2,1)S(1)}, bf16[272,768]{1,0:T(8,128)(2,1)S(1)}, u32[]{:S(2)}, u32[]{:S(2)}) collective-permute-start(bf16[272,768]{1,0:T(8,128)(2,1)S(1)} %shard_map.92), channel_id=1, source_target_pairs={{0,5},{1,4},{2,3},{3,2},{4,9},{5,8},{6,7},{7,6},{8,13},{9,12},{10,... | collective-permute-start | bytes 1253384 | tf_op jit(solution)/shard_map/ppermute | solution.py:279
  40.5 0.0 collective-permute-done.2.third_ref
  40.5 0.0 collective-permute-done.3.fourth_ref
  40.5 0.7 %shard_map.90.refs_1_.grad_ref = f32[256,768]{1,0:T(8,128)S(1)} custom-call(bf16[256,768]{1,0:T(8,128)(2,1)S(1)} %get-tuple-element.15.emb_ref, f32[256,128]{1,0:T(8,128)S(1)} %get-tuple-element.16.key_ref.refs_1_, bf16[144,768]{1,0:T(8,128)(2,1)S(1)} %collective-permute-done.2.third_ref, bf16[144,768]{1,0:T(8,128)(2,1)S(1)} %collective-permute-done.3.fourth_ref, ...), custom_call_target="tpu_custom_call" | custom-call | tf_op jit(solution)/shard_map/pallas_call | solution.py:322
  41.2 0.0 collective-permute-done.1.refs_0_
  41.2 2.0 %collective-permute-start.4 = (bf16[272,768]{1,0:T(8,128)(2,1)S(1)}, bf16[272,768]{1,0:T(8,128)(2,1)S(1)}, u32[]{:S(2)}, u32[]{:S(2)}) collective-permute-start(bf16[272,768]{1,0:T(8,128)(2,1)S(1)} %shard_map.91.first_ref), channel_id=1, source_target_pairs={{0,5},{1,4},{2,3},{3,2},{4,9},{5,8},{6,7},{7,6},{8,13},{9,12},{10,... | collective-permute-start | bytes 1253384 | tf_op jit(solution)/shard_map/ppermute | solution.py:279
  43.3 2.7 %collective-permute-done.5.second_ref = bf16[272,768]{1,0:T(8,128)(2,1)S(1)} collective-permute-done((bf16[272,768]{1,0:T(8,128)(2,1)S(1)}, bf16[272,768]{1,0:T(8,128)(2,1)S(1)}, u32[]{:S(2)}, u32[]{:S(2)}) %collective-permute-start.5) | collective-permute-done | bytes 417824 | tf_op jit(solution)/shard_map/ppermute | solution.py:279
  46.0 1.3 %shard_map.93.grad_ref = f32[256,768]{1,0:T(8,128)S(1)} custom-call(bf16[256,768]{1,0:T(8,128)(2,1)S(1)} %get-tuple-element.15.emb_ref, f32[256,128]{1,0:T(8,128)S(1)} %get-tuple-element.16.key_ref.refs_1_, bf16[272,768]{1,0:T(8,128)(2,1)S(1)} %shard_map.91.first_ref, bf16[272,768]{1,0:T(8,128)(2,1)S(1)} %collective-permute-done.5.second_ref, ...), custom_call_target="tpu_custom_call" | custom-call | tf_op jit(solution)/shard_map/pallas_call | solution.py:325
  47.4 3.4 %collective-permute-done.4.cols_ref = bf16[272,768]{1,0:T(8,128)(2,1)S(1)} collective-permute-done((bf16[272,768]{1,0:T(8,128)(2,1)S(1)}, bf16[272,768]{1,0:T(8,128)(2,1)S(1)}, u32[]{:S(2)}, u32[]{:S(2)}) %collective-permute-start.4) | collective-permute-done | bytes 417824 | tf_op jit(solution)/shard_map/ppermute | solution.py:279
  50.8 1.2 %shard_map.95 = bf16[128,768]{1,0:T(8,128)(2,1)S(1)} custom-call(bf16[256,768]{1,0:T(8,128)(2,1)S(1)} %get-tuple-element.15.emb_ref, f32[256,128]{1,0:T(8,128)S(1)} %get-tuple-element.16.key_ref.refs_1_, bf16[272,768]{1,0:T(8,128)(2,1)S(1)} %collective-permute-done.4.cols_ref, f32[256,768]{1,0:T(8,128)S(1)} %shard_map.93.grad_ref, ...), custom_call_target="tpu_custom_call" | custom-call | tf_op jit(solution)/shard_map/pallas_call | solution.py:328
  52.0 5.5 %collective-permute-start.6 = (bf16[128,768]{1,0:T(8,128)(2,1)S(1)}, bf16[128,768]{1,0:T(8,128)(2,1)S(1)}, u32[]{:S(2)}, u32[]{:S(2)}) collective-permute-start(bf16[128,768]{1,0:T(8,128)(2,1)S(1)} %shard_map.95), channel_id=1, source_target_pairs={{0,2},{1,3},{2,0},{3,1},{4,6},{5,7},{6,4},{7,5},{8,10},{9,11},{10,... | collective-permute-start | bytes 589832 | tf_op jit(solution)/shard_map/ppermute | solution.py:273
  57.5 1.2 %shard_map.94.own_ref = bf16[128,768]{1,0:T(8,128)(2,1)S(1)} custom-call(bf16[256,768]{1,0:T(8,128)(2,1)S(1)} %get-tuple-element.15.emb_ref, f32[256,128]{1,0:T(8,128)S(1)} %get-tuple-element.16.key_ref.refs_1_, bf16[272,768]{1,0:T(8,128)(2,1)S(1)} %collective-permute-done.4.cols_ref, f32[256,768]{1,0:T(8,128)S(1)} %shard_map.93.grad_ref, ...), custom_call_target="tpu_custom_call" | custom-call | tf_op jit(solution)/shard_map/pallas_call | solution.py:328
  58.7 0.0 collective-permute-done.6.given_ref
  58.7 0.8 %shard_map.96 = (bf16[128,768]{1,0:T(8,128)(2,1)}, bf16[128,768]{1,0:T(8,128)(2,1)}) custom-call(bf16[128,768]{1,0:T(8,128)(2,1)S(1)} %shard_map.94.own_ref, bf16[128,768]{1,0:T(8,128)(2,1)S(1)} %collective-permute-done.6.given_ref), custom_call_target="tpu_custom_call" | custom-call | tf_op jit(solution)/shard_map/pallas_call | solution.py:334
  (2 shorter events, 0.0 us)
Async XLA Ops:
  1.7 17.7 %collective-permute-start = (bf16[272,768]{1,0:T(8,128)(2,1)S(1)}, bf16[272,768]{1,0:T(8,128)(2,1)S(1)}, u32[]{:S(2)}, u32[]{:S(2)}) collective-permute-start(bf16[272,768]{1,0:T(8,128)(2,1)S(1)} %shard_map.86.raw_ref), channel_id=1, source_target_pairs={{0,2},{1,3},{2,0},{3,1},{4,6},{5,7},{6,4},{7,5},{8,10},{9,11},{10,... | collective-permute-start | bytes 1253384 | tf_op jit(solution)/shard_map/ppermute | solution.py:273
  20.0 21.2 %collective-permute-start.1 = (bf16[272,768]{1,0:T(8,128)(2,1)S(1)}, bf16[272,768]{1,0:T(8,128)(2,1)S(1)}, u32[]{:S(2)}, u32[]{:S(2)}) collective-permute-start(bf16[272,768]{1,0:T(8,128)(2,1)S(1)} %get-tuple-element.13.sent_ref), channel_id=1, source_target_pairs={{0,1},{1,0},{2,1023},{3,1022},{4,5},{5,4},{6,3},{7,2},{8,9},{9,8},... | collective-permute-start | bytes 1253384 | tf_op jit(solution)/shard_map/ppermute | solution.py:276
  30.4 10.1 %collective-permute-start.2 = (bf16[144,768]{1,0:T(8,128)(2,1)S(1)}, bf16[144,768]{1,0:T(8,128)(2,1)S(1)}, u32[]{:S(2)}, u32[]{:S(2)}) collective-permute-start(bf16[144,768]{1,0:T(8,128)(2,1)S(1)} %get-tuple-element.17), channel_id=1, source_target_pairs={{0,8},{1,9},{2,1018},{3,1019},{4,12},{5,13},{6,1022},{7,1023},{8,1... | collective-permute-start | bytes 663560 | tf_op jit(solution)/shard_map/ppermute | solution.py:282
  32.8 7.7 %collective-permute-start.3 = (bf16[144,768]{1,0:T(8,128)(2,1)S(1)}, bf16[144,768]{1,0:T(8,128)(2,1)S(1)}, u32[]{:S(2)}, u32[]{:S(2)}) collective-permute-start(bf16[144,768]{1,0:T(8,128)(2,1)S(1)} %get-tuple-element.17), channel_id=1, source_target_pairs={{0,9},{1,8},{2,1019},{3,1018},{4,13},{5,12},{6,1023},{7,1022},{8,1... | collective-permute-start | bytes 663560 | tf_op jit(solution)/shard_map/ppermute | solution.py:282
  37.2 8.8 %collective-permute-start.5 = (bf16[272,768]{1,0:T(8,128)(2,1)S(1)}, bf16[272,768]{1,0:T(8,128)(2,1)S(1)}, u32[]{:S(2)}, u32[]{:S(2)}) collective-permute-start(bf16[272,768]{1,0:T(8,128)(2,1)S(1)} %shard_map.92), channel_id=1, source_target_pairs={{0,5},{1,4},{2,3},{3,2},{4,9},{5,8},{6,7},{7,6},{8,13},{9,12},{10,... | collective-permute-start | bytes 1253384 | tf_op jit(solution)/shard_map/ppermute | solution.py:279
  41.2 9.5 %collective-permute-start.4 = (bf16[272,768]{1,0:T(8,128)(2,1)S(1)}, bf16[272,768]{1,0:T(8,128)(2,1)S(1)}, u32[]{:S(2)}, u32[]{:S(2)}) collective-permute-start(bf16[272,768]{1,0:T(8,128)(2,1)S(1)} %shard_map.91.first_ref), channel_id=1, source_target_pairs={{0,5},{1,4},{2,3},{3,2},{4,9},{5,8},{6,7},{7,6},{8,13},{9,12},{10,... | collective-permute-start | bytes 1253384 | tf_op jit(solution)/shard_map/ppermute | solution.py:279
  52.0 6.7 %collective-permute-start.6 = (bf16[128,768]{1,0:T(8,128)(2,1)S(1)}, bf16[128,768]{1,0:T(8,128)(2,1)S(1)}, u32[]{:S(2)}, u32[]{:S(2)}) collective-permute-start(bf16[128,768]{1,0:T(8,128)(2,1)S(1)} %shard_map.95), channel_id=1, source_target_pairs={{0,2},{1,3},{2,0},{3,1},{4,6},{5,7},{6,4},{7,5},{8,10},{9,11},{10,... | collective-permute-start | bytes 589832 | tf_op jit(solution)/shard_map/ppermute | solution.py:273

commit v3 on v2

--- a/solution.py
+++ b/solution.py
@@ -94,7 +94,7 @@
     return x * inv, inv
 
 
-def sent_kernel(raw_ref, other_ref, proj_ref, sent_ref, again_ref, far_ref):
+def sent_kernel(raw_ref, other_ref, proj_ref, sent_ref, again_ref):
     rows = (raw_ref.shape[0] - KEY_ROWS) // 2
     both = 2 * rows
     width = raw_ref.shape[1]
@@ -108,7 +108,6 @@
         )
     sent_ref[both:, both:] = jnp.zeros((KEY_ROWS, width - both), BF16)
     again_ref[...] = sent_ref[...]
-    far_ref[...] = sent_ref[rows:]
 
 
 def pair_grad(row_emb, row_key, col_emb, col_tile):
@@ -170,16 +169,26 @@
     pass
 
 
-def far_kernel(emb_ref, key_ref, third_ref, fourth_ref, grad_ref, out_ref):
-    both = emb_ref.shape[0]
+def far_pack_kernel(sent_ref, first_ref, second_ref, far_ref):
+    both = sent_ref.shape[0] - KEY_ROWS
     rows = both // 2
-    total = grad_ref[:rows]
-    for far_ref in (third_ref, fourth_ref):
-        total += pair_grad(
-            emb_ref[:rows], key_ref[:rows], far_ref[:rows], far_ref[rows:, rows:both]
-        )
-    out_ref[:rows] = total
-    out_ref[rows:] = grad_ref[rows:]
+    _, _, core = place()
+
+    def pack(swapped_ref):
+        for n, ref in enumerate((sent_ref, swapped_ref)):
+            at = slice(n * rows, (n + 1) * rows)
+            far_ref[at] = ref[rows:both]
+            far_ref[both:, at] = ref[both:, rows:both]
+
+    @pl.when(core == 0)
+    def _():
+        pack(first_ref)
+
+    @pl.when(core == 1)
+    def _():
+        pack(second_ref)
+
+    far_ref[both:, both:] = sent_ref[both:, both:]
 
 
 def near_kernel(emb_ref, key_ref, first_ref, second_ref, grad_ref, out_ref):
@@ -199,13 +208,14 @@
         pairs(second_ref, first_ref)
 
 
-def back_kernel(start, emb_ref, key_ref, cols_ref, grad_ref, unit_ref, inv_ref, proj_ref, out_ref):
+def back_kernel(part, emb_ref, key_ref, *refs):
+    *cols_refs, grad_ref, unit_ref, inv_ref, proj_ref, out_ref = refs
     rows = out_ref.shape[0]
     both = 2 * rows
-    at = slice(start, start + rows)
-    grad = grad_ref[at] + pair_grad(
-        emb_ref[at], key_ref[at], cols_ref[:both], cols_ref[both:, :both]
-    )
+    at = slice(part * rows, (part + 1) * rows)
+    grad = grad_ref[at]
+    for ref in cols_refs:
+        grad += pair_grad(emb_ref[at], key_ref[at], ref[:both], ref[both:, :both])
     unit = unit_ref[at]
     inner = jnp.sum(grad * unit, axis=-1, keepdims=True)
     grad_x = (inv_ref[at, :1] * (grad - inner * unit)).astype(BF16)
@@ -278,10 +288,8 @@
     def next_or_swap(x):
         return lax.ppermute(x, AXES, route(lambda s, c, h: (s + 1 - c, c, 1 - h)))
 
-    def second_next(x, cross):
-        return lax.ppermute(
-            x, AXES, route(lambda s, c, h: (s + 2 - 4 * c, c, 1 - h if cross else h))
-        )
+    def second_next(x):
+        return lax.ppermute(x, AXES, route(lambda s, c, h: (s + 2 - 4 * c, c, h)))
 
     packet = ((both + KEY_ROWS, width), BF16)
     block_rows = ((rows, width), BF16)
@@ -300,9 +308,7 @@
     col_proj, row_proj = call(
         load_kernel, [ANY] + [HBM] * 2, [square] * 2, scratch=[semaphores((2,))]
     )(raw, held(image_proj), held(text_proj))
-    sent, again, far = call(
-        sent_kernel, [VMEM] * 3, [packet, packet, ((rows + KEY_ROWS, width), BF16)]
-    )(raw, other, col_proj)
+    sent, again = call(sent_kernel, [VMEM] * 3, [packet] * 2)(raw, other, col_proj)
 
     def after(array, *others):
         return call(
@@ -310,8 +316,6 @@
         )(array, *others)[0]
 
     first = swap_or_next(sent)
-    third = second_next(far, False)
-    fourth = second_next(far, True)
     total = ((both, width), F32)
     emb, unit, inv, key, grad = call(
         own_kernel,
@@ -319,19 +323,21 @@
         [((both, width), BF16), total, ((both, 128), F32), ((both, 128), F32), total],
     )(raw, other, sent, row_proj, logit_scale, logit_bias)
     second = next_or_swap(after(again, key))
-    (grad,) = call(far_kernel, [VMEM] * 5, [total])(emb, key, third, fourth, grad)
-    first = after(first, grad)
+    first = after(first, key)
     fifth = next_or_swap(first)
+    (far,) = call(far_pack_kernel, [VMEM] * 3, [packet])(sent, first, second)
+    far = second_next(far)
     (grad,) = call(near_kernel, [VMEM] * 5, [total])(emb, key, first, second, grad)
-
-    def back(start):
-        return call(functools.partial(back_kernel, start), [VMEM] * 7, [block_rows])(
-            emb, key, fifth, grad, unit, inv, row_proj
-        )[0]
-
-    given = flip(back(rows))
-    own = back(0)
-    return call(choose_kernel, [VMEM] * 2, [block_rows] * 2, HBM, [semaphores((2,))])(own, given)
+    (other_out,) = call(functools.partial(back_kernel, 1), [VMEM] * 7, [block_rows])(
+        emb, key, fifth, grad, unit, inv, row_proj
+    )
+    given = flip(other_out)
+    (own_out,) = call(functools.partial(back_kernel, 0), [VMEM] * 8, [block_rows])(
+        emb, key, fifth, far, grad, unit, inv, row_proj
+    )
+    return call(choose_kernel, [VMEM] * 2, [block_rows] * 2, HBM, [semaphores((2,))])(
+        own_out, given
+    )
 
 
 def solution(mesh):

time: 59.8 us -> 55.6 us (0.930)
  the two profiles are of different devices: /device:TPU:1 before, /device:TPU:2 now
where the time goes in v3:
time: 55.6 us; the launch traced here: 55.3 us
  starting transfers between devices  24.8 us (45%)
  waiting for transfers between devices  19.1 us (34%)
  Pallas kernels  9.36 us (17%)
  between operations  2.05 us (4%)
    ppermute x1, starting transfers between devices, swap_or_next(): return lax.ppermute(x, AXES, route(lambda s, c, h: (s - c, c, 1 - h)))  15.1 us
    ppermute x2, waiting for transfers between devices, next_or_swap(): return lax.ppermute(x, AXES, route(lambda s, c, h: (s + 1 - c, c, 1 - h)))  11.9 us
    ppermute x1, waiting for transfers between devices, second_next(): return lax.ppermute(x, AXES, route(lambda s, c, h: (s + 2 - 4 * c, c, h)))  5.53 us
    ppermute x2, starting transfers between devices, flip(): return lax.ppermute(x, AXES, route(lambda s, c, h: (s, 1 - c, h)))  3.93 us
    ppermute x2, starting transfers between devices, next_or_swap(): return lax.ppermute(x, AXES, route(lambda s, c, h: (s + 1 - c, c, 1 - h)))  3.83 us
    ppermute x1, starting transfers between devices, second_next(): return lax.ppermute(x, AXES, route(lambda s, c, h: (s + 2 - 4 * c, c, h)))  1.92 us
    pallas_call x1, Pallas kernels, body(): call(load_kernel, [ANY] + [HBM] * 2, [square] * 2, scratch=[semaphores((2...  1.66 us
    pallas_call x1, Pallas kernels, body(): call(functools.partial(back_kernel, 0), [VMEM] * 8, [block_rows])  1.6 us
  transfers between devices with their start and end apart: 6, of which 5 were waited for; matrix products, arithmetic and copies ran while one was open for 0% of the time, Pallas kernels for 13%

profile of v3, /device:TPU:2, one launch (start us, length us, event | category | flops | bytes accessed | tf_op | source)
XLA Modules:
  0.0 55.3 jit_solution(5554165120131216101)
XLA Ops:
  0.6 1.1 %shard_map.86.raw_ref = bf16[272,768]{1,0:T(8,128)(2,1)S(1)} custom-call(bf16[128,768]{1,0:T(8,128)(2,1)} %image_ref.1, bf16[128,768]{1,0:T(8,128)(2,1)} %text_ref.1, s32[1,128]{1,0:T(1,128)} %bitcast.1), custom_call_target="tpu_custom_call" | custom-call | tf_op jit(solution)/shard_map/pallas_call | solution.py:300
  1.7 1.9 %collective-permute-start = (bf16[272,768]{1,0:T(8,128)(2,1)S(1)}, bf16[272,768]{1,0:T(8,128)(2,1)S(1)}, u32[]{:S(2)}, u32[]{:S(2)}) collective-permute-start(bf16[272,768]{1,0:T(8,128)(2,1)S(1)} %shard_map.86.raw_ref), channel_id=1, source_target_pairs={{0,2},{1,3},{2,0},{3,1},{4,6},{5,7},{6,4},{7,5},{8,10},{9,11},{10,... | collective-permute-start | bytes 1253384 | tf_op jit(solution)/shard_map/ppermute | solution.py:283
  3.6 1.7 %shard_map.87 = (bf16[768,768]{1,0:T(8,128)(2,1)S(1)}, bf16[768,768]{1,0:T(8,128)(2,1)S(1)}) custom-call(bf16[272,768]{1,0:T(8,128)(2,1)S(1)} %shard_map.86.raw_ref, bf16[768,768]{1,0:T(8,128)(2,1)} %image_proj_ref.1, bf16[768,768]{1,0:T(8,128)(2,1)} %text_proj_ref.1), custom_call_target="tpu_custom_call" | custom-call | tf_op jit(solution)/shard_map/pallas_call | solution.py:308
  5.3 0.1 collective-permute-done.other_ref
  5.4 0.6 %shard_map.88 = (bf16[272,768]{1,0:T(8,128)(2,1)S(1)}, bf16[272,768]{1,0:T(8,128)(2,1)S(1)}) custom-call(bf16[272,768]{1,0:T(8,128)(2,1)S(1)} %shard_map.86.raw_ref, bf16[272,768]{1,0:T(8,128)(2,1)S(1)} %collective-permute-done.other_ref, bf16[768,768]{1,0:T(8,128)(2,1)S(1)} %get-tuple-element.11.proj_ref), custom_call_target="tpu_custom_call" | custom-call | tf_op jit(solution)/shard_map/pallas_call | solution.py:311
  5.9 15.1 %collective-permute-start.1 = (bf16[272,768]{1,0:T(8,128)(2,1)S(1)}, bf16[272,768]{1,0:T(8,128)(2,1)S(1)}, u32[]{:S(2)}, u32[]{:S(2)}) collective-permute-start(bf16[272,768]{1,0:T(8,128)(2,1)S(1)} %get-tuple-element.12.sent_ref), channel_id=1, source_target_pairs={{0,1},{1,0},{2,1023},{3,1022},{4,5},{5,4},{6,3},{7,2},{8,9},{9,8},... | collective-permute-start | bytes 1253384 | tf_op jit(solution)/shard_map/ppermute | solution.py:286
  22.3 1.2 %shard_map.89 = (bf16[256,768]{1,0:T(8,128)(2,1)S(1)}, f32[256,768]{1,0:T(8,128)S(1)}, f32[256,128]{1,0:T(8,128)S(1)}, f32[256,128]{1,0:T(8,128)S(1)}, f32[256,768]{1,0:T(8,128)S(1)}) custom-call(bf16[272,768]{1,0:T(8,128)(2,1)S(1)} %shard_map.86.raw_ref, bf16[272,768]{1,0:T(8,128)(2,1)S(1)} %collective-permute-done.other_ref, ...), custom_call_target="tpu_custom_call" | custom-call | tf_op jit(solution)/shard_map/pallas_call | solution.py:320
  23.5 1.9 %collective-permute-start.3 = (bf16[272,768]{1,0:T(8,128)(2,1)S(1)}, bf16[272,768]{1,0:T(8,128)(2,1)S(1)}, u32[]{:S(2)}, u32[]{:S(2)}) collective-permute-start(bf16[272,768]{1,0:T(8,128)(2,1)S(1)} %shard_map.91), channel_id=1, source_target_pairs={{0,5},{1,4},{2,3},{3,2},{4,9},{5,8},{6,7},{7,6},{8,13},{9,12},{10,... | collective-permute-start | bytes 1253384 | tf_op jit(solution)/shard_map/ppermute | solution.py:289
  25.5 1.6 %collective-permute-done.1.refs_0_ = bf16[272,768]{1,0:T(8,128)(2,1)S(1)} collective-permute-done((bf16[272,768]{1,0:T(8,128)(2,1)S(1)}, bf16[272,768]{1,0:T(8,128)(2,1)S(1)}, u32[]{:S(2)}, u32[]{:S(2)}) %collective-permute-start.1) | collective-permute-done | bytes 417824 | tf_op jit(solution)/shard_map/ppermute | solution.py:286
  27.0 1.9 %collective-permute-start.2 = (bf16[272,768]{1,0:T(8,128)(2,1)S(1)}, bf16[272,768]{1,0:T(8,128)(2,1)S(1)}, u32[]{:S(2)}, u32[]{:S(2)}) collective-permute-start(bf16[272,768]{1,0:T(8,128)(2,1)S(1)} %shard_map.90.first_ref), channel_id=1, source_target_pairs={{0,5},{1,4},{2,3},{3,2},{4,9},{5,8},{6,7},{7,6},{8,13},{9,12},{10,... | collective-permute-start | bytes 1253384 | tf_op jit(solution)/shard_map/ppermute | solution.py:289
  29.0 10.6 %collective-permute-done.3.second_ref = bf16[272,768]{1,0:T(8,128)(2,1)S(1)} collective-permute-done((bf16[272,768]{1,0:T(8,128)(2,1)S(1)}, bf16[272,768]{1,0:T(8,128)(2,1)S(1)}, u32[]{:S(2)}, u32[]{:S(2)}) %collective-permute-start.3) | collective-permute-done | bytes 417824 | tf_op jit(solution)/shard_map/ppermute | solution.py:289
  39.6 1.9 %collective-permute-start.4 = (bf16[272,768]{1,0:T(8,128)(2,1)S(1)}, bf16[272,768]{1,0:T(8,128)(2,1)S(1)}, u32[]{:S(2)}, u32[]{:S(2)}) collective-permute-start(bf16[272,768]{1,0:T(8,128)(2,1)S(1)} %shard_map.92), channel_id=1, source_target_pairs={{0,8},{1,9},{2,1018},{3,1019},{4,12},{5,13},{6,1022},{7,1023},{8,1... | collective-permute-start | bytes 1253384 | tf_op jit(solution)/shard_map/ppermute | solution.py:292
  41.6 1.3 %shard_map.93.refs_2_.refs_1_ = f32[256,768]{1,0:T(8,128)S(1)} custom-call(bf16[256,768]{1,0:T(8,128)(2,1)S(1)} %get-tuple-element.14.emb_ref, f32[256,128]{1,0:T(8,128)S(1)} %get-tuple-element.15.refs_1_.key_ref, bf16[272,768]{1,0:T(8,128)(2,1)S(1)} %shard_map.90.first_ref, bf16[272,768]{1,0:T(8,128)(2,1)S(1)} %collective-permute-done.3.second_ref, ...), custom_call_target="tpu_custom_call" | custom-call | tf_op jit(solution)/shard_map/pallas_call | solution.py:330
  42.9 1.3 %collective-permute-done.2.refs_0_ = bf16[272,768]{1,0:T(8,128)(2,1)S(1)} collective-permute-done((bf16[272,768]{1,0:T(8,128)(2,1)S(1)}, bf16[272,768]{1,0:T(8,128)(2,1)S(1)}, u32[]{:S(2)}, u32[]{:S(2)}) %collective-permute-start.2) | collective-permute-done | bytes 417824 | tf_op jit(solution)/shard_map/ppermute | solution.py:289
  44.2 1.2 %shard_map.95 = bf16[128,768]{1,0:T(8,128)(2,1)S(1)} custom-call(bf16[256,768]{1,0:T(8,128)(2,1)S(1)} %get-tuple-element.14.emb_ref, f32[256,128]{1,0:T(8,128)S(1)} %get-tuple-element.15.refs_1_.key_ref, bf16[272,768]{1,0:T(8,128)(2,1)S(1)} %collective-permute-done.2.refs_0_, f32[256,768]{1,0:T(8,128)S(1)} %shard_map.93.refs_2_.refs_1_, ...), custom_call_target="tpu_custom_call" | custom-call | tf_op jit(solution)/shard_map/pallas_call | solution.py:331
  45.4 2.0 %collective-permute-start.5 = (bf16[128,768]{1,0:T(8,128)(2,1)S(1)}, bf16[128,768]{1,0:T(8,128)(2,1)S(1)}, u32[]{:S(2)}, u32[]{:S(2)}) collective-permute-start(bf16[128,768]{1,0:T(8,128)(2,1)S(1)} %shard_map.95), channel_id=1, source_target_pairs={{0,2},{1,3},{2,0},{3,1},{4,6},{5,7},{6,4},{7,5},{8,10},{9,11},{10,... | collective-permute-start | bytes 589832 | tf_op jit(solution)/shard_map/ppermute | solution.py:283
  47.4 5.5 %collective-permute-done.4.refs_1_ = bf16[272,768]{1,0:T(8,128)(2,1)S(1)} collective-permute-done((bf16[272,768]{1,0:T(8,128)(2,1)S(1)}, bf16[272,768]{1,0:T(8,128)(2,1)S(1)}, u32[]{:S(2)}, u32[]{:S(2)}) %collective-permute-start.4) | collective-permute-done | bytes 417824 | tf_op jit(solution)/shard_map/ppermute | solution.py:292
  52.9 1.6 %shard_map.94.own_ref = bf16[128,768]{1,0:T(8,128)(2,1)S(1)} custom-call(bf16[256,768]{1,0:T(8,128)(2,1)S(1)} %get-tuple-element.14.emb_ref, f32[256,128]{1,0:T(8,128)S(1)} %get-tuple-element.15.refs_1_.key_ref, bf16[272,768]{1,0:T(8,128)(2,1)S(1)} %collective-permute-done.2.refs_0_, bf16[272,768]{1,0:T(8,128)(2,1)S(1)} %collective-permute-done.4.refs_1_, ...), custom_call_target="tpu_custom_call" | custom-call | tf_op jit(solution)/shard_map/pallas_call | solution.py:335
  54.5 0.0 collective-permute-done.5.given_ref
  54.5 0.8 %shard_map.96 = (bf16[128,768]{1,0:T(8,128)(2,1)}, bf16[128,768]{1,0:T(8,128)(2,1)}) custom-call(bf16[128,768]{1,0:T(8,128)(2,1)S(1)} %shard_map.94.own_ref, bf16[128,768]{1,0:T(8,128)(2,1)S(1)} %collective-permute-done.5.given_ref), custom_call_target="tpu_custom_call" | custom-call | tf_op jit(solution)/shard_map/pallas_call | solution.py:338
  (3 shorter events, 0.0 us)
Async XLA Ops:
  1.7 3.7 %collective-permute-start = (bf16[272,768]{1,0:T(8,128)(2,1)S(1)}, bf16[272,768]{1,0:T(8,128)(2,1)S(1)}, u32[]{:S(2)}, u32[]{:S(2)}) collective-permute-start(bf16[272,768]{1,0:T(8,128)(2,1)S(1)} %shard_map.86.raw_ref), channel_id=1, source_target_pairs={{0,2},{1,3},{2,0},{3,1},{4,6},{5,7},{6,4},{7,5},{8,10},{9,11},{10,... | collective-permute-start | bytes 1253384 | tf_op jit(solution)/shard_map/ppermute | solution.py:283
  5.9 21.1 %collective-permute-start.1 = (bf16[272,768]{1,0:T(8,128)(2,1)S(1)}, bf16[272,768]{1,0:T(8,128)(2,1)S(1)}, u32[]{:S(2)}, u32[]{:S(2)}) collective-permute-start(bf16[272,768]{1,0:T(8,128)(2,1)S(1)} %get-tuple-element.12.sent_ref), channel_id=1, source_target_pairs={{0,1},{1,0},{2,1023},{3,1022},{4,5},{5,4},{6,3},{7,2},{8,9},{9,8},... | collective-permute-start | bytes 1253384 | tf_op jit(solution)/shard_map/ppermute | solution.py:286
  23.5 16.1 %collective-permute-start.3 = (bf16[272,768]{1,0:T(8,128)(2,1)S(1)}, bf16[272,768]{1,0:T(8,128)(2,1)S(1)}, u32[]{:S(2)}, u32[]{:S(2)}) collective-permute-start(bf16[272,768]{1,0:T(8,128)(2,1)S(1)} %shard_map.91), channel_id=1, source_target_pairs={{0,5},{1,4},{2,3},{3,2},{4,9},{5,8},{6,7},{7,6},{8,13},{9,12},{10,... | collective-permute-start | bytes 1253384 | tf_op jit(solution)/shard_map/ppermute | solution.py:289
  27.0 17.1 %collective-permute-start.2 = (bf16[272,768]{1,0:T(8,128)(2,1)S(1)}, bf16[272,768]{1,0:T(8,128)(2,1)S(1)}, u32[]{:S(2)}, u32[]{:S(2)}) collective-permute-start(bf16[272,768]{1,0:T(8,128)(2,1)S(1)} %shard_map.90.first_ref), channel_id=1, source_target_pairs={{0,5},{1,4},{2,3},{3,2},{4,9},{5,8},{6,7},{7,6},{8,13},{9,12},{10,... | collective-permute-start | bytes 1253384 | tf_op jit(solution)/shard_map/ppermute | solution.py:289
  39.6 13.3 %collective-permute-start.4 = (bf16[272,768]{1,0:T(8,128)(2,1)S(1)}, bf16[272,768]{1,0:T(8,128)(2,1)S(1)}, u32[]{:S(2)}, u32[]{:S(2)}) collective-permute-start(bf16[272,768]{1,0:T(8,128)(2,1)S(1)} %shard_map.92), channel_id=1, source_target_pairs={{0,8},{1,9},{2,1018},{3,1019},{4,12},{5,13},{6,1022},{7,1023},{8,1... | collective-permute-start | bytes 1253384 | tf_op jit(solution)/shard_map/ppermute | solution.py:292
  45.4 9.2 %collective-permute-start.5 = (bf16[128,768]{1,0:T(8,128)(2,1)S(1)}, bf16[128,768]{1,0:T(8,128)(2,1)S(1)}, u32[]{:S(2)}, u32[]{:S(2)}) collective-permute-start(bf16[128,768]{1,0:T(8,128)(2,1)S(1)} %shard_map.95), channel_id=1, source_target_pairs={{0,2},{1,3},{2,0},{3,1},{4,6},{5,7},{6,4},{7,5},{8,10},{9,11},{10,... | collective-permute-start | bytes 589832 | tf_op jit(solution)/shard_map/ppermute | solution.py:283

commit v4 on v3

--- a/solution.py
+++ b/solution.py
@@ -94,7 +94,7 @@
     return x * inv, inv
 
 
-def sent_kernel(raw_ref, other_ref, proj_ref, sent_ref, again_ref):
+def sent_kernel(raw_ref, other_ref, proj_ref, sent_ref, last_ref):
     rows = (raw_ref.shape[0] - KEY_ROWS) // 2
     both = 2 * rows
     width = raw_ref.shape[1]
@@ -107,7 +107,7 @@
             core == 0, text_key_tile(block ^ n, half, rows), ref[both:, :rows]
         )
     sent_ref[both:, both:] = jnp.zeros((KEY_ROWS, width - both), BF16)
-    again_ref[...] = sent_ref[...]
+    last_ref[...] = sent_ref[rows:]
 
 
 def pair_grad(row_emb, row_key, col_emb, col_tile):
@@ -169,43 +169,9 @@
     pass
 
 
-def far_pack_kernel(sent_ref, first_ref, second_ref, far_ref):
-    both = sent_ref.shape[0] - KEY_ROWS
-    rows = both // 2
-    _, _, core = place()
-
-    def pack(swapped_ref):
-        for n, ref in enumerate((sent_ref, swapped_ref)):
-            at = slice(n * rows, (n + 1) * rows)
-            far_ref[at] = ref[rows:both]
-            far_ref[both:, at] = ref[both:, rows:both]
-
-    @pl.when(core == 0)
-    def _():
-        pack(first_ref)
-
-    @pl.when(core == 1)
-    def _():
-        pack(second_ref)
-
-    far_ref[both:, both:] = sent_ref[both:, both:]
-
-
-def near_kernel(emb_ref, key_ref, first_ref, second_ref, grad_ref, out_ref):
-    _, _, core = place()
-    out_ref[...] = grad_ref[...]
-
-    def pairs(swapped_ref, near_ref):
-        own_pairs(emb_ref, key_ref, swapped_ref, out_ref, True)
-        out_ref[...] += all_pairs(emb_ref, key_ref, near_ref)
-
-    @pl.when(core == 0)
-    def _():
-        pairs(first_ref, second_ref)
-
-    @pl.when(core == 1)
-    def _():
-        pairs(second_ref, first_ref)
+def near_kernel(emb_ref, key_ref, one_ref, two_ref, grad_ref, out_ref):
+    out_ref[...] = grad_ref[...] + all_pairs(emb_ref, key_ref, one_ref)
+    out_ref[...] += all_pairs(emb_ref, key_ref, two_ref)
 
 
 def back_kernel(part, emb_ref, key_ref, *refs):
@@ -215,7 +181,9 @@
     at = slice(part * rows, (part + 1) * rows)
     grad = grad_ref[at]
     for ref in cols_refs:
-        grad += pair_grad(emb_ref[at], key_ref[at], ref[:both], ref[both:, :both])
+        start = max(0, both + KEY_ROWS - ref.shape[0])
+        n = both - start if start or part else rows
+        grad += pair_grad(emb_ref[at], key_ref[at], ref[:n], ref[both - start :, start : start + n])
     unit = unit_ref[at]
     inner = jnp.sum(grad * unit, axis=-1, keepdims=True)
     grad_x = (inv_ref[at, :1] * (grad - inner * unit)).astype(BF16)
@@ -282,14 +250,20 @@
     def flip(x):
         return lax.ppermute(x, AXES, route(lambda s, c, h: (s, 1 - c, h)))
 
-    def swap_or_next(x):
-        return lax.ppermute(x, AXES, route(lambda s, c, h: (s - c, c, 1 - h)))
-
-    def next_or_swap(x):
-        return lax.ppermute(x, AXES, route(lambda s, c, h: (s + 1 - c, c, 1 - h)))
+    def swap(x):
+        return lax.ppermute(x, AXES, route(lambda s, c, h: (s, c, 1 - h)))
+
+    def near(x):
+        return lax.ppermute(x, AXES, route(lambda s, c, h: (s + 1 - 2 * c, c, 1 - h)))
+
+    def across(x):
+        return lax.ppermute(x, AXES, route(lambda s, c, h: (s + 1 - 2 * c, c, h)))
 
     def second_next(x):
         return lax.ppermute(x, AXES, route(lambda s, c, h: (s + 2 - 4 * c, c, h)))
+
+    def second_across(x):
+        return lax.ppermute(x, AXES, route(lambda s, c, h: (s + 2 - 4 * c, c, 1 - h)))
 
     packet = ((both + KEY_ROWS, width), BF16)
     block_rows = ((rows, width), BF16)
@@ -308,32 +282,32 @@
     col_proj, row_proj = call(
         load_kernel, [ANY] + [HBM] * 2, [square] * 2, scratch=[semaphores((2,))]
     )(raw, held(image_proj), held(text_proj))
-    sent, again = call(sent_kernel, [VMEM] * 3, [packet] * 2)(raw, other, col_proj)
+    last_packet = ((rows + KEY_ROWS, width), BF16)
+    sent, last = call(sent_kernel, [VMEM] * 3, [packet, last_packet])(raw, other, col_proj)
 
     def after(array, *others):
         return call(
             after_kernel, [ANY] * (1 + len(others)), [packet], ANY, aliases={0: 0}
         )(array, *others)[0]
 
-    first = swap_or_next(sent)
+    near_one = near(sent)
+    near_two = across(sent)
+    swapped = swap(sent)
+    third = second_next(last)
+    fourth = second_across(last)
     total = ((both, width), F32)
     emb, unit, inv, key, grad = call(
         own_kernel,
         [VMEM] * 4 + [SMEM] * 2,
         [((both, width), BF16), total, ((both, 128), F32), ((both, 128), F32), total],
     )(raw, other, sent, row_proj, logit_scale, logit_bias)
-    second = next_or_swap(after(again, key))
-    first = after(first, key)
-    fifth = next_or_swap(first)
-    (far,) = call(far_pack_kernel, [VMEM] * 3, [packet])(sent, first, second)
-    far = second_next(far)
-    (grad,) = call(near_kernel, [VMEM] * 5, [total])(emb, key, first, second, grad)
+    (grad,) = call(near_kernel, [VMEM] * 5, [total])(emb, key, near_one, near_two, grad)
     (other_out,) = call(functools.partial(back_kernel, 1), [VMEM] * 7, [block_rows])(
-        emb, key, fifth, grad, unit, inv, row_proj
+        emb, key, swapped, grad, unit, inv, row_proj
     )
     given = flip(other_out)
-    (own_out,) = call(functools.partial(back_kernel, 0), [VMEM] * 8, [block_rows])(
-        emb, key, fifth, far, grad, unit, inv, row_proj
+    (own_out,) = call(functools.partial(back_kernel, 0), [VMEM] * 9, [block_rows])(
+        emb, key, swapped, third, fourth, grad, unit, inv, row_proj
     )
     return call(choose_kernel, [VMEM] * 2, [block_rows] * 2, HBM, [semaphores((2,))])(
         own_out, given

time: 55.6 us -> 51.4 us (0.924)
  the two profiles are of different devices: /device:TPU:2 before, /device:TPU:1 now
where the time goes in v4:
time: 51.4 us; the launch traced here: 50.9 us
  starting transfers between devices  39.2 us (76%)
  Pallas kernels  8.87 us (17%)
  between operations  2.08 us (4%)
  waiting for transfers between devices  0.73 us (1%)
    ppermute x2, starting transfers between devices, flip(): return lax.ppermute(x, AXES, route(lambda s, c, h: (s, 1 - c, h)))  18.8 us
    ppermute x1, starting transfers between devices, near(): lax.ppermute(x, AXES, route(lambda s, c, h: (s + 1 - 2 * c, c, 1 - h)))  10.4 us
    ppermute x1, starting transfers between devices, second_across(): lax.ppermute(x, AXES, route(lambda s, c, h: (s + 2 - 4 * c, c, 1 - h)))  3.01 us
    ppermute x1, starting transfers between devices, across(): return lax.ppermute(x, AXES, route(lambda s, c, h: (s + 1 - 2 * c, c, h)))  2.43 us
    ppermute x1, starting transfers between devices, second_next(): return lax.ppermute(x, AXES, route(lambda s, c, h: (s + 2 - 4 * c, c, h)))  2.37 us
    ppermute x1, starting transfers between devices, swap(): return lax.ppermute(x, AXES, route(lambda s, c, h: (s, c, 1 - h)))  2.16 us
    pallas_call x1, Pallas kernels, body(): call(load_kernel, [ANY] + [HBM] * 2, [square] * 2, scratch=[semaphores((2...  1.66 us
    pallas_call x1, Pallas kernels, body(): call(functools.partial(back_kernel, 0), [VMEM] * 9, [block_rows])  1.47 us
  transfers between devices with their start and end apart: 7, of which 1 were waited for; matrix products, arithmetic and copies ran while one was open for 0% of the time, Pallas kernels for 13%

profile of v4, /device:TPU:1, one launch (start us, length us, event | category | flops | bytes accessed | tf_op | source)
XLA Modules:
  0.0 50.9 jit_solution(7980283058198441837)
XLA Ops:
  0.6 1.1 %shard_map.86.raw_ref = bf16[272,768]{1,0:T(8,128)(2,1)S(1)} custom-call(bf16[128,768]{1,0:T(8,128)(2,1)} %image_ref.1, bf16[128,768]{1,0:T(8,128)(2,1)} %text_ref.1, s32[1,128]{1,0:T(1,128)} %bitcast.1), custom_call_target="tpu_custom_call" | custom-call | tf_op jit(solution)/shard_map/pallas_call | solution.py:274
  1.7 16.1 %collective-permute-start = (bf16[272,768]{1,0:T(8,128)(2,1)S(1)}, bf16[272,768]{1,0:T(8,128)(2,1)S(1)}, u32[]{:S(2)}, u32[]{:S(2)}) collective-permute-start(bf16[272,768]{1,0:T(8,128)(2,1)S(1)} %shard_map.86.raw_ref), channel_id=1, source_target_pairs={{0,2},{1,3},{2,0},{3,1},{4,6},{5,7},{6,4},{7,5},{8,10},{9,11},{10,... | collective-permute-start | bytes 1253384 | tf_op jit(solution)/shard_map/ppermute | solution.py:251
  17.8 1.7 %shard_map.87 = (bf16[768,768]{1,0:T(8,128)(2,1)S(1)}, bf16[768,768]{1,0:T(8,128)(2,1)S(1)}) custom-call(bf16[272,768]{1,0:T(8,128)(2,1)S(1)} %shard_map.86.raw_ref, bf16[768,768]{1,0:T(8,128)(2,1)} %image_proj_ref.1, bf16[768,768]{1,0:T(8,128)(2,1)} %text_proj_ref.1), custom_call_target="tpu_custom_call" | custom-call | tf_op jit(solution)/shard_map/pallas_call | solution.py:282
  19.4 0.0 collective-permute-done.other_ref
  19.5 0.6 %shard_map.88 = (bf16[272,768]{1,0:T(8,128)(2,1)S(1)}, bf16[144,768]{1,0:T(8,128)(2,1)S(1)}) custom-call(bf16[272,768]{1,0:T(8,128)(2,1)S(1)} %shard_map.86.raw_ref, bf16[272,768]{1,0:T(8,128)(2,1)S(1)} %collective-permute-done.other_ref, bf16[768,768]{1,0:T(8,128)(2,1)S(1)} %get-tuple-element.11.proj_ref), custom_call_target="tpu_custom_call" | custom-call | tf_op jit(solution)/shard_map/pallas_call | solution.py:286
  20.0 10.4 %collective-permute-start.4 = (bf16[272,768]{1,0:T(8,128)(2,1)S(1)}, bf16[272,768]{1,0:T(8,128)(2,1)S(1)}, u32[]{:S(2)}, u32[]{:S(2)}) collective-permute-start(bf16[272,768]{1,0:T(8,128)(2,1)S(1)} %get-tuple-element.12.sent_ref), channel_id=1, source_target_pairs={{0,5},{1,4},{2,1023},{3,1022},{4,9},{5,8},{6,3},{7,2},{8,13},{9,12... | collective-permute-start | bytes 1253384 | tf_op jit(solution)/shard_map/ppermute | solution.py:257
  30.4 2.4 %collective-permute-start.5 = (bf16[272,768]{1,0:T(8,128)(2,1)S(1)}, bf16[272,768]{1,0:T(8,128)(2,1)S(1)}, u32[]{:S(2)}, u32[]{:S(2)}) collective-permute-start(bf16[272,768]{1,0:T(8,128)(2,1)S(1)} %get-tuple-element.12.sent_ref), channel_id=1, source_target_pairs={{0,4},{1,5},{2,1022},{3,1023},{4,8},{5,9},{6,2},{7,3},{8,12},{9,13... | collective-permute-start | bytes 1253384 | tf_op jit(solution)/shard_map/ppermute | solution.py:260
  32.9 2.2 %collective-permute-start.1 = (bf16[272,768]{1,0:T(8,128)(2,1)S(1)}, bf16[272,768]{1,0:T(8,128)(2,1)S(1)}, u32[]{:S(2)}, u32[]{:S(2)}) collective-permute-start(bf16[272,768]{1,0:T(8,128)(2,1)S(1)} %get-tuple-element.12.sent_ref), channel_id=1, source_target_pairs={{0,1},{1,0},{2,3},{3,2},{4,5},{5,4},{6,7},{7,6},{8,9},{9,8},{10,11... | collective-permute-start | bytes 1253384 | tf_op jit(solution)/shard_map/ppermute | solution.py:254
  35.0 2.4 %collective-permute-start.2 = (bf16[144,768]{1,0:T(8,128)(2,1)S(1)}, bf16[144,768]{1,0:T(8,128)(2,1)S(1)}, u32[]{:S(2)}, u32[]{:S(2)}) collective-permute-start(bf16[144,768]{1,0:T(8,128)(2,1)S(1)} %get-tuple-element.16), channel_id=1, source_target_pairs={{0,8},{1,9},{2,1018},{3,1019},{4,12},{5,13},{6,1022},{7,1023},{8,1... | collective-permute-start | bytes 663560 | tf_op jit(solution)/shard_map/ppermute | solution.py:263
  37.4 3.0 %collective-permute-start.3 = (bf16[144,768]{1,0:T(8,128)(2,1)S(1)}, bf16[144,768]{1,0:T(8,128)(2,1)S(1)}, u32[]{:S(2)}, u32[]{:S(2)}) collective-permute-start(bf16[144,768]{1,0:T(8,128)(2,1)S(1)} %get-tuple-element.16), channel_id=1, source_target_pairs={{0,9},{1,8},{2,1019},{3,1018},{4,13},{5,12},{6,1023},{7,1022},{8,1... | collective-permute-start | bytes 663560 | tf_op jit(solution)/shard_map/ppermute | solution.py:266
  41.7 1.2 %shard_map.89 = (bf16[256,768]{1,0:T(8,128)(2,1)S(1)}, f32[256,768]{1,0:T(8,128)S(1)}, f32[256,128]{1,0:T(8,128)S(1)}, f32[256,128]{1,0:T(8,128)S(1)}, f32[256,768]{1,0:T(8,128)S(1)}) custom-call(bf16[272,768]{1,0:T(8,128)(2,1)S(1)} %shard_map.86.raw_ref, bf16[272,768]{1,0:T(8,128)(2,1)S(1)} %collective-permute-done.other_ref, ...), custom_call_target="tpu_custom_call" | custom-call | tf_op jit(solution)/shard_map/pallas_call | solution.py:299
  42.9 0.0 collective-permute-done.4.one_ref
  42.9 0.0 collective-permute-done.5.two_ref
  42.9 1.0 %shard_map.90.refs_3_.refs_1_ = f32[256,768]{1,0:T(8,128)S(1)} custom-call(bf16[256,768]{1,0:T(8,128)(2,1)S(1)} %get-tuple-element.14.emb_ref, f32[256,128]{1,0:T(8,128)S(1)} %get-tuple-element.15.key_ref, bf16[272,768]{1,0:T(8,128)(2,1)S(1)} %collective-permute-done.4.one_ref, bf16[272,768]{1,0:T(8,128)(2,1)S(1)} %collective-permute-done.5.two_ref, ...), custom_call_target="tpu_custom_call" | custom-call | tf_op jit(solution)/shard_map/pallas_call | solution.py:304
  43.9 0.7 %collective-permute-done.1.refs_0_ = bf16[272,768]{1,0:T(8,128)(2,1)S(1)} collective-permute-done((bf16[272,768]{1,0:T(8,128)(2,1)S(1)}, bf16[272,768]{1,0:T(8,128)(2,1)S(1)}, u32[]{:S(2)}, u32[]{:S(2)}) %collective-permute-start.1) | collective-permute-done | bytes 417824 | tf_op jit(solution)/shard_map/ppermute | solution.py:254
  44.7 1.2 %shard_map.92 = bf16[128,768]{1,0:T(8,128)(2,1)S(1)} custom-call(bf16[256,768]{1,0:T(8,128)(2,1)S(1)} %get-tuple-element.14.emb_ref, f32[256,128]{1,0:T(8,128)S(1)} %get-tuple-element.15.key_ref, bf16[272,768]{1,0:T(8,128)(2,1)S(1)} %collective-permute-done.1.refs_0_, f32[256,768]{1,0:T(8,128)S(1)} %shard_map.90.refs_3_.refs_1_, ...), custom_call_target="tpu_custom_call" | custom-call | tf_op jit(solution)/shard_map/pallas_call | solution.py:305
  45.8 2.7 %collective-permute-start.6 = (bf16[128,768]{1,0:T(8,128)(2,1)S(1)}, bf16[128,768]{1,0:T(8,128)(2,1)S(1)}, u32[]{:S(2)}, u32[]{:S(2)}) collective-permute-start(bf16[128,768]{1,0:T(8,128)(2,1)S(1)} %shard_map.92), channel_id=1, source_target_pairs={{0,2},{1,3},{2,0},{3,1},{4,6},{5,7},{6,4},{7,5},{8,10},{9,11},{10,... | collective-permute-start | bytes 589832 | tf_op jit(solution)/shard_map/ppermute | solution.py:251
  48.6 0.0 collective-permute-done.2.refs_1_
  48.6 0.0 collective-permute-done.3.refs_2_
  48.6 1.5 %shard_map.91.own_ref = bf16[128,768]{1,0:T(8,128)(2,1)S(1)} custom-call(bf16[256,768]{1,0:T(8,128)(2,1)S(1)} %get-tuple-element.14.emb_ref, f32[256,128]{1,0:T(8,128)S(1)} %get-tuple-element.15.key_ref, bf16[272,768]{1,0:T(8,128)(2,1)S(1)} %collective-permute-done.1.refs_0_, bf16[144,768]{1,0:T(8,128)(2,1)S(1)} %collective-permute-done.2.refs_1_, ...), custom_call_target="tpu_custom_call" | custom-call | tf_op jit(solution)/shard_map/pallas_call | solution.py:309
  50.1 0.0 collective-permute-done.6.given_ref
  50.1 0.8 %shard_map.93 = (bf16[128,768]{1,0:T(8,128)(2,1)}, bf16[128,768]{1,0:T(8,128)(2,1)}) custom-call(bf16[128,768]{1,0:T(8,128)(2,1)S(1)} %shard_map.91.own_ref, bf16[128,768]{1,0:T(8,128)(2,1)S(1)} %collective-permute-done.6.given_ref), custom_call_target="tpu_custom_call" | custom-call | tf_op jit(solution)/shard_map/pallas_call | solution.py:312
Async XLA Ops:
  1.7 17.7 %collective-permute-start = (bf16[272,768]{1,0:T(8,128)(2,1)S(1)}, bf16[272,768]{1,0:T(8,128)(2,1)S(1)}, u32[]{:S(2)}, u32[]{:S(2)}) collective-permute-start(bf16[272,768]{1,0:T(8,128)(2,1)S(1)} %shard_map.86.raw_ref), channel_id=1, source_target_pairs={{0,2},{1,3},{2,0},{3,1},{4,6},{5,7},{6,4},{7,5},{8,10},{9,11},{10,... | collective-permute-start | bytes 1253384 | tf_op jit(solution)/shard_map/ppermute | solution.py:251
  20.0 22.9 %collective-permute-start.4 = (bf16[272,768]{1,0:T(8,128)(2,1)S(1)}, bf16[272,768]{1,0:T(8,128)(2,1)S(1)}, u32[]{:S(2)}, u32[]{:S(2)}) collective-permute-start(bf16[272,768]{1,0:T(8,128)(2,1)S(1)} %get-tuple-element.12.sent_ref), channel_id=1, source_target_pairs={{0,5},{1,4},{2,1023},{3,1022},{4,9},{5,8},{6,3},{7,2},{8,13},{9,12... | collective-permute-start | bytes 1253384 | tf_op jit(solution)/shard_map/ppermute | solution.py:257
  30.4 12.5 %collective-permute-start.5 = (bf16[272,768]{1,0:T(8,128)(2,1)S(1)}, bf16[272,768]{1,0:T(8,128)(2,1)S(1)}, u32[]{:S(2)}, u32[]{:S(2)}) collective-permute-start(bf16[272,768]{1,0:T(8,128)(2,1)S(1)} %get-tuple-element.12.sent_ref), channel_id=1, source_target_pairs={{0,4},{1,5},{2,1022},{3,1023},{4,8},{5,9},{6,2},{7,3},{8,12},{9,13... | collective-permute-start | bytes 1253384 | tf_op jit(solution)/shard_map/ppermute | solution.py:260
  32.9 11.8 %collective-permute-start.1 = (bf16[272,768]{1,0:T(8,128)(2,1)S(1)}, bf16[272,768]{1,0:T(8,128)(2,1)S(1)}, u32[]{:S(2)}, u32[]{:S(2)}) collective-permute-start(bf16[272,768]{1,0:T(8,128)(2,1)S(1)} %get-tuple-element.12.sent_ref), channel_id=1, source_target_pairs={{0,1},{1,0},{2,3},{3,2},{4,5},{5,4},{6,7},{7,6},{8,9},{9,8},{10,11... | collective-permute-start | bytes 1253384 | tf_op jit(solution)/shard_map/ppermute | solution.py:254
  35.0 13.5 %collective-permute-start.2 = (bf16[144,768]{1,0:T(8,128)(2,1)S(1)}, bf16[144,768]{1,0:T(8,128)(2,1)S(1)}, u32[]{:S(2)}, u32[]{:S(2)}) collective-permute-start(bf16[144,768]{1,0:T(8,128)(2,1)S(1)} %get-tuple-element.16), channel_id=1, source_target_pairs={{0,8},{1,9},{2,1018},{3,1019},{4,12},{5,13},{6,1022},{7,1023},{8,1... | collective-permute-start | bytes 663560 | tf_op jit(solution)/shard_map/ppermute | solution.py:263
  37.4 11.2 %collective-permute-start.3 = (bf16[144,768]{1,0:T(8,128)(2,1)S(1)}, bf16[144,768]{1,0:T(8,128)(2,1)S(1)}, u32[]{:S(2)}, u32[]{:S(2)}) collective-permute-start(bf16[144,768]{1,0:T(8,128)(2,1)S(1)} %get-tuple-element.16), channel_id=1, source_target_pairs={{0,9},{1,8},{2,1019},{3,1018},{4,13},{5,12},{6,1023},{7,1022},{8,1... | collective-permute-start | bytes 663560 | tf_op jit(solution)/shard_map/ppermute | solution.py:266
  45.8 4.3 %collective-permute-start.6 = (bf16[128,768]{1,0:T(8,128)(2,1)S(1)}, bf16[128,768]{1,0:T(8,128)(2,1)S(1)}, u32[]{:S(2)}, u32[]{:S(2)}) collective-permute-start(bf16[128,768]{1,0:T(8,128)(2,1)S(1)} %shard_map.92), channel_id=1, source_target_pairs={{0,2},{1,3},{2,0},{3,1},{4,6},{5,7},{6,4},{7,5},{8,10},{9,11},{10,... | collective-permute-start | bytes 589832 | tf_op jit(solution)/shard_map/ppermute | solution.py:251

commit v5 on v4

--- a/solution.py
+++ b/solution.py
@@ -171,7 +171,7 @@
 
 def near_kernel(emb_ref, key_ref, one_ref, two_ref, grad_ref, out_ref):
     out_ref[...] = grad_ref[...] + all_pairs(emb_ref, key_ref, one_ref)
-    out_ref[...] += all_pairs(emb_ref, key_ref, two_ref)
+    own_pairs(emb_ref, key_ref, two_ref, out_ref, True)
 
 
 def back_kernel(part, emb_ref, key_ref, *refs):
@@ -182,7 +182,7 @@
     grad = grad_ref[at]
     for ref in cols_refs:
         start = max(0, both + KEY_ROWS - ref.shape[0])
-        n = both - start if start or part else rows
+        n = both - start
         grad += pair_grad(emb_ref[at], key_ref[at], ref[:n], ref[both - start :, start : start + n])
     unit = unit_ref[at]
     inner = jnp.sum(grad * unit, axis=-1, keepdims=True)
@@ -291,8 +291,8 @@
         )(array, *others)[0]
 
     near_one = near(sent)
+    swapped = swap(sent)
     near_two = across(sent)
-    swapped = swap(sent)
     third = second_next(last)
     fourth = second_across(last)
     total = ((both, width), F32)
@@ -301,13 +301,13 @@
         [VMEM] * 4 + [SMEM] * 2,
         [((both, width), BF16), total, ((both, 128), F32), ((both, 128), F32), total],
     )(raw, other, sent, row_proj, logit_scale, logit_bias)
-    (grad,) = call(near_kernel, [VMEM] * 5, [total])(emb, key, near_one, near_two, grad)
+    (grad,) = call(near_kernel, [VMEM] * 5, [total])(emb, key, near_one, swapped, grad)
     (other_out,) = call(functools.partial(back_kernel, 1), [VMEM] * 7, [block_rows])(
-        emb, key, swapped, grad, unit, inv, row_proj
+        emb, key, near_two, grad, unit, inv, row_proj
     )
     given = flip(other_out)
     (own_out,) = call(functools.partial(back_kernel, 0), [VMEM] * 9, [block_rows])(
-        emb, key, swapped, third, fourth, grad, unit, inv, row_proj
+        emb, key, near_two, third, fourth, grad, unit, inv, row_proj
     )
     return call(choose_kernel, [VMEM] * 2, [block_rows] * 2, HBM, [semaphores((2,))])(
         own_out, given

time: 51.4 us -> 50.9 us (level)
  starting transfers between devices: 39.2 us -> 37.9 us
  waiting for transfers between devices: 0.73 us -> 1.62 us
    ppermute x1, starting transfers between devices: 3.01 us -> 1.92 us  [second_across(): lax.ppermute(x, AXES, route(lambda s, c, h: (s + 2 - 4 * c, c, 1 - h)))]
    ppermute x1, waiting for transfers between devices: 0.71 us -> 1.61 us  [swap(): return lax.ppermute(x, AXES, route(lambda s, c, h: (s, c, 1 - h)))]
    ppermute x1, starting transfers between devices: 2.43 us -> 3.28 us  [across(): return lax.ppermute(x, AXES, route(lambda s, c, h: (s + 1 - 2 * c, c, h)))]
    ppermute x2, starting transfers between devices: 18.8 us -> 18 us  [flip(): return lax.ppermute(x, AXES, route(lambda s, c, h: (s, 1 - c, h)))]
where the time goes in v5:
time: 50.9 us; the launch traced here: 50.5 us
  starting transfers between devices  37.9 us (74%)
  Pallas kernels  8.98 us (18%)
  between operations  2.08 us (4%)
  waiting for transfers between devices  1.62 us (3%)
    ppermute x2, starting transfers between devices, flip(): return lax.ppermute(x, AXES, route(lambda s, c, h: (s, 1 - c, h)))  18 us
    ppermute x1, starting transfers between devices, near(): lax.ppermute(x, AXES, route(lambda s, c, h: (s + 1 - 2 * c, c, 1 - h)))  10.4 us
    ppermute x1, starting transfers between devices, across(): return lax.ppermute(x, AXES, route(lambda s, c, h: (s + 1 - 2 * c, c, h)))  3.28 us
    ppermute x1, starting transfers between devices, second_next(): return lax.ppermute(x, AXES, route(lambda s, c, h: (s + 2 - 4 * c, c, h)))  2.37 us
    ppermute x1, starting transfers between devices, swap(): return lax.ppermute(x, AXES, route(lambda s, c, h: (s, c, 1 - h)))  1.92 us
    ppermute x1, starting transfers between devices, second_across(): lax.ppermute(x, AXES, route(lambda s, c, h: (s + 2 - 4 * c, c, 1 - h)))  1.92 us
    pallas_call x1, Pallas kernels, body(): call(load_kernel, [ANY] + [HBM] * 2, [square] * 2, scratch=[semaphores((2...  1.66 us
    ppermute x1, waiting for transfers between devices, swap(): return lax.ppermute(x, AXES, route(lambda s, c, h: (s, c, 1 - h)))  1.61 us
  transfers between devices with their start and end apart: 7, of which 1 were waited for; matrix products, arithmetic and copies ran while one was open for 0% of the time, Pallas kernels for 13%

profile of v5, /device:TPU:1, one launch (start us, length us, event | category | flops | bytes accessed | tf_op | source)
XLA Modules:
  0.0 50.5 jit_solution(4876572934909687837)
XLA Ops:
  0.6 1.1 %shard_map.86.raw_ref = bf16[272,768]{1,0:T(8,128)(2,1)S(1)} custom-call(bf16[128,768]{1,0:T(8,128)(2,1)} %image_ref.1, bf16[128,768]{1,0:T(8,128)(2,1)} %text_ref.1, s32[1,128]{1,0:T(1,128)} %bitcast.1), custom_call_target="tpu_custom_call" | custom-call | tf_op jit(solution)/shard_map/pallas_call | solution.py:274
  1.7 16.1 %collective-permute-start = (bf16[272,768]{1,0:T(8,128)(2,1)S(1)}, bf16[272,768]{1,0:T(8,128)(2,1)S(1)}, u32[]{:S(2)}, u32[]{:S(2)}) collective-permute-start(bf16[272,768]{1,0:T(8,128)(2,1)S(1)} %shard_map.86.raw_ref), channel_id=1, source_target_pairs={{0,2},{1,3},{2,0},{3,1},{4,6},{5,7},{6,4},{7,5},{8,10},{9,11},{10,... | collective-permute-start | bytes 1253384 | tf_op jit(solution)/shard_map/ppermute | solution.py:251
  17.8 1.7 %shard_map.87 = (bf16[768,768]{1,0:T(8,128)(2,1)S(1)}, bf16[768,768]{1,0:T(8,128)(2,1)S(1)}) custom-call(bf16[272,768]{1,0:T(8,128)(2,1)S(1)} %shard_map.86.raw_ref, bf16[768,768]{1,0:T(8,128)(2,1)} %image_proj_ref.1, bf16[768,768]{1,0:T(8,128)(2,1)} %text_proj_ref.1), custom_call_target="tpu_custom_call" | custom-call | tf_op jit(solution)/shard_map/pallas_call | solution.py:282
  19.4 0.0 collective-permute-done.other_ref
  19.5 0.6 %shard_map.88 = (bf16[272,768]{1,0:T(8,128)(2,1)S(1)}, bf16[144,768]{1,0:T(8,128)(2,1)S(1)}) custom-call(bf16[272,768]{1,0:T(8,128)(2,1)S(1)} %shard_map.86.raw_ref, bf16[272,768]{1,0:T(8,128)(2,1)S(1)} %collective-permute-done.other_ref, bf16[768,768]{1,0:T(8,128)(2,1)S(1)} %get-tuple-element.11.proj_ref), custom_call_target="tpu_custom_call" | custom-call | tf_op jit(solution)/shard_map/pallas_call | solution.py:286
  20.0 10.4 %collective-permute-start.4 = (bf16[272,768]{1,0:T(8,128)(2,1)S(1)}, bf16[272,768]{1,0:T(8,128)(2,1)S(1)}, u32[]{:S(2)}, u32[]{:S(2)}) collective-permute-start(bf16[272,768]{1,0:T(8,128)(2,1)S(1)} %get-tuple-element.12.sent_ref), channel_id=1, source_target_pairs={{0,5},{1,4},{2,1023},{3,1022},{4,9},{5,8},{6,3},{7,2},{8,13},{9,12... | collective-permute-start | bytes 1253384 | tf_op jit(solution)/shard_map/ppermute | solution.py:257
  30.4 1.9 %collective-permute-start.5 = (bf16[272,768]{1,0:T(8,128)(2,1)S(1)}, bf16[272,768]{1,0:T(8,128)(2,1)S(1)}, u32[]{:S(2)}, u32[]{:S(2)}) collective-permute-start(bf16[272,768]{1,0:T(8,128)(2,1)S(1)} %get-tuple-element.12.sent_ref), channel_id=1, source_target_pairs={{0,1},{1,0},{2,3},{3,2},{4,5},{5,4},{6,7},{7,6},{8,9},{9,8},{10,11... | collective-permute-start | bytes 1253384 | tf_op jit(solution)/shard_map/ppermute | solution.py:254
  32.4 3.3 %collective-permute-start.1 = (bf16[272,768]{1,0:T(8,128)(2,1)S(1)}, bf16[272,768]{1,0:T(8,128)(2,1)S(1)}, u32[]{:S(2)}, u32[]{:S(2)}) collective-permute-start(bf16[272,768]{1,0:T(8,128)(2,1)S(1)} %get-tuple-element.12.sent_ref), channel_id=1, source_target_pairs={{0,4},{1,5},{2,1022},{3,1023},{4,8},{5,9},{6,2},{7,3},{8,12},{9,13... | collective-permute-start | bytes 1253384 | tf_op jit(solution)/shard_map/ppermute | solution.py:260
  35.7 2.4 %collective-permute-start.2 = (bf16[144,768]{1,0:T(8,128)(2,1)S(1)}, bf16[144,768]{1,0:T(8,128)(2,1)S(1)}, u32[]{:S(2)}, u32[]{:S(2)}) collective-permute-start(bf16[144,768]{1,0:T(8,128)(2,1)S(1)} %get-tuple-element.16), channel_id=1, source_target_pairs={{0,8},{1,9},{2,1018},{3,1019},{4,12},{5,13},{6,1022},{7,1023},{8,1... | collective-permute-start | bytes 663560 | tf_op jit(solution)/shard_map/ppermute | solution.py:263
  38.0 1.9 %collective-permute-start.3 = (bf16[144,768]{1,0:T(8,128)(2,1)S(1)}, bf16[144,768]{1,0:T(8,128)(2,1)S(1)}, u32[]{:S(2)}, u32[]{:S(2)}) collective-permute-start(bf16[144,768]{1,0:T(8,128)(2,1)S(1)} %get-tuple-element.16), channel_id=1, source_target_pairs={{0,9},{1,8},{2,1019},{3,1018},{4,13},{5,12},{6,1023},{7,1022},{8,1... | collective-permute-start | bytes 663560 | tf_op jit(solution)/shard_map/ppermute | solution.py:266
  41.3 1.2 %shard_map.89 = (bf16[256,768]{1,0:T(8,128)(2,1)S(1)}, f32[256,768]{1,0:T(8,128)S(1)}, f32[256,128]{1,0:T(8,128)S(1)}, f32[256,128]{1,0:T(8,128)S(1)}, f32[256,768]{1,0:T(8,128)S(1)}) custom-call(bf16[272,768]{1,0:T(8,128)(2,1)S(1)} %shard_map.86.raw_ref, bf16[272,768]{1,0:T(8,128)(2,1)S(1)} %collective-permute-done.other_ref, ...), custom_call_target="tpu_custom_call" | custom-call | tf_op jit(solution)/shard_map/pallas_call | solution.py:299
  42.4 0.0 collective-permute-done.4.one_ref
  42.4 1.6 %collective-permute-done.5.two_ref = bf16[272,768]{1,0:T(8,128)(2,1)S(1)} collective-permute-done((bf16[272,768]{1,0:T(8,128)(2,1)S(1)}, bf16[272,768]{1,0:T(8,128)(2,1)S(1)}, u32[]{:S(2)}, u32[]{:S(2)}) %collective-permute-start.5) | collective-permute-done | bytes 417824 | tf_op jit(solution)/shard_map/ppermute | solution.py:254
  44.1 1.0 %shard_map.90.refs_3_.refs_1_ = f32[256,768]{1,0:T(8,128)S(1)} custom-call(bf16[256,768]{1,0:T(8,128)(2,1)S(1)} %get-tuple-element.14.emb_ref, f32[256,128]{1,0:T(8,128)S(1)} %get-tuple-element.15.key_ref, bf16[272,768]{1,0:T(8,128)(2,1)S(1)} %collective-permute-done.4.one_ref, bf16[272,768]{1,0:T(8,128)(2,1)S(1)} %collective-permute-done.5.two_ref, ...), custom_call_target="tpu_custom_call" | custom-call | tf_op jit(solution)/shard_map/pallas_call | solution.py:304
  45.1 0.0 collective-permute-done.1.refs_0_
  45.1 1.2 %shard_map.92 = bf16[128,768]{1,0:T(8,128)(2,1)S(1)} custom-call(bf16[256,768]{1,0:T(8,128)(2,1)S(1)} %get-tuple-element.14.emb_ref, f32[256,128]{1,0:T(8,128)S(1)} %get-tuple-element.15.key_ref, bf16[272,768]{1,0:T(8,128)(2,1)S(1)} %collective-permute-done.1.refs_0_, f32[256,768]{1,0:T(8,128)S(1)} %shard_map.90.refs_3_.refs_1_, ...), custom_call_target="tpu_custom_call" | custom-call | tf_op jit(solution)/shard_map/pallas_call | solution.py:305
  46.3 1.9 %collective-permute-start.6 = (bf16[128,768]{1,0:T(8,128)(2,1)S(1)}, bf16[128,768]{1,0:T(8,128)(2,1)S(1)}, u32[]{:S(2)}, u32[]{:S(2)}) collective-permute-start(bf16[128,768]{1,0:T(8,128)(2,1)S(1)} %shard_map.92), channel_id=1, source_target_pairs={{0,2},{1,3},{2,0},{3,1},{4,6},{5,7},{6,4},{7,5},{8,10},{9,11},{10,... | collective-permute-start | bytes 589832 | tf_op jit(solution)/shard_map/ppermute | solution.py:251
  48.2 0.0 collective-permute-done.2.refs_1_
  48.2 0.0 collective-permute-done.3.refs_2_
  48.2 1.5 %shard_map.91.own_ref = bf16[128,768]{1,0:T(8,128)(2,1)S(1)} custom-call(bf16[256,768]{1,0:T(8,128)(2,1)S(1)} %get-tuple-element.14.emb_ref, f32[256,128]{1,0:T(8,128)S(1)} %get-tuple-element.15.key_ref, bf16[272,768]{1,0:T(8,128)(2,1)S(1)} %collective-permute-done.1.refs_0_, bf16[144,768]{1,0:T(8,128)(2,1)S(1)} %collective-permute-done.2.refs_1_, ...), custom_call_target="tpu_custom_call" | custom-call | tf_op jit(solution)/shard_map/pallas_call | solution.py:309
  49.8 0.0 collective-permute-done.6.given_ref
  49.8 0.8 %shard_map.93 = (bf16[128,768]{1,0:T(8,128)(2,1)}, bf16[128,768]{1,0:T(8,128)(2,1)}) custom-call(bf16[128,768]{1,0:T(8,128)(2,1)S(1)} %shard_map.91.own_ref, bf16[128,768]{1,0:T(8,128)(2,1)S(1)} %collective-permute-done.6.given_ref), custom_call_target="tpu_custom_call" | custom-call | tf_op jit(solution)/shard_map/pallas_call | solution.py:312
Async XLA Ops:
  1.7 17.7 %collective-permute-start = (bf16[272,768]{1,0:T(8,128)(2,1)S(1)}, bf16[272,768]{1,0:T(8,128)(2,1)S(1)}, u32[]{:S(2)}, u32[]{:S(2)}) collective-permute-start(bf16[272,768]{1,0:T(8,128)(2,1)S(1)} %shard_map.86.raw_ref), channel_id=1, source_target_pairs={{0,2},{1,3},{2,0},{3,1},{4,6},{5,7},{6,4},{7,5},{8,10},{9,11},{10,... | collective-permute-start | bytes 1253384 | tf_op jit(solution)/shard_map/ppermute | solution.py:251
  20.0 22.4 %collective-permute-start.4 = (bf16[272,768]{1,0:T(8,128)(2,1)S(1)}, bf16[272,768]{1,0:T(8,128)(2,1)S(1)}, u32[]{:S(2)}, u32[]{:S(2)}) collective-permute-start(bf16[272,768]{1,0:T(8,128)(2,1)S(1)} %get-tuple-element.12.sent_ref), channel_id=1, source_target_pairs={{0,5},{1,4},{2,1023},{3,1022},{4,9},{5,8},{6,3},{7,2},{8,13},{9,12... | collective-permute-start | bytes 1253384 | tf_op jit(solution)/shard_map/ppermute | solution.py:257
  30.4 13.6 %collective-permute-start.5 = (bf16[272,768]{1,0:T(8,128)(2,1)S(1)}, bf16[272,768]{1,0:T(8,128)(2,1)S(1)}, u32[]{:S(2)}, u32[]{:S(2)}) collective-permute-start(bf16[272,768]{1,0:T(8,128)(2,1)S(1)} %get-tuple-element.12.sent_ref), channel_id=1, source_target_pairs={{0,1},{1,0},{2,3},{3,2},{4,5},{5,4},{6,7},{7,6},{8,9},{9,8},{10,11... | collective-permute-start | bytes 1253384 | tf_op jit(solution)/shard_map/ppermute | solution.py:254
  32.4 12.7 %collective-permute-start.1 = (bf16[272,768]{1,0:T(8,128)(2,1)S(1)}, bf16[272,768]{1,0:T(8,128)(2,1)S(1)}, u32[]{:S(2)}, u32[]{:S(2)}) collective-permute-start(bf16[272,768]{1,0:T(8,128)(2,1)S(1)} %get-tuple-element.12.sent_ref), channel_id=1, source_target_pairs={{0,4},{1,5},{2,1022},{3,1023},{4,8},{5,9},{6,2},{7,3},{8,12},{9,13... | collective-permute-start | bytes 1253384 | tf_op jit(solution)/shard_map/ppermute | solution.py:260
  35.7 12.6 %collective-permute-start.2 = (bf16[144,768]{1,0:T(8,128)(2,1)S(1)}, bf16[144,768]{1,0:T(8,128)(2,1)S(1)}, u32[]{:S(2)}, u32[]{:S(2)}) collective-permute-start(bf16[144,768]{1,0:T(8,128)(2,1)S(1)} %get-tuple-element.16), channel_id=1, source_target_pairs={{0,8},{1,9},{2,1018},{3,1019},{4,12},{5,13},{6,1022},{7,1023},{8,1... | collective-permute-start | bytes 663560 | tf_op jit(solution)/shard_map/ppermute | solution.py:263
  38.0 10.2 %collective-permute-start.3 = (bf16[144,768]{1,0:T(8,128)(2,1)S(1)}, bf16[144,768]{1,0:T(8,128)(2,1)S(1)}, u32[]{:S(2)}, u32[]{:S(2)}) collective-permute-start(bf16[144,768]{1,0:T(8,128)(2,1)S(1)} %get-tuple-element.16), channel_id=1, source_target_pairs={{0,9},{1,8},{2,1019},{3,1018},{4,13},{5,12},{6,1023},{7,1022},{8,1... | collective-permute-start | bytes 663560 | tf_op jit(solution)/shard_map/ppermute | solution.py:266
  46.3 3.5 %collective-permute-start.6 = (bf16[128,768]{1,0:T(8,128)(2,1)S(1)}, bf16[128,768]{1,0:T(8,128)(2,1)S(1)}, u32[]{:S(2)}, u32[]{:S(2)}) collective-permute-start(bf16[128,768]{1,0:T(8,128)(2,1)S(1)} %shard_map.92), channel_id=1, source_target_pairs={{0,2},{1,3},{2,0},{3,1},{4,6},{5,7},{6,4},{7,5},{8,10},{9,11},{10,... | collective-permute-start | bytes 589832 | tf_op jit(solution)/shard_map/ppermute | solution.py:251

commit v6 on v5

--- a/solution.py
+++ b/solution.py
@@ -46,7 +46,9 @@
     image_ref,
     text_ref,
     match_ref,
+    proj_ref,
     raw_ref,
+    held_ref,
     match_vmem,
     sems,
 ):
@@ -55,6 +57,7 @@
         pltpu.make_async_copy(match_ref, match_vmem, sems.at[0]),
         pltpu.make_async_copy(image_ref, raw_ref.at[:rows], sems.at[1]),
         pltpu.make_async_copy(text_ref, raw_ref.at[rows : 2 * rows], sems.at[2]),
+        pltpu.make_async_copy(proj_ref, held_ref, sems.at[3]),
     ]
     for copy in copies:
         copy.start()
@@ -66,26 +69,15 @@
         copy.wait()
 
 
-def load_kernel(raw_ref, image_proj_ref, text_proj_ref, col_proj_ref, row_proj_ref, sems):
+def scalars_kernel(raw_ref, scale_ref, bias_ref, out_ref):
+    lane = lax.broadcasted_iota(jnp.int32, out_ref.shape, 1)
+    out_ref[...] = jnp.where(lane == 1, scale_ref[0], bias_ref[0])
+
+
+def by_core(on_text, on_image):
     _, _, core = place()
-
-    def load(col_from, row_from):
-        copies = [
-            pltpu.make_async_copy(col_from, col_proj_ref, sems.at[0]),
-            pltpu.make_async_copy(row_from, row_proj_ref, sems.at[1]),
-        ]
-        for copy in copies:
-            copy.start()
-        for copy in copies:
-            copy.wait()
-
-    @pl.when(core == 0)
-    def _():
-        load(text_proj_ref, image_proj_ref)
-
-    @pl.when(core == 1)
-    def _():
-        load(image_proj_ref, text_proj_ref)
+    pl.when(core == 0)(on_text)
+    pl.when(core == 1)(on_image)
 
 
 def normed(feats, proj):
@@ -94,15 +86,21 @@
     return x * inv, inv
 
 
-def sent_kernel(raw_ref, other_ref, proj_ref, sent_ref, last_ref):
+def sent_kernel(
+    raw_ref, other_ref, scalars_ref, image_proj_ref, text_proj_ref, sent_ref, last_ref
+):
     rows = (raw_ref.shape[0] - KEY_ROWS) // 2
     both = 2 * rows
     width = raw_ref.shape[1]
     block, half, core = place()
-    start = pl.multiple_of((1 - core) * rows, rows)
+
+    def project(start, proj_ref):
+        for n, ref in enumerate((raw_ref, other_ref)):
+            unit, _ = normed(ref[start : start + rows], proj_ref[...])
+            sent_ref[n * rows : (n + 1) * rows] = unit.astype(BF16)
+
+    by_core(lambda: project(rows, text_proj_ref), lambda: project(0, image_proj_ref))
     for n, ref in enumerate((raw_ref, other_ref)):
-        unit, _ = normed(ref[pl.ds(start, rows)], proj_ref[...])
-        sent_ref[n * rows : (n + 1) * rows] = unit.astype(BF16)
         sent_ref[both:, n * rows : (n + 1) * rows] = jnp.where(
             core == 0, text_key_tile(block ^ n, half, rows), ref[both:, :rows]
         )
@@ -122,9 +120,10 @@
     raw_ref,
     other_ref,
     sent_ref,
-    proj_ref,
-    scale_ref,
-    bias_ref,
+    scalars_ref,
+    near_ref,
+    image_proj_ref,
+    text_proj_ref,
     emb_ref,
     unit_ref,
     inv_ref,
@@ -134,18 +133,23 @@
     rows = (raw_ref.shape[0] - KEY_ROWS) // 2
     both = 2 * rows
     block, half, core = place()
-    start = pl.multiple_of(core * rows, rows)
     lane = lax.broadcasted_iota(jnp.int32, (rows, 128), 1)
+
+    def project(start, proj_ref):
+        for n, ref in enumerate((raw_ref, other_ref)):
+            at = slice(n * rows, (n + 1) * rows)
+            unit, inv = normed(ref[start : start + rows], proj_ref[...])
+            unit_ref[at] = unit
+            inv_ref[at] = jnp.broadcast_to(inv, (rows, 128))
+            emb_ref[at] = unit.astype(BF16)
+
+    by_core(lambda: project(0, image_proj_ref), lambda: project(rows, text_proj_ref))
     for n, ref in enumerate((raw_ref, other_ref)):
         at = slice(n * rows, (n + 1) * rows)
-        unit, inv = normed(ref[pl.ds(start, rows)], proj_ref[...])
-        unit_ref[at] = unit
-        inv_ref[at] = jnp.broadcast_to(inv, (rows, 128))
-        emb_ref[at] = unit.astype(BF16)
         tile = jnp.where(core == 0, ref[both:, :rows], text_key_tile(block ^ n, half, rows))
-        scalars = jnp.where(lane == 1, scale_ref[0], bias_ref[0])
-        key_ref[at] = jnp.where(lane == 0, as_column(joined_key(tile)), scalars)
-    own_pairs(emb_ref, key_ref, sent_ref, grad_ref, False)
+        key_ref[at] = jnp.where(lane == 0, as_column(joined_key(tile)), scalars_ref[:1])
+    grad_ref[...] = all_pairs(emb_ref, key_ref, near_ref)
+    own_pairs(emb_ref, key_ref, sent_ref, grad_ref, True)
 
 
 def own_pairs(emb_ref, key_ref, cols_ref, grad_ref, add):
@@ -169,25 +173,24 @@
     pass
 
 
-def near_kernel(emb_ref, key_ref, one_ref, two_ref, grad_ref, out_ref):
-    out_ref[...] = grad_ref[...] + all_pairs(emb_ref, key_ref, one_ref)
-    own_pairs(emb_ref, key_ref, two_ref, out_ref, True)
-
-
 def back_kernel(part, emb_ref, key_ref, *refs):
-    *cols_refs, grad_ref, unit_ref, inv_ref, proj_ref, out_ref = refs
+    *cols_refs, grad_ref, unit_ref, inv_ref, image_proj_ref, text_proj_ref, out_ref = refs
     rows = out_ref.shape[0]
     both = 2 * rows
     at = slice(part * rows, (part + 1) * rows)
     grad = grad_ref[at]
-    for ref in cols_refs:
+    for place_in, ref in enumerate(cols_refs):
         start = max(0, both + KEY_ROWS - ref.shape[0])
-        n = both - start
+        n = rows if place_in + part == 0 else both - start
         grad += pair_grad(emb_ref[at], key_ref[at], ref[:n], ref[both - start :, start : start + n])
     unit = unit_ref[at]
     inner = jnp.sum(grad * unit, axis=-1, keepdims=True)
     grad_x = (inv_ref[at, :1] * (grad - inner * unit)).astype(BF16)
-    out_ref[...] = rows_dot(grad_x, proj_ref[...]).astype(BF16)
+
+    def finish(proj_ref):
+        out_ref[...] = rows_dot(grad_x, proj_ref[...]).astype(BF16)
+
+    by_core(lambda: finish(image_proj_ref), lambda: finish(text_proj_ref))
 
 
 def choose_kernel(own_ref, given_ref, image_ref, text_ref, sems):
@@ -218,7 +221,9 @@
 ANY = pl.BlockSpec(memory_space=pl.ANY)
 
 
-def call(kernel, in_specs, outs, out_spec=VMEM, scratch=(), aliases={}, vmem=24 * 2**20):
+def call(
+    kernel, in_specs, outs, out_spec=VMEM, scratch=(), aliases={}, vmem=24 * 2**20, nbytes=0
+):
     where = pltpu.VMEM if out_spec is VMEM else jax.ShapeDtypeStruct
     shapes = tuple(where(shape, kind) for shape, kind in outs)
     return pl.pallas_call(
@@ -229,7 +234,7 @@
         scratch_shapes=scratch,
         input_output_aliases=aliases,
         compiler_params=pltpu.CompilerParams(vmem_limit_bytes=vmem),
-        cost_estimate=pl.CostEstimate(flops=0, bytes_accessed=0, transcendentals=0),
+        cost_estimate=pl.CostEstimate(flops=0, bytes_accessed=nbytes, transcendentals=0),
     )
 
 
@@ -271,19 +276,20 @@
     def held(x):
         return pltpu.with_memory_space_constraint(x, pltpu.HBM)
 
-    (raw,) = call(
+    raw, text_proj = call(
         pack_kernel,
-        [HBM] * 3,
-        [packet],
-        scratch=[pltpu.VMEM((1, rows), jnp.int32), semaphores((3,))],
-    )(held(image_feats), held(text_feats), held(match.reshape(1, rows)))
+        [HBM] * 4,
+        [packet, ((width, width), BF16)],
+        scratch=[pltpu.VMEM((1, rows), jnp.int32), semaphores((4,))],
+    )(held(image_feats), held(text_feats), held(match.reshape(1, rows)), held(text_proj))
     other = flip(raw)
-    square = ((width, width), BF16)
-    col_proj, row_proj = call(
-        load_kernel, [ANY] + [HBM] * 2, [square] * 2, scratch=[semaphores((2,))]
-    )(raw, held(image_proj), held(text_proj))
+    (scalars,) = call(scalars_kernel, [ANY] + [SMEM] * 2, [((8, 128), F32)])(
+        raw, logit_scale, logit_bias
+    )
     last_packet = ((rows + KEY_ROWS, width), BF16)
-    sent, last = call(sent_kernel, [VMEM] * 3, [packet, last_packet])(raw, other, col_proj)
+    sent, last = call(sent_kernel, [VMEM] * 5, [packet, last_packet])(
+        raw, other, scalars, image_proj, text_proj
+    )
 
     def after(array, *others):
         return call(
@@ -298,16 +304,15 @@
     total = ((both, width), F32)
     emb, unit, inv, key, grad = call(
         own_kernel,
-        [VMEM] * 4 + [SMEM] * 2,
+        [VMEM] * 7,
         [((both, width), BF16), total, ((both, 128), F32), ((both, 128), F32), total],
-    )(raw, other, sent, row_proj, logit_scale, logit_bias)
-    (grad,) = call(near_kernel, [VMEM] * 5, [total])(emb, key, near_one, swapped, grad)
-    (other_out,) = call(functools.partial(back_kernel, 1), [VMEM] * 7, [block_rows])(
-        emb, key, near_two, grad, unit, inv, row_proj
+    )(raw, other, sent, scalars, near_one, image_proj, text_proj)
+    (other_out,) = call(functools.partial(back_kernel, 1), [VMEM] * 9, [block_rows])(
+        emb, key, swapped, near_two, grad, unit, inv, image_proj, text_proj
     )
     given = flip(other_out)
-    (own_out,) = call(functools.partial(back_kernel, 0), [VMEM] * 9, [block_rows])(
-        emb, key, near_two, third, fourth, grad, unit, inv, row_proj
+    (own_out,) = call(functools.partial(back_kernel, 0), [VMEM] * 11, [block_rows])(
+        emb, key, swapped, near_two, third, fourth, grad, unit, inv, image_proj, text_proj
     )
     return call(choose_kernel, [VMEM] * 2, [block_rows] * 2, HBM, [semaphores((2,))])(
         own_out, given

time: 50.9 us -> 50.9 us (level)
  Pallas kernels: 8.98 us -> 7.83 us
  waiting for transfers between devices: 1.62 us -> 2.45 us
    pallas_call x7 -> x6, Pallas kernels: 8.2 us -> 7.06 us  [the longest x1 1.69 us: body(): call(own_kernel, [VMEM] * 7, [((both, width), BF16), total, ((both, 128),...]
    ppermute x1, waiting for transfers between devices: 1.61 us -> 2.38 us  [swap(): return lax.ppermute(x, AXES, route(lambda s, c, h: (s, c, 1 - h)))]
  transfers between devices with their start and end apart: 7 -> 7, of which waited for: 1 -> 2; matrix products, arithmetic and copies ran while one was open for 0% -> 0% of each run, Pallas kernels for 13% -> 10%
where the time goes in v6:
time: 50.9 us; the launch traced here: 50.5 us
  starting transfers between devices  38.2 us (75%)
  Pallas kernels  7.83 us (15%)
  waiting for transfers between devices  2.45 us (5%)
  between operations  2.05 us (4%)
    ppermute x2, starting transfers between devices, flip(): return lax.ppermute(x, AXES, route(lambda s, c, h: (s, 1 - c, h)))  18.3 us
    ppermute x1, starting transfers between devices, near(): lax.ppermute(x, AXES, route(lambda s, c, h: (s + 1 - 2 * c, c, 1 - h)))  10.4 us
    ppermute x1, starting transfers between devices, across(): return lax.ppermute(x, AXES, route(lambda s, c, h: (s + 1 - 2 * c, c, h)))  3.28 us
    ppermute x1, waiting for transfers between devices, swap(): return lax.ppermute(x, AXES, route(lambda s, c, h: (s, c, 1 - h)))  2.38 us
    ppermute x1, starting transfers between devices, second_next(): return lax.ppermute(x, AXES, route(lambda s, c, h: (s + 2 - 4 * c, c, h)))  2.37 us
    ppermute x1, starting transfers between devices, swap(): return lax.ppermute(x, AXES, route(lambda s, c, h: (s, c, 1 - h)))  1.92 us
    ppermute x1, starting transfers between devices, second_across(): lax.ppermute(x, AXES, route(lambda s, c, h: (s + 2 - 4 * c, c, 1 - h)))  1.92 us
    pallas_call x1, Pallas kernels, body(): call(own_kernel, [VMEM] * 7, [((both, width), BF16), total, ((both, 128),...  1.69 us
  transfers between devices with their start and end apart: 7, of which 2 were waited for; matrix products, arithmetic and copies ran while one was open for 0% of the time, Pallas kernels for 10%

profile of v6, /device:TPU:1, one launch (start us, length us, event | category | flops | bytes accessed | tf_op | source)
XLA Modules:
  0.0 50.5 jit_solution(18437949956852366444)
XLA Ops:
  0.6 0.0 copy-start
  0.6 1.6 %shard_map.86 = (bf16[272,768]{1,0:T(8,128)(2,1)S(1)}, bf16[768,768]{1,0:T(8,128)(2,1)S(1)}) custom-call(bf16[128,768]{1,0:T(8,128)(2,1)} %image_ref.1, bf16[128,768]{1,0:T(8,128)(2,1)} %text_ref.1, s32[1,128]{1,0:T(1,128)} %bitcast.1, bf16[768,768]{1,0:T(8,128)(2,1)} %proj_ref.1), custom_call_target="tpu_custom_call" | custom-call | tf_op jit(solution)/shard_map/pallas_call | solution.py:279
  2.3 16.1 %collective-permute-start = (bf16[272,768]{1,0:T(8,128)(2,1)S(1)}, bf16[272,768]{1,0:T(8,128)(2,1)S(1)}, u32[]{:S(2)}, u32[]{:S(2)}) collective-permute-start(bf16[272,768]{1,0:T(8,128)(2,1)S(1)} %get-tuple-element.11.raw_ref), channel_id=1, source_target_pairs={{0,2},{1,3},{2,0},{3,1},{4,6},{5,7},{6,4},{7,5},{8,10},{9,11},{10,... | collective-permute-start | bytes 1253384 | tf_op jit(solution)/shard_map/ppermute | solution.py:256
  19.6 0.1 collective-permute-done.other_ref
  19.7 0.0 copy-done
  19.7 0.6 %shard_map.88 = (bf16[272,768]{1,0:T(8,128)(2,1)S(1)}, bf16[144,768]{1,0:T(8,128)(2,1)S(1)}) custom-call(bf16[272,768]{1,0:T(8,128)(2,1)S(1)} %get-tuple-element.11.raw_ref, bf16[272,768]{1,0:T(8,128)(2,1)S(1)} %collective-permute-done.other_ref, f32[8,128]{1,0:T(8,128)S(1)} %shard_map.87.scalars_ref, bf16[768,768]{1,0:T(8,128)(2,1)S(1)} %copy-done, ...), custom_call_target="tpu_custom_call" | custom-call | tf_op jit(solution)/shard_map/pallas_call | solution.py:290
  20.3 10.4 %collective-permute-start.1 = (bf16[272,768]{1,0:T(8,128)(2,1)S(1)}, bf16[272,768]{1,0:T(8,128)(2,1)S(1)}, u32[]{:S(2)}, u32[]{:S(2)}) collective-permute-start(bf16[272,768]{1,0:T(8,128)(2,1)S(1)} %get-tuple-element.13.sent_ref), channel_id=1, source_target_pairs={{0,5},{1,4},{2,1023},{3,1022},{4,9},{5,8},{6,3},{7,2},{8,13},{9,12... | collective-permute-start | bytes 1253384 | tf_op jit(solution)/shard_map/ppermute | solution.py:262
  30.7 1.9 %collective-permute-start.2 = (bf16[272,768]{1,0:T(8,128)(2,1)S(1)}, bf16[272,768]{1,0:T(8,128)(2,1)S(1)}, u32[]{:S(2)}, u32[]{:S(2)}) collective-permute-start(bf16[272,768]{1,0:T(8,128)(2,1)S(1)} %get-tuple-element.13.sent_ref), channel_id=1, source_target_pairs={{0,1},{1,0},{2,3},{3,2},{4,5},{5,4},{6,7},{7,6},{8,9},{9,8},{10,11... | collective-permute-start | bytes 1253384 | tf_op jit(solution)/shard_map/ppermute | solution.py:259
  32.6 3.3 %collective-permute-start.3 = (bf16[272,768]{1,0:T(8,128)(2,1)S(1)}, bf16[272,768]{1,0:T(8,128)(2,1)S(1)}, u32[]{:S(2)}, u32[]{:S(2)}) collective-permute-start(bf16[272,768]{1,0:T(8,128)(2,1)S(1)} %get-tuple-element.13.sent_ref), channel_id=1, source_target_pairs={{0,4},{1,5},{2,1022},{3,1023},{4,8},{5,9},{6,2},{7,3},{8,12},{9,13... | collective-permute-start | bytes 1253384 | tf_op jit(solution)/shard_map/ppermute | solution.py:265
  35.9 2.4 %collective-permute-start.4 = (bf16[144,768]{1,0:T(8,128)(2,1)S(1)}, bf16[144,768]{1,0:T(8,128)(2,1)S(1)}, u32[]{:S(2)}, u32[]{:S(2)}) collective-permute-start(bf16[144,768]{1,0:T(8,128)(2,1)S(1)} %get-tuple-element.16), channel_id=1, source_target_pairs={{0,8},{1,9},{2,1018},{3,1019},{4,12},{5,13},{6,1022},{7,1023},{8,1... | collective-permute-start | bytes 663560 | tf_op jit(solution)/shard_map/ppermute | solution.py:268
  38.3 1.9 %collective-permute-start.5 = (bf16[144,768]{1,0:T(8,128)(2,1)S(1)}, bf16[144,768]{1,0:T(8,128)(2,1)S(1)}, u32[]{:S(2)}, u32[]{:S(2)}) collective-permute-start(bf16[144,768]{1,0:T(8,128)(2,1)S(1)} %get-tuple-element.16), channel_id=1, source_target_pairs={{0,9},{1,8},{2,1019},{3,1018},{4,13},{5,12},{6,1023},{7,1022},{8,1... | collective-permute-start | bytes 663560 | tf_op jit(solution)/shard_map/ppermute | solution.py:271
  40.2 0.0 collective-permute-done.1.near_ref
  40.2 1.7 %shard_map.89 = (bf16[256,768]{1,0:T(8,128)(2,1)S(1)}, f32[256,768]{1,0:T(8,128)S(1)}, f32[256,128]{1,0:T(8,128)S(1)}, f32[256,128]{1,0:T(8,128)S(1)}, f32[256,768]{1,0:T(8,128)S(1)}) custom-call(bf16[272,768]{1,0:T(8,128)(2,1)S(1)} %get-tuple-element.11.raw_ref, bf16[272,768]{1,0:T(8,128)(2,1)S(1)} %collective-permute-done.other_ref, ...), custom_call_target="tpu_custom_call" | custom-call | tf_op jit(solution)/shard_map/pallas_call | solution.py:305
  41.9 2.4 %collective-permute-done.2.refs_0_ = bf16[272,768]{1,0:T(8,128)(2,1)S(1)} collective-permute-done((bf16[272,768]{1,0:T(8,128)(2,1)S(1)}, bf16[272,768]{1,0:T(8,128)(2,1)S(1)}, u32[]{:S(2)}, u32[]{:S(2)}) %collective-permute-start.2) | collective-permute-done | bytes 417824 | tf_op jit(solution)/shard_map/ppermute | solution.py:259
  44.3 0.0 collective-permute-done.3.refs_1_
  44.3 1.6 %shard_map.91 = bf16[128,768]{1,0:T(8,128)(2,1)S(1)} custom-call(bf16[256,768]{1,0:T(8,128)(2,1)S(1)} %get-tuple-element.14.emb_ref, f32[256,128]{1,0:T(8,128)S(1)} %get-tuple-element.15.key_ref, bf16[272,768]{1,0:T(8,128)(2,1)S(1)} %collective-permute-done.2.refs_0_, bf16[272,768]{1,0:T(8,128)(2,1)S(1)} %collective-permute-done.3.refs_1_, ...), custom_call_target="tpu_custom_call" | custom-call | tf_op jit(solution)/shard_map/pallas_call | solution.py:310
  45.9 2.2 %collective-permute-start.6 = (bf16[128,768]{1,0:T(8,128)(2,1)S(1)}, bf16[128,768]{1,0:T(8,128)(2,1)S(1)}, u32[]{:S(2)}, u32[]{:S(2)}) collective-permute-start(bf16[128,768]{1,0:T(8,128)(2,1)S(1)} %shard_map.91), channel_id=1, source_target_pairs={{0,2},{1,3},{2,0},{3,1},{4,6},{5,7},{6,4},{7,5},{8,10},{9,11},{10,... | collective-permute-start | bytes 589832 | tf_op jit(solution)/shard_map/ppermute | solution.py:256
  48.1 0.0 collective-permute-done.4.refs_2_
  48.1 0.0 collective-permute-done.5.refs_3_
  48.1 1.6 %shard_map.90.own_ref = bf16[128,768]{1,0:T(8,128)(2,1)S(1)} custom-call(bf16[256,768]{1,0:T(8,128)(2,1)S(1)} %get-tuple-element.14.emb_ref, f32[256,128]{1,0:T(8,128)S(1)} %get-tuple-element.15.key_ref, bf16[272,768]{1,0:T(8,128)(2,1)S(1)} %collective-permute-done.2.refs_0_, bf16[272,768]{1,0:T(8,128)(2,1)S(1)} %collective-permute-done.3.refs_1_, ...), custom_call_target="tpu_custom_call" | custom-call | tf_op jit(solution)/shard_map/pallas_call | solution.py:314
  49.8 0.0 collective-permute-done.6.given_ref
  49.8 0.8 %shard_map.92 = (bf16[128,768]{1,0:T(8,128)(2,1)}, bf16[128,768]{1,0:T(8,128)(2,1)}) custom-call(bf16[128,768]{1,0:T(8,128)(2,1)S(1)} %shard_map.90.own_ref, bf16[128,768]{1,0:T(8,128)(2,1)S(1)} %collective-permute-done.6.given_ref), custom_call_target="tpu_custom_call" | custom-call | tf_op jit(solution)/shard_map/pallas_call | solution.py:317
  (1 shorter events, 0.0 us)
Async XLA Ops:
  0.6 19.1 %copy-start = (bf16[768,768]{1,0:T(8,128)(2,1)S(1)}, bf16[768,768]{1,0:T(8,128)(2,1)}, u32[]{:S(2)}) copy-start(bf16[768,768]{1,0:T(8,128)(2,1)} %refs_5_.1) | copy-start | bytes 3538948
  2.3 17.4 %collective-permute-start = (bf16[272,768]{1,0:T(8,128)(2,1)S(1)}, bf16[272,768]{1,0:T(8,128)(2,1)S(1)}, u32[]{:S(2)}, u32[]{:S(2)}) collective-permute-start(bf16[272,768]{1,0:T(8,128)(2,1)S(1)} %get-tuple-element.11.raw_ref), channel_id=1, source_target_pairs={{0,2},{1,3},{2,0},{3,1},{4,6},{5,7},{6,4},{7,5},{8,10},{9,11},{10,... | collective-permute-start | bytes 1253384 | tf_op jit(solution)/shard_map/ppermute | solution.py:256
  20.3 19.9 %collective-permute-start.1 = (bf16[272,768]{1,0:T(8,128)(2,1)S(1)}, bf16[272,768]{1,0:T(8,128)(2,1)S(1)}, u32[]{:S(2)}, u32[]{:S(2)}) collective-permute-start(bf16[272,768]{1,0:T(8,128)(2,1)S(1)} %get-tuple-element.13.sent_ref), channel_id=1, source_target_pairs={{0,5},{1,4},{2,1023},{3,1022},{4,9},{5,8},{6,3},{7,2},{8,13},{9,12... | collective-permute-start | bytes 1253384 | tf_op jit(solution)/shard_map/ppermute | solution.py:262
  30.7 13.6 %collective-permute-start.2 = (bf16[272,768]{1,0:T(8,128)(2,1)S(1)}, bf16[272,768]{1,0:T(8,128)(2,1)S(1)}, u32[]{:S(2)}, u32[]{:S(2)}) collective-permute-start(bf16[272,768]{1,0:T(8,128)(2,1)S(1)} %get-tuple-element.13.sent_ref), channel_id=1, source_target_pairs={{0,1},{1,0},{2,3},{3,2},{4,5},{5,4},{6,7},{7,6},{8,9},{9,8},{10,11... | collective-permute-start | bytes 1253384 | tf_op jit(solution)/shard_map/ppermute | solution.py:259
  32.6 11.7 %collective-permute-start.3 = (bf16[272,768]{1,0:T(8,128)(2,1)S(1)}, bf16[272,768]{1,0:T(8,128)(2,1)S(1)}, u32[]{:S(2)}, u32[]{:S(2)}) collective-permute-start(bf16[272,768]{1,0:T(8,128)(2,1)S(1)} %get-tuple-element.13.sent_ref), channel_id=1, source_target_pairs={{0,4},{1,5},{2,1022},{3,1023},{4,8},{5,9},{6,2},{7,3},{8,12},{9,13... | collective-permute-start | bytes 1253384 | tf_op jit(solution)/shard_map/ppermute | solution.py:265
  35.9 12.2 %collective-permute-start.4 = (bf16[144,768]{1,0:T(8,128)(2,1)S(1)}, bf16[144,768]{1,0:T(8,128)(2,1)S(1)}, u32[]{:S(2)}, u32[]{:S(2)}) collective-permute-start(bf16[144,768]{1,0:T(8,128)(2,1)S(1)} %get-tuple-element.16), channel_id=1, source_target_pairs={{0,8},{1,9},{2,1018},{3,1019},{4,12},{5,13},{6,1022},{7,1023},{8,1... | collective-permute-start | bytes 663560 | tf_op jit(solution)/shard_map/ppermute | solution.py:268
  38.3 9.8 %collective-permute-start.5 = (bf16[144,768]{1,0:T(8,128)(2,1)S(1)}, bf16[144,768]{1,0:T(8,128)(2,1)S(1)}, u32[]{:S(2)}, u32[]{:S(2)}) collective-permute-start(bf16[144,768]{1,0:T(8,128)(2,1)S(1)} %get-tuple-element.16), channel_id=1, source_target_pairs={{0,9},{1,8},{2,1019},{3,1018},{4,13},{5,12},{6,1023},{7,1022},{8,1... | collective-permute-start | bytes 663560 | tf_op jit(solution)/shard_map/ppermute | solution.py:271
  45.9 3.9 %collective-permute-start.6 = (bf16[128,768]{1,0:T(8,128)(2,1)S(1)}, bf16[128,768]{1,0:T(8,128)(2,1)S(1)}, u32[]{:S(2)}, u32[]{:S(2)}) collective-permute-start(bf16[128,768]{1,0:T(8,128)(2,1)S(1)} %shard_map.91), channel_id=1, source_target_pairs={{0,2},{1,3},{2,0},{3,1},{4,6},{5,7},{6,4},{7,5},{8,10},{9,11},{10,... | collective-permute-start | bytes 589832 | tf_op jit(solution)/shard_map/ppermute | solution.py:256

commit v7 on v5

--- a/solution.py
+++ b/solution.py
@@ -122,6 +122,7 @@
     raw_ref,
     other_ref,
     sent_ref,
+    near_ref,
     proj_ref,
     scale_ref,
     bias_ref,
@@ -145,7 +146,8 @@
         tile = jnp.where(core == 0, ref[both:, :rows], text_key_tile(block ^ n, half, rows))
         scalars = jnp.where(lane == 1, scale_ref[0], bias_ref[0])
         key_ref[at] = jnp.where(lane == 0, as_column(joined_key(tile)), scalars)
-    own_pairs(emb_ref, key_ref, sent_ref, grad_ref, False)
+    grad_ref[...] = all_pairs(emb_ref, key_ref, near_ref)
+    own_pairs(emb_ref, key_ref, sent_ref, grad_ref, True)
 
 
 def own_pairs(emb_ref, key_ref, cols_ref, grad_ref, add):
@@ -169,20 +171,15 @@
     pass
 
 
-def near_kernel(emb_ref, key_ref, one_ref, two_ref, grad_ref, out_ref):
-    out_ref[...] = grad_ref[...] + all_pairs(emb_ref, key_ref, one_ref)
-    own_pairs(emb_ref, key_ref, two_ref, out_ref, True)
-
-
 def back_kernel(part, emb_ref, key_ref, *refs):
     *cols_refs, grad_ref, unit_ref, inv_ref, proj_ref, out_ref = refs
     rows = out_ref.shape[0]
     both = 2 * rows
     at = slice(part * rows, (part + 1) * rows)
     grad = grad_ref[at]
-    for ref in cols_refs:
+    for place_in, ref in enumerate(cols_refs):
         start = max(0, both + KEY_ROWS - ref.shape[0])
-        n = both - start
+        n = rows if place_in + part == 0 else both - start
         grad += pair_grad(emb_ref[at], key_ref[at], ref[:n], ref[both - start :, start : start + n])
     unit = unit_ref[at]
     inner = jnp.sum(grad * unit, axis=-1, keepdims=True)
@@ -298,16 +295,15 @@
     total = ((both, width), F32)
     emb, unit, inv, key, grad = call(
         own_kernel,
-        [VMEM] * 4 + [SMEM] * 2,
+        [VMEM] * 5 + [SMEM] * 2,
         [((both, width), BF16), total, ((both, 128), F32), ((both, 128), F32), total],
-    )(raw, other, sent, row_proj, logit_scale, logit_bias)
-    (grad,) = call(near_kernel, [VMEM] * 5, [total])(emb, key, near_one, swapped, grad)
-    (other_out,) = call(functools.partial(back_kernel, 1), [VMEM] * 7, [block_rows])(
-        emb, key, near_two, grad, unit, inv, row_proj
+    )(raw, other, sent, near_one, row_proj, logit_scale, logit_bias)
+    (other_out,) = call(functools.partial(back_kernel, 1), [VMEM] * 8, [block_rows])(
+        emb, key, swapped, near_two, grad, unit, inv, row_proj
     )
     given = flip(other_out)
-    (own_out,) = call(functools.partial(back_kernel, 0), [VMEM] * 9, [block_rows])(
-        emb, key, near_two, third, fourth, grad, unit, inv, row_proj
+    (own_out,) = call(functools.partial(back_kernel, 0), [VMEM] * 10, [block_rows])(
+        emb, key, swapped, near_two, third, fourth, grad, unit, inv, row_proj
     )
     return call(choose_kernel, [VMEM] * 2, [block_rows] * 2, HBM, [semaphores((2,))])(
         own_out, given

time: 50.9 us -> 50.4 us (level)
    pallas_call x4 -> x3, Pallas kernels: 4.9 us -> 4.84 us  [the longest x1 1.66 us: body(): call(functools.partial(back_kernel, 0), [VMEM] * 10, [block_rows])]
where the time goes in v7:
time: 50.4 us; the launch traced here: 50.1 us
  starting transfers between devices  37.9 us (75%)
  Pallas kernels  8.91 us (18%)
  between operations  2.06 us (4%)
  waiting for transfers between devices  1.21 us (2%)
    ppermute x2, starting transfers between devices, flip(): return lax.ppermute(x, AXES, route(lambda s, c, h: (s, 1 - c, h)))  18 us
    ppermute x1, starting transfers between devices, near(): lax.ppermute(x, AXES, route(lambda s, c, h: (s + 1 - 2 * c, c, 1 - h)))  10.4 us
    ppermute x1, starting transfers between devices, across(): return lax.ppermute(x, AXES, route(lambda s, c, h: (s + 1 - 2 * c, c, h)))  3.28 us
    ppermute x1, starting transfers between devices, second_next(): return lax.ppermute(x, AXES, route(lambda s, c, h: (s + 2 - 4 * c, c, h)))  2.37 us
    ppermute x1, starting transfers between devices, swap(): return lax.ppermute(x, AXES, route(lambda s, c, h: (s, c, 1 - h)))  1.92 us
    ppermute x1, starting transfers between devices, second_across(): lax.ppermute(x, AXES, route(lambda s, c, h: (s + 2 - 4 * c, c, 1 - h)))  1.92 us
    pallas_call x1, Pallas kernels, body(): call(load_kernel, [ANY] + [HBM] * 2, [square] * 2, scratch=[semaphores((2...  1.66 us
    pallas_call x1, Pallas kernels, body(): call(functools.partial(back_kernel, 0), [VMEM] * 10, [block_rows])  1.66 us
  transfers between devices with their start and end apart: 7, of which 1 were waited for; matrix products, arithmetic and copies ran while one was open for 0% of the time, Pallas kernels for 13%

profile of v7, /device:TPU:1, one launch (start us, length us, event | category | flops | bytes accessed | tf_op | source)
XLA Modules:
  0.0 50.1 jit_solution(6416096136353434460)
XLA Ops:
  0.6 1.1 %shard_map.86.raw_ref = bf16[272,768]{1,0:T(8,128)(2,1)S(1)} custom-call(bf16[128,768]{1,0:T(8,128)(2,1)} %image_ref.1, bf16[128,768]{1,0:T(8,128)(2,1)} %text_ref.1, s32[1,128]{1,0:T(1,128)} %bitcast.1), custom_call_target="tpu_custom_call" | custom-call | tf_op jit(solution)/shard_map/pallas_call | solution.py:271
  1.7 16.1 %collective-permute-start = (bf16[272,768]{1,0:T(8,128)(2,1)S(1)}, bf16[272,768]{1,0:T(8,128)(2,1)S(1)}, u32[]{:S(2)}, u32[]{:S(2)}) collective-permute-start(bf16[272,768]{1,0:T(8,128)(2,1)S(1)} %shard_map.86.raw_ref), channel_id=1, source_target_pairs={{0,2},{1,3},{2,0},{3,1},{4,6},{5,7},{6,4},{7,5},{8,10},{9,11},{10,... | collective-permute-start | bytes 1253384 | tf_op jit(solution)/shard_map/ppermute | solution.py:248
  17.8 1.7 %shard_map.87 = (bf16[768,768]{1,0:T(8,128)(2,1)S(1)}, bf16[768,768]{1,0:T(8,128)(2,1)S(1)}) custom-call(bf16[272,768]{1,0:T(8,128)(2,1)S(1)} %shard_map.86.raw_ref, bf16[768,768]{1,0:T(8,128)(2,1)} %image_proj_ref.1, bf16[768,768]{1,0:T(8,128)(2,1)} %text_proj_ref.1), custom_call_target="tpu_custom_call" | custom-call | tf_op jit(solution)/shard_map/pallas_call | solution.py:279
  19.4 0.0 collective-permute-done.other_ref
  19.5 0.6 %shard_map.88 = (bf16[272,768]{1,0:T(8,128)(2,1)S(1)}, bf16[144,768]{1,0:T(8,128)(2,1)S(1)}) custom-call(bf16[272,768]{1,0:T(8,128)(2,1)S(1)} %shard_map.86.raw_ref, bf16[272,768]{1,0:T(8,128)(2,1)S(1)} %collective-permute-done.other_ref, bf16[768,768]{1,0:T(8,128)(2,1)S(1)} %get-tuple-element.11.proj_ref), custom_call_target="tpu_custom_call" | custom-call | tf_op jit(solution)/shard_map/pallas_call | solution.py:283
  20.0 10.4 %collective-permute-start.1 = (bf16[272,768]{1,0:T(8,128)(2,1)S(1)}, bf16[272,768]{1,0:T(8,128)(2,1)S(1)}, u32[]{:S(2)}, u32[]{:S(2)}) collective-permute-start(bf16[272,768]{1,0:T(8,128)(2,1)S(1)} %get-tuple-element.12.sent_ref), channel_id=1, source_target_pairs={{0,5},{1,4},{2,1023},{3,1022},{4,9},{5,8},{6,3},{7,2},{8,13},{9,12... | collective-permute-start | bytes 1253384 | tf_op jit(solution)/shard_map/ppermute | solution.py:254
  30.4 1.9 %collective-permute-start.2 = (bf16[272,768]{1,0:T(8,128)(2,1)S(1)}, bf16[272,768]{1,0:T(8,128)(2,1)S(1)}, u32[]{:S(2)}, u32[]{:S(2)}) collective-permute-start(bf16[272,768]{1,0:T(8,128)(2,1)S(1)} %get-tuple-element.12.sent_ref), channel_id=1, source_target_pairs={{0,1},{1,0},{2,3},{3,2},{4,5},{5,4},{6,7},{7,6},{8,9},{9,8},{10,11... | collective-permute-start | bytes 1253384 | tf_op jit(solution)/shard_map/ppermute | solution.py:251
  32.4 3.3 %collective-permute-start.3 = (bf16[272,768]{1,0:T(8,128)(2,1)S(1)}, bf16[272,768]{1,0:T(8,128)(2,1)S(1)}, u32[]{:S(2)}, u32[]{:S(2)}) collective-permute-start(bf16[272,768]{1,0:T(8,128)(2,1)S(1)} %get-tuple-element.12.sent_ref), channel_id=1, source_target_pairs={{0,4},{1,5},{2,1022},{3,1023},{4,8},{5,9},{6,2},{7,3},{8,12},{9,13... | collective-permute-start | bytes 1253384 | tf_op jit(solution)/shard_map/ppermute | solution.py:257
  35.6 2.4 %collective-permute-start.4 = (bf16[144,768]{1,0:T(8,128)(2,1)S(1)}, bf16[144,768]{1,0:T(8,128)(2,1)S(1)}, u32[]{:S(2)}, u32[]{:S(2)}) collective-permute-start(bf16[144,768]{1,0:T(8,128)(2,1)S(1)} %get-tuple-element.16), channel_id=1, source_target_pairs={{0,8},{1,9},{2,1018},{3,1019},{4,12},{5,13},{6,1022},{7,1023},{8,1... | collective-permute-start | bytes 663560 | tf_op jit(solution)/shard_map/ppermute | solution.py:260
  38.0 1.9 %collective-permute-start.5 = (bf16[144,768]{1,0:T(8,128)(2,1)S(1)}, bf16[144,768]{1,0:T(8,128)(2,1)S(1)}, u32[]{:S(2)}, u32[]{:S(2)}) collective-permute-start(bf16[144,768]{1,0:T(8,128)(2,1)S(1)} %get-tuple-element.16), channel_id=1, source_target_pairs={{0,9},{1,8},{2,1019},{3,1018},{4,13},{5,12},{6,1023},{7,1022},{8,1... | collective-permute-start | bytes 663560 | tf_op jit(solution)/shard_map/ppermute | solution.py:263
  41.2 0.0 collective-permute-done.1.near_ref
  41.3 1.6 %shard_map.89 = (bf16[256,768]{1,0:T(8,128)(2,1)S(1)}, f32[256,768]{1,0:T(8,128)S(1)}, f32[256,128]{1,0:T(8,128)S(1)}, f32[256,128]{1,0:T(8,128)S(1)}, f32[256,768]{1,0:T(8,128)S(1)}) custom-call(bf16[272,768]{1,0:T(8,128)(2,1)S(1)} %shard_map.86.raw_ref, bf16[272,768]{1,0:T(8,128)(2,1)S(1)} %collective-permute-done.other_ref, ...), custom_call_target="tpu_custom_call" | custom-call | tf_op jit(solution)/shard_map/pallas_call | solution.py:296
  42.9 1.2 %collective-permute-done.2.refs_0_ = bf16[272,768]{1,0:T(8,128)(2,1)S(1)} collective-permute-done((bf16[272,768]{1,0:T(8,128)(2,1)S(1)}, bf16[272,768]{1,0:T(8,128)(2,1)S(1)}, u32[]{:S(2)}, u32[]{:S(2)}) %collective-permute-start.2) | collective-permute-done | bytes 417824 | tf_op jit(solution)/shard_map/ppermute | solution.py:251
  44.1 0.0 collective-permute-done.3.refs_1_
  44.1 1.6 %shard_map.91 = bf16[128,768]{1,0:T(8,128)(2,1)S(1)} custom-call(bf16[256,768]{1,0:T(8,128)(2,1)S(1)} %get-tuple-element.14.emb_ref, f32[256,128]{1,0:T(8,128)S(1)} %get-tuple-element.15.key_ref, bf16[272,768]{1,0:T(8,128)(2,1)S(1)} %collective-permute-done.2.refs_0_, bf16[272,768]{1,0:T(8,128)(2,1)S(1)} %collective-permute-done.3.refs_1_, ...), custom_call_target="tpu_custom_call" | custom-call | tf_op jit(solution)/shard_map/pallas_call | solution.py:301
  45.6 1.9 %collective-permute-start.6 = (bf16[128,768]{1,0:T(8,128)(2,1)S(1)}, bf16[128,768]{1,0:T(8,128)(2,1)S(1)}, u32[]{:S(2)}, u32[]{:S(2)}) collective-permute-start(bf16[128,768]{1,0:T(8,128)(2,1)S(1)} %shard_map.91), channel_id=1, source_target_pairs={{0,2},{1,3},{2,0},{3,1},{4,6},{5,7},{6,4},{7,5},{8,10},{9,11},{10,... | collective-permute-start | bytes 589832 | tf_op jit(solution)/shard_map/ppermute | solution.py:248
  47.6 0.0 collective-permute-done.4.refs_2_
  47.6 0.0 collective-permute-done.5.refs_3_
  47.6 1.7 %shard_map.90.own_ref = bf16[128,768]{1,0:T(8,128)(2,1)S(1)} custom-call(bf16[256,768]{1,0:T(8,128)(2,1)S(1)} %get-tuple-element.14.emb_ref, f32[256,128]{1,0:T(8,128)S(1)} %get-tuple-element.15.key_ref, bf16[272,768]{1,0:T(8,128)(2,1)S(1)} %collective-permute-done.2.refs_0_, bf16[272,768]{1,0:T(8,128)(2,1)S(1)} %collective-permute-done.3.refs_1_, ...), custom_call_target="tpu_custom_call" | custom-call | tf_op jit(solution)/shard_map/pallas_call | solution.py:305
  49.3 0.0 collective-permute-done.6.given_ref
  49.3 0.8 %shard_map.92 = (bf16[128,768]{1,0:T(8,128)(2,1)}, bf16[128,768]{1,0:T(8,128)(2,1)}) custom-call(bf16[128,768]{1,0:T(8,128)(2,1)S(1)} %shard_map.90.own_ref, bf16[128,768]{1,0:T(8,128)(2,1)S(1)} %collective-permute-done.6.given_ref), custom_call_target="tpu_custom_call" | custom-call | tf_op jit(solution)/shard_map/pallas_call | solution.py:308
Async XLA Ops:
  1.7 17.7 %collective-permute-start = (bf16[272,768]{1,0:T(8,128)(2,1)S(1)}, bf16[272,768]{1,0:T(8,128)(2,1)S(1)}, u32[]{:S(2)}, u32[]{:S(2)}) collective-permute-start(bf16[272,768]{1,0:T(8,128)(2,1)S(1)} %shard_map.86.raw_ref), channel_id=1, source_target_pairs={{0,2},{1,3},{2,0},{3,1},{4,6},{5,7},{6,4},{7,5},{8,10},{9,11},{10,... | collective-permute-start | bytes 1253384 | tf_op jit(solution)/shard_map/ppermute | solution.py:248
  20.0 21.2 %collective-permute-start.1 = (bf16[272,768]{1,0:T(8,128)(2,1)S(1)}, bf16[272,768]{1,0:T(8,128)(2,1)S(1)}, u32[]{:S(2)}, u32[]{:S(2)}) collective-permute-start(bf16[272,768]{1,0:T(8,128)(2,1)S(1)} %get-tuple-element.12.sent_ref), channel_id=1, source_target_pairs={{0,5},{1,4},{2,1023},{3,1022},{4,9},{5,8},{6,3},{7,2},{8,13},{9,12... | collective-permute-start | bytes 1253384 | tf_op jit(solution)/shard_map/ppermute | solution.py:254
  30.4 13.6 %collective-permute-start.2 = (bf16[272,768]{1,0:T(8,128)(2,1)S(1)}, bf16[272,768]{1,0:T(8,128)(2,1)S(1)}, u32[]{:S(2)}, u32[]{:S(2)}) collective-permute-start(bf16[272,768]{1,0:T(8,128)(2,1)S(1)} %get-tuple-element.12.sent_ref), channel_id=1, source_target_pairs={{0,1},{1,0},{2,3},{3,2},{4,5},{5,4},{6,7},{7,6},{8,9},{9,8},{10,11... | collective-permute-start | bytes 1253384 | tf_op jit(solution)/shard_map/ppermute | solution.py:251
  32.4 11.7 %collective-permute-start.3 = (bf16[272,768]{1,0:T(8,128)(2,1)S(1)}, bf16[272,768]{1,0:T(8,128)(2,1)S(1)}, u32[]{:S(2)}, u32[]{:S(2)}) collective-permute-start(bf16[272,768]{1,0:T(8,128)(2,1)S(1)} %get-tuple-element.12.sent_ref), channel_id=1, source_target_pairs={{0,4},{1,5},{2,1022},{3,1023},{4,8},{5,9},{6,2},{7,3},{8,12},{9,13... | collective-permute-start | bytes 1253384 | tf_op jit(solution)/shard_map/ppermute | solution.py:257
  35.6 11.9 %collective-permute-start.4 = (bf16[144,768]{1,0:T(8,128)(2,1)S(1)}, bf16[144,768]{1,0:T(8,128)(2,1)S(1)}, u32[]{:S(2)}, u32[]{:S(2)}) collective-permute-start(bf16[144,768]{1,0:T(8,128)(2,1)S(1)} %get-tuple-element.16), channel_id=1, source_target_pairs={{0,8},{1,9},{2,1018},{3,1019},{4,12},{5,13},{6,1022},{7,1023},{8,1... | collective-permute-start | bytes 663560 | tf_op jit(solution)/shard_map/ppermute | solution.py:260
  38.0 9.6 %collective-permute-start.5 = (bf16[144,768]{1,0:T(8,128)(2,1)S(1)}, bf16[144,768]{1,0:T(8,128)(2,1)S(1)}, u32[]{:S(2)}, u32[]{:S(2)}) collective-permute-start(bf16[144,768]{1,0:T(8,128)(2,1)S(1)} %get-tuple-element.16), channel_id=1, source_target_pairs={{0,9},{1,8},{2,1019},{3,1018},{4,13},{5,12},{6,1023},{7,1022},{8,1... | collective-permute-start | bytes 663560 | tf_op jit(solution)/shard_map/ppermute | solution.py:263
  45.6 3.6 %collective-permute-start.6 = (bf16[128,768]{1,0:T(8,128)(2,1)S(1)}, bf16[128,768]{1,0:T(8,128)(2,1)S(1)}, u32[]{:S(2)}, u32[]{:S(2)}) collective-permute-start(bf16[128,768]{1,0:T(8,128)(2,1)S(1)} %shard_map.91), channel_id=1, source_target_pairs={{0,2},{1,3},{2,0},{3,1},{4,6},{5,7},{6,4},{7,5},{8,10},{9,11},{10,... | collective-permute-start | bytes 589832 | tf_op jit(solution)/shard_map/ppermute | solution.py:248

commit v8 on v7

--- a/solution.py
+++ b/solution.py
@@ -113,8 +113,9 @@
 def pair_grad(row_emb, row_key, col_emb, col_tile):
     scale, bias = row_key[:, 1:2], row_key[:, 2:3]
     logits = scale * rows_dot(row_emb, col_emb) + bias
-    sign = jnp.where(row_key[:, :1] == joined_key(col_tile), F32(1.0), F32(-1.0))
-    coef = (-sign * scale / (1.0 + jnp.exp(sign * logits))).astype(BF16)
+    paired = row_key[:, :1] == joined_key(col_tile)
+    top = jnp.where(paired, -scale, scale)
+    coef = (top / (1.0 + jnp.exp(jnp.where(paired, logits, -logits)))).astype(BF16)
     return jnp.dot(coef, col_emb, preferred_element_type=F32)
 
 

time: 50.4 us -> 50.4 us (level)
  no operation moved by 1% of the time
where the time goes in v8:
time: 50.4 us; the launch traced here: 50.1 us
  starting transfers between devices  37.9 us (75%)
  Pallas kernels  8.99 us (18%)
  between operations  2.06 us (4%)
  waiting for transfers between devices  1.14 us (2%)
    ppermute x2, starting transfers between devices, flip(): return lax.ppermute(x, AXES, route(lambda s, c, h: (s, 1 - c, h)))  18 us
    ppermute x1, starting transfers between devices, near(): lax.ppermute(x, AXES, route(lambda s, c, h: (s + 1 - 2 * c, c, 1 - h)))  10.4 us
    ppermute x1, starting transfers between devices, across(): return lax.ppermute(x, AXES, route(lambda s, c, h: (s + 1 - 2 * c, c, h)))  3.28 us
    ppermute x1, starting transfers between devices, second_next(): return lax.ppermute(x, AXES, route(lambda s, c, h: (s + 2 - 4 * c, c, h)))  2.37 us
    ppermute x1, starting transfers between devices, second_across(): lax.ppermute(x, AXES, route(lambda s, c, h: (s + 2 - 4 * c, c, 1 - h)))  1.92 us
    ppermute x1, starting transfers between devices, swap(): return lax.ppermute(x, AXES, route(lambda s, c, h: (s, c, 1 - h)))  1.92 us
    pallas_call x1, Pallas kernels, body(): call(own_kernel, [VMEM] * 5 + [SMEM] * 2, [((both, width), BF16), total,...  1.67 us
    pallas_call x1, Pallas kernels, body(): call(load_kernel, [ANY] + [HBM] * 2, [square] * 2, scratch=[semaphores((2...  1.66 us
  transfers between devices with their start and end apart: 7, of which 1 were waited for; matrix products, arithmetic and copies ran while one was open for 0% of the time, Pallas kernels for 13%

profile of v8, /device:TPU:1, one launch (start us, length us, event | category | flops | bytes accessed | tf_op | source)
XLA Modules:
  0.0 50.1 jit_solution(4418131987221040409)
XLA Ops:
  0.6 1.1 %shard_map.86.raw_ref = bf16[272,768]{1,0:T(8,128)(2,1)S(1)} custom-call(bf16[128,768]{1,0:T(8,128)(2,1)} %image_ref.1, bf16[128,768]{1,0:T(8,128)(2,1)} %text_ref.1, s32[1,128]{1,0:T(1,128)} %bitcast.1), custom_call_target="tpu_custom_call" | custom-call | tf_op jit(solution)/shard_map/pallas_call | solution.py:272
  1.7 16.1 %collective-permute-start = (bf16[272,768]{1,0:T(8,128)(2,1)S(1)}, bf16[272,768]{1,0:T(8,128)(2,1)S(1)}, u32[]{:S(2)}, u32[]{:S(2)}) collective-permute-start(bf16[272,768]{1,0:T(8,128)(2,1)S(1)} %shard_map.86.raw_ref), channel_id=1, source_target_pairs={{0,2},{1,3},{2,0},{3,1},{4,6},{5,7},{6,4},{7,5},{8,10},{9,11},{10,... | collective-permute-start | bytes 1253384 | tf_op jit(solution)/shard_map/ppermute | solution.py:249
  17.8 1.7 %shard_map.87 = (bf16[768,768]{1,0:T(8,128)(2,1)S(1)}, bf16[768,768]{1,0:T(8,128)(2,1)S(1)}) custom-call(bf16[272,768]{1,0:T(8,128)(2,1)S(1)} %shard_map.86.raw_ref, bf16[768,768]{1,0:T(8,128)(2,1)} %image_proj_ref.1, bf16[768,768]{1,0:T(8,128)(2,1)} %text_proj_ref.1), custom_call_target="tpu_custom_call" | custom-call | tf_op jit(solution)/shard_map/pallas_call | solution.py:280
  19.4 0.0 collective-permute-done.other_ref
  19.5 0.6 %shard_map.88 = (bf16[272,768]{1,0:T(8,128)(2,1)S(1)}, bf16[144,768]{1,0:T(8,128)(2,1)S(1)}) custom-call(bf16[272,768]{1,0:T(8,128)(2,1)S(1)} %shard_map.86.raw_ref, bf16[272,768]{1,0:T(8,128)(2,1)S(1)} %collective-permute-done.other_ref, bf16[768,768]{1,0:T(8,128)(2,1)S(1)} %get-tuple-element.11.proj_ref), custom_call_target="tpu_custom_call" | custom-call | tf_op jit(solution)/shard_map/pallas_call | solution.py:284
  20.0 10.4 %collective-permute-start.1 = (bf16[272,768]{1,0:T(8,128)(2,1)S(1)}, bf16[272,768]{1,0:T(8,128)(2,1)S(1)}, u32[]{:S(2)}, u32[]{:S(2)}) collective-permute-start(bf16[272,768]{1,0:T(8,128)(2,1)S(1)} %get-tuple-element.12.sent_ref), channel_id=1, source_target_pairs={{0,5},{1,4},{2,1023},{3,1022},{4,9},{5,8},{6,3},{7,2},{8,13},{9,12... | collective-permute-start | bytes 1253384 | tf_op jit(solution)/shard_map/ppermute | solution.py:255
  30.4 1.9 %collective-permute-start.2 = (bf16[272,768]{1,0:T(8,128)(2,1)S(1)}, bf16[272,768]{1,0:T(8,128)(2,1)S(1)}, u32[]{:S(2)}, u32[]{:S(2)}) collective-permute-start(bf16[272,768]{1,0:T(8,128)(2,1)S(1)} %get-tuple-element.12.sent_ref), channel_id=1, source_target_pairs={{0,1},{1,0},{2,3},{3,2},{4,5},{5,4},{6,7},{7,6},{8,9},{9,8},{10,11... | collective-permute-start | bytes 1253384 | tf_op jit(solution)/shard_map/ppermute | solution.py:252
  32.4 3.3 %collective-permute-start.3 = (bf16[272,768]{1,0:T(8,128)(2,1)S(1)}, bf16[272,768]{1,0:T(8,128)(2,1)S(1)}, u32[]{:S(2)}, u32[]{:S(2)}) collective-permute-start(bf16[272,768]{1,0:T(8,128)(2,1)S(1)} %get-tuple-element.12.sent_ref), channel_id=1, source_target_pairs={{0,4},{1,5},{2,1022},{3,1023},{4,8},{5,9},{6,2},{7,3},{8,12},{9,13... | collective-permute-start | bytes 1253384 | tf_op jit(solution)/shard_map/ppermute | solution.py:258
  35.6 2.4 %collective-permute-start.4 = (bf16[144,768]{1,0:T(8,128)(2,1)S(1)}, bf16[144,768]{1,0:T(8,128)(2,1)S(1)}, u32[]{:S(2)}, u32[]{:S(2)}) collective-permute-start(bf16[144,768]{1,0:T(8,128)(2,1)S(1)} %get-tuple-element.16), channel_id=1, source_target_pairs={{0,8},{1,9},{2,1018},{3,1019},{4,12},{5,13},{6,1022},{7,1023},{8,1... | collective-permute-start | bytes 663560 | tf_op jit(solution)/shard_map/ppermute | solution.py:261
  38.0 1.9 %collective-permute-start.5 = (bf16[144,768]{1,0:T(8,128)(2,1)S(1)}, bf16[144,768]{1,0:T(8,128)(2,1)S(1)}, u32[]{:S(2)}, u32[]{:S(2)}) collective-permute-start(bf16[144,768]{1,0:T(8,128)(2,1)S(1)} %get-tuple-element.16), channel_id=1, source_target_pairs={{0,9},{1,8},{2,1019},{3,1018},{4,13},{5,12},{6,1023},{7,1022},{8,1... | collective-permute-start | bytes 663560 | tf_op jit(solution)/shard_map/ppermute | solution.py:264
  41.2 0.0 collective-permute-done.1.near_ref
  41.3 1.7 %shard_map.89 = (bf16[256,768]{1,0:T(8,128)(2,1)S(1)}, f32[256,768]{1,0:T(8,128)S(1)}, f32[256,128]{1,0:T(8,128)S(1)}, f32[256,128]{1,0:T(8,128)S(1)}, f32[256,768]{1,0:T(8,128)S(1)}) custom-call(bf16[272,768]{1,0:T(8,128)(2,1)S(1)} %shard_map.86.raw_ref, bf16[272,768]{1,0:T(8,128)(2,1)S(1)} %collective-permute-done.other_ref, ...), custom_call_target="tpu_custom_call" | custom-call | tf_op jit(solution)/shard_map/pallas_call | solution.py:297
  42.9 1.1 %collective-permute-done.2.refs_0_ = bf16[272,768]{1,0:T(8,128)(2,1)S(1)} collective-permute-done((bf16[272,768]{1,0:T(8,128)(2,1)S(1)}, bf16[272,768]{1,0:T(8,128)(2,1)S(1)}, u32[]{:S(2)}, u32[]{:S(2)}) %collective-permute-start.2) | collective-permute-done | bytes 417824 | tf_op jit(solution)/shard_map/ppermute | solution.py:252
  44.1 0.0 collective-permute-done.3.refs_1_
  44.1 1.6 %shard_map.91 = bf16[128,768]{1,0:T(8,128)(2,1)S(1)} custom-call(bf16[256,768]{1,0:T(8,128)(2,1)S(1)} %get-tuple-element.14.emb_ref, f32[256,128]{1,0:T(8,128)S(1)} %get-tuple-element.15.key_ref, bf16[272,768]{1,0:T(8,128)(2,1)S(1)} %collective-permute-done.2.refs_0_, bf16[272,768]{1,0:T(8,128)(2,1)S(1)} %collective-permute-done.3.refs_1_, ...), custom_call_target="tpu_custom_call" | custom-call | tf_op jit(solution)/shard_map/pallas_call | solution.py:302
  45.6 1.9 %collective-permute-start.6 = (bf16[128,768]{1,0:T(8,128)(2,1)S(1)}, bf16[128,768]{1,0:T(8,128)(2,1)S(1)}, u32[]{:S(2)}, u32[]{:S(2)}) collective-permute-start(bf16[128,768]{1,0:T(8,128)(2,1)S(1)} %shard_map.91), channel_id=1, source_target_pairs={{0,2},{1,3},{2,0},{3,1},{4,6},{5,7},{6,4},{7,5},{8,10},{9,11},{10,... | collective-permute-start | bytes 589832 | tf_op jit(solution)/shard_map/ppermute | solution.py:249
  47.6 0.0 collective-permute-done.4.refs_2_
  47.6 0.0 collective-permute-done.5.refs_3_
  47.6 1.7 %shard_map.90.own_ref = bf16[128,768]{1,0:T(8,128)(2,1)S(1)} custom-call(bf16[256,768]{1,0:T(8,128)(2,1)S(1)} %get-tuple-element.14.emb_ref, f32[256,128]{1,0:T(8,128)S(1)} %get-tuple-element.15.key_ref, bf16[272,768]{1,0:T(8,128)(2,1)S(1)} %collective-permute-done.2.refs_0_, bf16[272,768]{1,0:T(8,128)(2,1)S(1)} %collective-permute-done.3.refs_1_, ...), custom_call_target="tpu_custom_call" | custom-call | tf_op jit(solution)/shard_map/pallas_call | solution.py:306
  49.3 0.0 collective-permute-done.6.given_ref
  49.3 0.8 %shard_map.92 = (bf16[128,768]{1,0:T(8,128)(2,1)}, bf16[128,768]{1,0:T(8,128)(2,1)}) custom-call(bf16[128,768]{1,0:T(8,128)(2,1)S(1)} %shard_map.90.own_ref, bf16[128,768]{1,0:T(8,128)(2,1)S(1)} %collective-permute-done.6.given_ref), custom_call_target="tpu_custom_call" | custom-call | tf_op jit(solution)/shard_map/pallas_call | solution.py:309
Async XLA Ops:
  1.7 17.7 %collective-permute-start = (bf16[272,768]{1,0:T(8,128)(2,1)S(1)}, bf16[272,768]{1,0:T(8,128)(2,1)S(1)}, u32[]{:S(2)}, u32[]{:S(2)}) collective-permute-start(bf16[272,768]{1,0:T(8,128)(2,1)S(1)} %shard_map.86.raw_ref), channel_id=1, source_target_pairs={{0,2},{1,3},{2,0},{3,1},{4,6},{5,7},{6,4},{7,5},{8,10},{9,11},{10,... | collective-permute-start | bytes 1253384 | tf_op jit(solution)/shard_map/ppermute | solution.py:249
  20.0 21.2 %collective-permute-start.1 = (bf16[272,768]{1,0:T(8,128)(2,1)S(1)}, bf16[272,768]{1,0:T(8,128)(2,1)S(1)}, u32[]{:S(2)}, u32[]{:S(2)}) collective-permute-start(bf16[272,768]{1,0:T(8,128)(2,1)S(1)} %get-tuple-element.12.sent_ref), channel_id=1, source_target_pairs={{0,5},{1,4},{2,1023},{3,1022},{4,9},{5,8},{6,3},{7,2},{8,13},{9,12... | collective-permute-start | bytes 1253384 | tf_op jit(solution)/shard_map/ppermute | solution.py:255
  30.4 13.6 %collective-permute-start.2 = (bf16[272,768]{1,0:T(8,128)(2,1)S(1)}, bf16[272,768]{1,0:T(8,128)(2,1)S(1)}, u32[]{:S(2)}, u32[]{:S(2)}) collective-permute-start(bf16[272,768]{1,0:T(8,128)(2,1)S(1)} %get-tuple-element.12.sent_ref), channel_id=1, source_target_pairs={{0,1},{1,0},{2,3},{3,2},{4,5},{5,4},{6,7},{7,6},{8,9},{9,8},{10,11... | collective-permute-start | bytes 1253384 | tf_op jit(solution)/shard_map/ppermute | solution.py:252
  32.4 11.7 %collective-permute-start.3 = (bf16[272,768]{1,0:T(8,128)(2,1)S(1)}, bf16[272,768]{1,0:T(8,128)(2,1)S(1)}, u32[]{:S(2)}, u32[]{:S(2)}) collective-permute-start(bf16[272,768]{1,0:T(8,128)(2,1)S(1)} %get-tuple-element.12.sent_ref), channel_id=1, source_target_pairs={{0,4},{1,5},{2,1022},{3,1023},{4,8},{5,9},{6,2},{7,3},{8,12},{9,13... | collective-permute-start | bytes 1253384 | tf_op jit(solution)/shard_map/ppermute | solution.py:258
  35.6 11.9 %collective-permute-start.4 = (bf16[144,768]{1,0:T(8,128)(2,1)S(1)}, bf16[144,768]{1,0:T(8,128)(2,1)S(1)}, u32[]{:S(2)}, u32[]{:S(2)}) collective-permute-start(bf16[144,768]{1,0:T(8,128)(2,1)S(1)} %get-tuple-element.16), channel_id=1, source_target_pairs={{0,8},{1,9},{2,1018},{3,1019},{4,12},{5,13},{6,1022},{7,1023},{8,1... | collective-permute-start | bytes 663560 | tf_op jit(solution)/shard_map/ppermute | solution.py:261
  38.0 9.6 %collective-permute-start.5 = (bf16[144,768]{1,0:T(8,128)(2,1)S(1)}, bf16[144,768]{1,0:T(8,128)(2,1)S(1)}, u32[]{:S(2)}, u32[]{:S(2)}) collective-permute-start(bf16[144,768]{1,0:T(8,128)(2,1)S(1)} %get-tuple-element.16), channel_id=1, source_target_pairs={{0,9},{1,8},{2,1019},{3,1018},{4,13},{5,12},{6,1023},{7,1022},{8,1... | collective-permute-start | bytes 663560 | tf_op jit(solution)/shard_map/ppermute | solution.py:264
  45.6 3.6 %collective-permute-start.6 = (bf16[128,768]{1,0:T(8,128)(2,1)S(1)}, bf16[128,768]{1,0:T(8,128)(2,1)S(1)}, u32[]{:S(2)}, u32[]{:S(2)}) collective-permute-start(bf16[128,768]{1,0:T(8,128)(2,1)S(1)} %shard_map.91), channel_id=1, source_target_pairs={{0,2},{1,3},{2,0},{3,1},{4,6},{5,7},{6,4},{7,5},{8,10},{9,11},{10,... | collective-permute-start | bytes 589832 | tf_op jit(solution)/shard_map/ppermute | solution.py:249
